TPU v7x, 32 devices: a whole 2x2x4 slice. The times are simulated.
32 devices in a mesh: grp: 2 (over core), trk: 16 (over z, y, x).
Axes of the slice: x: 2, y: 2, z: 4, core: 2. Of those that a mesh axis runs over, the one named last changes fastest.
Arguments:
- fields: bfloat16 [32, 128, 512], P('grp', 'trk'), may hold values from -81 to 81
- upstream: bfloat16 [32, 128, 512], P('grp', 'trk'), may hold values from -6 to 6
- ln_gain: float32 [512], replicated, may hold values from 0.1 to 1.9
- weights: bfloat16 [4, 512, 512], P(None, 'grp', 'trk'), may hold values from -8 to 8
Outputs:
- grad_fields: bfloat16 [32, 128, 512], P('grp', 'trk')
- grad_weights: float32 [4, 512, 512], P(None, 'grp', 'trk')
- grad_gain: float32 [512], replicated
All inputs are finite; a program needn't handle non-finite values.
Results may differ from a plain program's by a relative error of at most 0.014.
The roundings to bfloat16 on the way count: a program that leaves them out, or rounds other values in their place, can miss the bound.
Values may be sent and summed in bfloat16 or wider, within the bound.
No kernel may reach another device: no remote copies, remote signals or barrier semaphores. Data moves between devices by JAX's collectives and lax.ppermute only.
A program may use at most 64 MiB of HBM per device.

v0:
```python
import jax
import jax.numpy as jnp
from jax import lax
from jax.sharding import PartitionSpec as P

HEADS = 8


def normalize(fields, ln_gain):
    values = fields.astype(jnp.float32)
    row_mean = jnp.mean(values, -1, keepdims=True)
    offset = values - row_mean
    row_var = jnp.mean(offset * offset, -1, keepdims=True)
    inv_std = lax.rsqrt(row_var + 1e-05)
    centred = offset * inv_std
    normed = (centred * ln_gain).astype(jnp.bfloat16)
    return (normed, centred, inv_std)


def project(normed, w_in):
    return [
        jnp.einsum("rti,ij->rtj", normed, w_in[index], preferred_element_type=jnp.float32).astype(
            jnp.bfloat16
        )
        for index in range(3)
    ]


def split_heads(block, heads):
    rows, length, width = block.shape
    return (
        block.reshape(rows, length, heads, width // heads)
        .transpose(0, 2, 1, 3)
        .reshape(rows * heads, length, width // heads)
    )


def merge_heads(block, rows):
    items, length, size = block.shape
    return (
        block.reshape(rows, items // rows, length, size)
        .transpose(0, 2, 1, 3)
        .reshape(rows, length, items // rows * size)
    )


def head_back(members):
    query, keyed, valued, grad_out = members
    scaling = query.shape[-1] ** (-0.5)
    scores = jnp.einsum("qd,kd->qk", query, keyed, preferred_element_type=jnp.float32) * scaling
    row_max = jnp.max(scores, -1, keepdims=True)
    shifted = jnp.exp(scores - row_max)
    attn_prob = shifted / jnp.sum(shifted, -1, keepdims=True)
    prob_low = attn_prob.astype(jnp.bfloat16)
    output = jnp.einsum("qk,kd->qd", prob_low, valued, preferred_element_type=jnp.float32).astype(
        jnp.bfloat16
    )
    dprobs = jnp.einsum("qd,kd->qk", grad_out, valued, preferred_element_type=jnp.float32)
    row_dot = jnp.sum(attn_prob * dprobs, -1, keepdims=True)
    score_grad = (attn_prob * (dprobs - row_dot) * scaling).astype(jnp.bfloat16)
    grad_value = jnp.einsum(
        "qk,qd->kd", prob_low, grad_out, preferred_element_type=jnp.float32
    ).astype(jnp.bfloat16)
    grad_query = jnp.einsum(
        "qk,kd->qd", score_grad, keyed, preferred_element_type=jnp.float32
    ).astype(jnp.bfloat16)
    grad_key = jnp.einsum(
        "qk,qd->kd", score_grad, query, preferred_element_type=jnp.float32
    ).astype(jnp.bfloat16)
    return (output, grad_query, grad_key, grad_value)


def attend_back(query_proj, key_proj, value_proj, upstream_rows, w_out):
    rows = query_proj.shape[0]
    grad_attended = jnp.einsum(
        "rtj,ij->rti", upstream_rows, w_out, preferred_element_type=jnp.float32
    ).astype(jnp.bfloat16)
    pieces = lax.map(
        head_back,
        (
            split_heads(query_proj, HEADS),
            split_heads(key_proj, HEADS),
            split_heads(value_proj, HEADS),
            split_heads(grad_attended, HEADS),
        ),
    )
    return [merge_heads(piece, rows) for piece in pieces]


def input_grad(grad_query, grad_key, grad_value, w_in, centred, inv_std, ln_gain):
    stacked = jnp.stack([grad_query, grad_key, grad_value], 2)
    grad_normed = jnp.einsum("rtcj,cij->rti", stacked, w_in, preferred_element_type=jnp.float32)
    width = grad_normed.shape[-1]
    gain_term = jnp.sum((grad_normed * centred).reshape(-1, width), 0)
    scaled = grad_normed * ln_gain
    branch = inv_std * (
        scaled
        - jnp.mean(scaled, -1, keepdims=True)
        - centred * jnp.mean(scaled * centred, -1, keepdims=True)
    )
    return (branch.astype(jnp.bfloat16), gain_term)


def proj_grads(normed, grad_query, grad_key, grad_value):
    return [
        jnp.einsum("rti,rtj->ij", normed, member, preferred_element_type=jnp.float32)
        for member in (grad_query, grad_key, grad_value)
    ]


def shards(fields, upstream, ln_gain, weights):
    w_part = lax.all_gather(weights, "trk", axis=2, tiled=True)
    w_full = lax.all_gather(w_part, "grp", axis=1, tiled=True)
    w_in = w_full[:3]
    w_out = w_full[3]
    rows_dev, trk_dev, width = fields.shape
    cell_count = rows_dev * lax.axis_size("grp") * trk_dev * lax.axis_size("trk")
    normed, centred, inv_std = normalize(fields, ln_gain)
    query_proj, key_proj, value_proj = project(normed, w_in)
    query_rows, key_rows, value_rows, upstream_rows = (
        lax.all_to_all(query_proj, "trk", split_axis=0, concat_axis=1, tiled=True),
        lax.all_to_all(key_proj, "trk", split_axis=0, concat_axis=1, tiled=True),
        lax.all_to_all(value_proj, "trk", split_axis=0, concat_axis=1, tiled=True),
        lax.all_to_all(upstream, "trk", split_axis=0, concat_axis=1, tiled=True),
    )
    attended, grad_query, grad_key, grad_value = attend_back(
        query_rows, key_rows, value_rows, upstream_rows, w_out
    )
    back_query, back_key, back_value = (
        lax.all_to_all(grad_query, "trk", split_axis=1, concat_axis=0, tiled=True),
        lax.all_to_all(grad_key, "trk", split_axis=1, concat_axis=0, tiled=True),
        lax.all_to_all(grad_value, "trk", split_axis=1, concat_axis=0, tiled=True),
    )
    grad_list = proj_grads(normed, back_query, back_key, back_value)
    branch_cells, gain_term = input_grad(
        back_query, back_key, back_value, w_in, centred, inv_std, ln_gain
    )
    out_grad = jnp.einsum(
        "rti,rtj->ij", attended, upstream_rows, preferred_element_type=jnp.float32
    )
    raw_grad = jnp.stack(grad_list + [out_grad])
    partial_grad = lax.psum_scatter(
        raw_grad.astype(jnp.bfloat16), "grp", scatter_dimension=1, tiled=True
    ).astype(jnp.float32)
    summed_grad = lax.psum_scatter(partial_grad, "trk", scatter_dimension=2, tiled=True)
    gain_sum = lax.psum(gain_term, ("grp", "trk"))
    factor = float(cell_count) ** (-0.5)
    grad_fields = (upstream.astype(jnp.float32) + branch_cells.astype(jnp.float32)).astype(
        jnp.bfloat16
    )
    return (grad_fields, summed_grad * factor, gain_sum * factor)


def solution(mesh):
    in_specs = (P("grp", "trk", None), P("grp", "trk", None), P(), P(None, "grp", "trk"))
    out_specs = (P("grp", "trk", None), P(None, "grp", "trk"), P())
    return jax.shard_map(shards, mesh=mesh, in_specs=in_specs, out_specs=out_specs, check_vma=False)
```

profile of v0, /device:TPU:0, one launch (start us, length us, event | category | flops | bytes accessed | tf_op | source)
XLA Modules:
  0.0 319.8 jit_solution(12672143530181477418)
XLA Ops:
  7.2 1.5 copy.60
  8.8 60.5 %all-gather.3.cloned.1.call-done = bf16[4,256,512]{1,0,2:T(4,128)(2,1)} async-done(((bf16[4,256,32]{1,0,2:T(4,128)(2,1)}), bf16[4,256,512]{1,0,2:T(4,128)(2,1)}) %all-gather.3.cloned.1.call-update) | async-done | bytes 1048592 | tf_op jit(solution)/shard_map/all_gather | solution.py:112
  69.4 2.4 copy.61
  71.8 4.4 %all-to-all-start.3 = ((bf16[16,8,512]{2,1,0:T(8,128)(2,1)}), bf16[16,8,512]{2,1,0:T(8,128)(2,1)S(1)}, u32[]{:S(2)}, u32[]{:S(2)}) async-start(bf16[16,8,512]{2,1,0:T(8,128)(2,1)} %param.7), calls=%async_computation.3 | async-start | bytes 262144 | tf_op jit(solution)/shard_map/all_to_all | solution.py:124
  76.5 4.8 %all-gather.5.cloned.1.call-done = bf16[4,512,512]{2,1,0:T(8,128)(2,1)} async-done(((bf16[4,256,512]{2,1,0:T(8,128)(2,1)}), bf16[4,512,512]{2,1,0:T(8,128)(2,1)}) %all-gather.5.cloned.1.call-update) | async-done | bytes 2097168 | tf_op jit(solution)/shard_map/all_gather | solution.py:113
  81.3 2.0 convolution_convert_fusion.8
  83.3 0.7 all-to-all-done.3
  84.0 6.1 %all-to-all-start = ((bf16[16,8,512]{2,1,0:T(8,128)(2,1)}), bf16[16,8,512]{2,1,0:T(8,128)(2,1)S(1)}, u32[]{:S(2)}, u32[]{:S(2)}) async-start(bf16[16,8,512]{2,1,0:T(8,128)(2,1)} %convolution_convert_fusion.8), calls=%async_computation | async-start | bytes 262144 | tf_op jit(solution)/shard_map/all_to_all | solution.py:121
  90.1 2.0 convolution_convert_fusion.7
  92.1 5.9 %all-to-all-done = bf16[16,8,512]{2,1,0:T(8,128)(2,1)S(1)} async-done(((bf16[16,8,512]{2,1,0:T(8,128)(2,1)}), bf16[16,8,512]{2,1,0:T(8,128)(2,1)S(1)}, u32[]{:S(2)}, u32[]{:S(2)}) %all-to-all-start) | async-done | bytes 131104 | tf_op jit(solution)/shard_map/all_to_all | solution.py:121
  98.0 3.5 %all-to-all-start.1 = ((bf16[16,8,512]{2,1,0:T(8,128)(2,1)}), bf16[16,8,512]{2,1,0:T(8,128)(2,1)S(1)}, u32[]{:S(2)}, u32[]{:S(2)}) async-start(bf16[16,8,512]{2,1,0:T(8,128)(2,1)} %convolution_convert_fusion.7), calls=%async_computation.1 | async-start | bytes 262144 | tf_op jit(solution)/shard_map/all_to_all | solution.py:122
  101.5 2.0 convolution_convert_fusion.6
  103.5 5.8 %all-to-all-done.1 = bf16[16,8,512]{2,1,0:T(8,128)(2,1)S(1)} async-done(((bf16[16,8,512]{2,1,0:T(8,128)(2,1)}), bf16[16,8,512]{2,1,0:T(8,128)(2,1)S(1)}, u32[]{:S(2)}, u32[]{:S(2)}) %all-to-all-start.1) | async-done | bytes 131104 | tf_op jit(solution)/shard_map/all_to_all | solution.py:122
  109.3 3.5 %all-to-all-start.2 = ((bf16[16,8,512]{2,1,0:T(8,128)(2,1)}), bf16[16,8,512]{2,1,0:T(8,128)(2,1)S(1)}, u32[]{:S(2)}, u32[]{:S(2)}) async-start(bf16[16,8,512]{2,1,0:T(8,128)(2,1)} %convolution_convert_fusion.6), calls=%async_computation.2 | async-start | bytes 262144 | tf_op jit(solution)/shard_map/all_to_all | solution.py:123
  112.8 1.3 convolution_convert_fusion.5
  114.8 5.8 %all-to-all-done.2 = bf16[16,8,512]{2,1,0:T(8,128)(2,1)S(1)} async-done(((bf16[16,8,512]{2,1,0:T(8,128)(2,1)}), bf16[16,8,512]{2,1,0:T(8,128)(2,1)S(1)}, u32[]{:S(2)}, u32[]{:S(2)}) %all-to-all-start.2) | async-done | bytes 131104 | tf_op jit(solution)/shard_map/all_to_all | solution.py:123
  120.8 9.9 %while.16 = (s32[]{:T(128)}, bf16[8,128,64]{1,2,0:T(8,128)(2,1)S(1)}, bf16[8,128,64]{1,2,0:T(8,128)(2,1)S(1)}, bf16[8,128,64]{1,2,0:T(8,128)(2,1)S(1)}, bf16[8,1...) while((s32[]{:T(128)}, ...), condition=%wide.region_6.7_spmd, body=%wide.region_2.6_spmd.sunk | while | flops 12942978 | bytes 930413 | solution.py:78
  121.0 0.2 fusion.107
  121.7 0.2 fusion.109
  122.0 0.2 fusion.105
  122.3 0.2 fusion.107
  122.9 0.2 fusion.109
  123.3 0.2 fusion.105
  123.5 0.2 fusion.107
  124.1 0.2 fusion.109
  124.7 0.2 fusion.107
  125.4 0.2 fusion.109
  126.0 0.2 fusion.107
  126.6 0.2 fusion.109
  127.2 0.2 fusion.107
  127.8 0.2 fusion.109
  128.4 0.2 fusion.107
  129.1 0.2 fusion.109
  129.7 0.2 fusion.107
  130.3 0.2 fusion.109
  130.7 0.2 copy.69
  130.9 0.5 broadcast.50
  131.4 1.4 reduce.1
  132.8 0.7 reshape.146
  133.5 3.5 %all-to-all-start.6 = ((bf16[16,2,2048]{2,1,0:T(2,128)(2,1)}), bf16[16,2,2048]{2,1,0:T(2,128)(2,1)S(1)}, u32[]{:S(2)}, u32[]{:S(2)}) async-start(bf16[16,2,2048]{2,1,0:T(2,128)(2,1)} %reshape.146), calls=%async_computation.6 | async-start | bytes 262144 | tf_op jit(solution)/shard_map/all_to_all | solution.py:132
  137.3 1.4 reduce.2
  138.7 0.7 reshape.148
  139.6 1.4 reduce.3
  141.0 0.7 reshape.150
  141.7 0.3 fusion.41
  142.0 2.8 all-to-all-done.6
  144.8 4.1 %all-to-all-start.5 = ((bf16[16,2,2048]{2,1,0:T(2,128)(2,1)}), bf16[16,2,2048]{2,1,0:T(2,128)(2,1)S(1)}, u32[]{:S(2)}, u32[]{:S(2)}) async-start(bf16[16,2,2048]{2,1,0:T(2,128)(2,1)} %reshape.148), calls=%async_computation.5 | async-start | bytes 262144 | tf_op jit(solution)/shard_map/all_to_all | solution.py:131
  149.1 0.4 fusion.42
  149.5 7.2 %all-to-all-done.5 = bf16[16,2,2048]{2,1,0:T(2,128)(2,1)S(1)} async-done(((bf16[16,2,2048]{2,1,0:T(2,128)(2,1)}), bf16[16,2,2048]{2,1,0:T(2,128)(2,1)S(1)}, u32[]{:S(2)}, u32[]{:S(2)}) %all-to-all-start.5) | async-done | bytes 131104 | tf_op jit(solution)/shard_map/all_to_all | solution.py:131
  156.7 3.5 %all-to-all-start.4 = ((bf16[16,2,2048]{2,1,0:T(2,128)(2,1)}), bf16[16,2,2048]{2,1,0:T(2,128)(2,1)S(1)}, u32[]{:S(2)}, u32[]{:S(2)}) async-start(bf16[16,2,2048]{2,1,0:T(2,128)(2,1)} %reshape.150), calls=%async_computation.4 | async-start | bytes 262144 | tf_op jit(solution)/shard_map/all_to_all | solution.py:130
  160.4 0.4 fusion.43
  160.8 7.2 %all-to-all-done.4 = bf16[16,2,2048]{2,1,0:T(2,128)(2,1)S(1)} async-done(((bf16[16,2,2048]{2,1,0:T(2,128)(2,1)}), bf16[16,2,2048]{2,1,0:T(2,128)(2,1)S(1)}, u32[]{:S(2)}, u32[]{:S(2)}) %all-to-all-start.4) | async-done | bytes 131104 | tf_op jit(solution)/shard_map/all_to_all | solution.py:130
  168.1 0.4 fusion.44
  168.6 1.6 pad_maximum_fusion
  170.2 6.9 %reduce-scatter.2.cloned.1.call-done = bf16[4,256,512]{2,1,0:T(8,128)(2,1)} async-done(((bf16[4,512,512]{2,1,0:T(8,128)(2,1)}), bf16[4,256,512]{2,1,0:T(8,128)(2,1)}) %reduce-scatter.2.cloned.1.call-update) | async-done | bytes 1048592 | tf_op jit(solution)/shard_map/reduce_scatter | solution.py:142
  177.1 2.5 copy.73
  179.6 0.6 dynamic-slice
  181.2 0.7 fusion.62
  181.9 42.1 %psum.7 = f32[512]{0:T(512)S(1)} all-reduce(f32[512]{0:T(512)S(1)} %get-tuple-element.108), channel_id=1, replica_groups=mesh['grp'=2,'trk'=16] {'grp','trk'}, use_global_device_ids=true, to_apply=%region_12.13 | all-reduce | flops 512 | bytes 4096 | tf_op jit(solution)/shard_map/psum | solution.py:146
  224.1 0.6 broadcast_multiply_fusion.3
  224.6 1.7 add_convert_fusion
  226.4 85.3 %all-reduce.3.cloned.1.call-done = f32[4,256,512]{1,0,2:T(4,128)} async-done(((f32[4,256,512]{1,0,2:T(4,128)}), f32[4,256,512]{1,0,2:T(4,128)}) %all-reduce.3.cloned.1.call-update) | async-done | bytes 2097168
  311.7 0.9 dynamic-slice_multiply_fusion
  312.6 0.7 copy.74
  (86 shorter events, 8.3 us)
Async XLA Ops:
  7.2 69.1 %copy-start = (bf16[16,8,512]{2,1,0:T(8,128)(2,1)S(1)}, bf16[16,8,512]{2,1,0:T(8,128)(2,1)}, u32[]{:S(2)}) copy-start(bf16[16,8,512]{2,1,0:T(8,128)(2,1)} %param.6) | copy-start | bytes 393220
  7.2 74.2 %copy-start.1 = (f32[512]{0:T(512)S(1)}, f32[512]{0:T(512)}, u32[]{:S(2)}) copy-start(f32[512]{0:T(512)} %param.8) | copy-start | bytes 6148
  7.2 62.2 %all-gather.3.cloned.1.call-start = ((), (), s32[]{:S(2)}) async-start(), calls=%async_computation.8 | async-start | bytes 1114112 | tf_op jit(solution)/shard_map/all_gather | solution.py:112
  8.8 72.5 %all-gather.5.cloned.1.call-start = ((), (), s32[]{:S(2)}) async-start(), calls=%async_computation.9 | async-start | bytes 3145728 | tf_op jit(solution)/shard_map/all_gather | solution.py:113
  71.8 12.2 %all-to-all-start.3 = ((bf16[16,8,512]{2,1,0:T(8,128)(2,1)}), bf16[16,8,512]{2,1,0:T(8,128)(2,1)S(1)}, u32[]{:S(2)}, u32[]{:S(2)}) async-start(bf16[16,8,512]{2,1,0:T(8,128)(2,1)} %param.7), calls=%async_computation.3 | async-start | bytes 262144 | tf_op jit(solution)/shard_map/all_to_all | solution.py:124
  84.0 14.0 %all-to-all-start = ((bf16[16,8,512]{2,1,0:T(8,128)(2,1)}), bf16[16,8,512]{2,1,0:T(8,128)(2,1)S(1)}, u32[]{:S(2)}, u32[]{:S(2)}) async-start(bf16[16,8,512]{2,1,0:T(8,128)(2,1)} %convolution_convert_fusion.8), calls=%async_computation | async-start | bytes 262144 | tf_op jit(solution)/shard_map/all_to_all | solution.py:121
  98.0 11.3 %all-to-all-start.1 = ((bf16[16,8,512]{2,1,0:T(8,128)(2,1)}), bf16[16,8,512]{2,1,0:T(8,128)(2,1)S(1)}, u32[]{:S(2)}, u32[]{:S(2)}) async-start(bf16[16,8,512]{2,1,0:T(8,128)(2,1)} %convolution_convert_fusion.7), calls=%async_computation.1 | async-start | bytes 262144 | tf_op jit(solution)/shard_map/all_to_all | solution.py:122
  109.3 11.3 %all-to-all-start.2 = ((bf16[16,8,512]{2,1,0:T(8,128)(2,1)}), bf16[16,8,512]{2,1,0:T(8,128)(2,1)S(1)}, u32[]{:S(2)}, u32[]{:S(2)}) async-start(bf16[16,8,512]{2,1,0:T(8,128)(2,1)} %convolution_convert_fusion.6), calls=%async_computation.2 | async-start | bytes 262144 | tf_op jit(solution)/shard_map/all_to_all | solution.py:123
  133.5 11.3 %all-to-all-start.6 = ((bf16[16,2,2048]{2,1,0:T(2,128)(2,1)}), bf16[16,2,2048]{2,1,0:T(2,128)(2,1)S(1)}, u32[]{:S(2)}, u32[]{:S(2)}) async-start(bf16[16,2,2048]{2,1,0:T(2,128)(2,1)} %reshape.146), calls=%async_computation.6 | async-start | bytes 262144 | tf_op jit(solution)/shard_map/all_to_all | solution.py:132
  144.8 11.9 %all-to-all-start.5 = ((bf16[16,2,2048]{2,1,0:T(2,128)(2,1)}), bf16[16,2,2048]{2,1,0:T(2,128)(2,1)S(1)}, u32[]{:S(2)}, u32[]{:S(2)}) async-start(bf16[16,2,2048]{2,1,0:T(2,128)(2,1)} %reshape.148), calls=%async_computation.5 | async-start | bytes 262144 | tf_op jit(solution)/shard_map/all_to_all | solution.py:131
  156.7 11.3 %all-to-all-start.4 = ((bf16[16,2,2048]{2,1,0:T(2,128)(2,1)}), bf16[16,2,2048]{2,1,0:T(2,128)(2,1)S(1)}, u32[]{:S(2)}, u32[]{:S(2)}) async-start(bf16[16,2,2048]{2,1,0:T(2,128)(2,1)} %reshape.150), calls=%async_computation.4 | async-start | bytes 262144 | tf_op jit(solution)/shard_map/all_to_all | solution.py:130
  160.2 16.8 %reduce-scatter.2.cloned.1.call-start = ((), (), s32[]{:S(2)}) async-start(), calls=%async_computation.10 | async-start | bytes 3145728 | tf_op jit(solution)/shard_map/reduce_scatter | solution.py:142
  170.1 9.5 %copy-start.3 = (u32[32]{0:T(128)S(1)}, u32[32]{0:T(128)}, u32[]{:S(2)}) copy-start(u32[32]{0:T(128)} %constant.42) | copy-start | bytes 388
  170.1 141.5 %all-reduce.3.cloned.1.call-start = ((), (), s32[]{:S(2)}) async-start(), calls=%async_computation.11 | async-start | bytes 4194304
  179.6 1.6 copy-start.2
Sparse Core Ops, SparseCore 0:
  11.4 57.9 all-gather.2
  71.9 9.3 all-gather.4
  170.3 6.7 reduce-scatter.1
  183.3 128.3 all-reduce.2
where the time goes:
time: 321 us; the launch traced here: 320 us
  waiting for transfers between devices  193 us (60%)
  blocking collectives  42.1 us (13%)
  starting transfers between devices  28.8 us (9%)
  matrix products  18.5 us (6%)
  between operations  14.8 us (5%)
  local copies, waits for them, and re-layouts  12.4 us (4%)
  other arithmetic  10 us (3%)
    unnamed x5, waiting for transfers between devices  85.3 us
    all_gather x1, waiting for transfers between devices, shards(): w_part = lax.all_gather(weights, 'trk', axis=2, tiled=True)  60.5 us
    psum x1, blocking collectives, shards(): gain_sum = lax.psum(gain_term, ('grp', 'trk'))  42.1 us
    all_to_all x1, waiting for transfers between devices, shards(): lax.all_to_all(grad_key, 'trk', split_axis=1, concat_axis=0, tiled=True)  7.25 us
    all_to_all x1, waiting for transfers between devices, shards(): lax.all_to_all(grad_query, 'trk', split_axis=1, concat_axis=0, tiled=True)  7.17 us
    reduce_scatter x1, waiting for transfers between devices, shards(): lax.psum_scatter(raw_grad.astype(jnp.bfloat16), 'grp', scatter_dimension=...  6.85 us
  transfers between devices with their start and end apart: 11, of which 11 were waited for; matrix products, arithmetic and copies ran while one was open for 6% of the time, Pallas kernels for 0%

commit v1 on v0

v1 whole, which is shorter than its diff:
```python
import functools

import jax
import jax.numpy as jnp
from jax import lax
from jax.experimental import pallas as pl
from jax.experimental.pallas import tpu as pltpu
from jax.sharding import PartitionSpec as P

HEADS = 8
BF = jnp.bfloat16
F32 = jnp.float32


def dot(a, b, dims):
    return lax.dot_general(a, b, (dims, ((), ())), preferred_element_type=F32)


def row_kernel(groups, place, rows_ref, gain_ref, *refs):
    w_refs, rest = refs[:groups], refs[groups:]
    wg_ref, cells_ref, w_all, norm_s, att_s = rest
    group, half_at = place[0], place[1]
    senders, pair, _ = rows_ref.shape
    tracks = pair // 2
    width = gain_ref.shape[1]
    length = senders * tracks
    fan, halves, _, cols, part = w_refs[0].shape
    both = rows_ref[...].astype(F32)
    values = both[:, :tracks].reshape(length, width)
    upstream = both[:, tracks:].reshape(length, width)
    gain = gain_ref[...]
    for step in range(groups):
        owner = lax.rem(group - step + groups, groups)
        lanes = pl.ds(pl.multiple_of(owner * part, part), part)
        for far in range(halves):
            base = lax.rem(half_at + far, halves) * (fan * cols)
            for near in range(fan):
                at = pl.ds(pl.multiple_of(base + near * cols, cols), cols)
                for index in range(4):
                    w_all[index, at, lanes] = w_refs[step][near, far, index]
    row_mean = jnp.mean(values, -1, keepdims=True)
    offset = values - row_mean
    row_var = jnp.mean(offset * offset, -1, keepdims=True)
    inv_std = lax.rsqrt(row_var + 1e-05)
    centred = offset * inv_std
    normed = (centred * gain).astype(BF)
    up = upstream.astype(BF)
    projected = [dot(normed, w_all[index], ((1,), (1,))).astype(BF) for index in range(3)]
    grad_att = dot(up, w_all[3], ((1,), (0,))).astype(BF)
    size = width // HEADS
    scaling = size ** (-0.5)
    span = 2 * size
    lane = lax.broadcasted_iota(jnp.int32, (length, span), 1)
    first = lane < size
    pieces = [[], [], [], []]
    for at in range(0, width, span):
        query, keyed, valued = [member[:, at : at + span] for member in projected]
        grad_out = grad_att[:, at : at + span]
        zero = jnp.zeros_like(query)
        query2 = jnp.concatenate([jnp.where(first, query, zero), jnp.where(first, zero, query)], 0)
        grad2 = jnp.concatenate(
            [jnp.where(first, grad_out, zero), jnp.where(first, zero, grad_out)], 0
        )
        scores = dot(query2, keyed, ((1,), (1,))) * scaling
        shifted = jnp.exp(scores - jnp.max(scores, -1, keepdims=True))
        prob = shifted / jnp.sum(shifted, -1, keepdims=True)
        prob_low = prob.astype(BF)
        dprobs = dot(grad2, valued, ((1,), (1,)))
        row_dot = jnp.sum(prob * dprobs, -1, keepdims=True)
        score_grad = (prob * (dprobs - row_dot) * scaling).astype(BF)
        out2 = dot(prob_low, valued, ((1,), (0,)))
        gq2 = dot(score_grad, keyed, ((1,), (0,)))
        pieces[0].append(jnp.where(first, gq2[:length], gq2[length:]).astype(BF))
        pieces[1].append(dot(score_grad, query2, ((0,), (0,))).astype(BF))
        pieces[2].append(dot(prob_low, grad2, ((0,), (0,))).astype(BF))
        pieces[3].append(jnp.where(first, out2[:length], out2[length:]).astype(BF))
    grads = [jnp.concatenate(piece, 1) for piece in pieces[:3]]
    attended = jnp.concatenate(pieces[3], 1)
    grad_normed = sum(dot(grads[index], w_all[index], ((1,), (0,))) for index in range(3))
    gain_term = jnp.sum(grad_normed * centred, 0, keepdims=True)
    scaled = grad_normed * gain
    branch = inv_std * (
        scaled
        - jnp.mean(scaled, -1, keepdims=True)
        - centred * jnp.mean(scaled * centred, -1, keepdims=True)
    )
    cells = upstream + branch.astype(BF).astype(F32)
    high = gain_term.astype(BF).astype(F32)
    low = gain_term - high
    which = lax.broadcasted_iota(jnp.int32, (tracks, width), 0)
    extra = jnp.where(which == 0, high, jnp.where(which == 1, low, 0.0))
    extra = jnp.broadcast_to(extra[None], (senders, tracks, width))
    cells_ref[...] = jnp.concatenate(
        [cells.reshape(senders, tracks, width), extra], 1
    ).astype(BF)
    for at in range(groups):
        norm_s[at] = normed[:, at * part : (at + 1) * part]
        att_s[at] = attended[:, at * part : (at + 1) * part]
    for step in range(groups):
        owner = lax.rem(group + step, groups)
        norm_part, att_part = norm_s[owner], att_s[owner]
        for index in range(4):
            if index < 3:
                block = dot(grads[index], norm_part, ((0,), (0,))).astype(BF)
            else:
                block = dot(up, att_part, ((0,), (0,))).astype(BF)
            block = block.reshape(halves, fan, cols, part)
            for far in range(halves):
                to = lax.rem(half_at + far, halves)
                for near in range(fan):
                    wg_ref[step, near, to, index] = block[far, near]


def ring(size, step):
    return [(i, (i + step) % size) for i in range(size)]


def join_blocks(blocks, half_at):
    fan, halves, four, cols, part = blocks.shape
    blocks = jnp.where(half_at == 0, blocks, blocks[:, ::-1])
    return blocks.transpose(2, 1, 0, 3, 4).reshape(1, 1, four, halves * fan * cols, part)


def cut_blocks(joined, half_at, shape):
    fan, halves, four, cols, part = shape
    blocks = joined.reshape(-1, four, halves, fan, cols, part).transpose(0, 3, 2, 1, 4, 5)
    return jnp.where(half_at == 0, blocks, blocks[:, :, ::-1])


def shards(fields, upstream, ln_gain, weights):
    groups, count = lax.axis_size("grp"), lax.axis_size("trk")
    rows_dev, trk_dev, width = fields.shape
    _, part, cols = weights.shape
    cell_count = rows_dev * groups * trk_dev * count
    fan = count // 2
    near = [[half * fan + i for i in range(fan)] for half in range(2)]
    group, track = lax.axis_index("grp"), lax.axis_index("trk")
    half_at = track // fan
    both = jnp.concatenate([fields, upstream], 1)
    row = lax.all_to_all(both, "trk", split_axis=0, concat_axis=0, tiled=True)
    own = weights.transpose(0, 2, 1)
    held = jnp.stack([own, lax.ppermute(own, "trk", ring(count, fan))])
    sent = jnp.broadcast_to(held[None], (fan,) + held.shape)
    w_part = lax.all_to_all(
        sent, "trk", split_axis=0, concat_axis=0, tiled=True, axis_index_groups=near
    )
    w_parts = [w_part] + [lax.ppermute(w_part, "grp", ring(groups, k)) for k in range(1, groups)]
    blocks_shape = w_part.shape
    narrow = cols % 16 != 0
    if narrow:
        w_parts = [join_blocks(blocks, half_at) for blocks in w_parts]
    place = jnp.stack([group, half_at]).astype(jnp.int32)
    vmem = pl.BlockSpec(memory_space=pltpu.VMEM)
    wg, cells = pl.pallas_call(
        functools.partial(row_kernel, groups),
        out_shape=(
            jax.ShapeDtypeStruct((groups,) + w_parts[0].shape, BF),
            jax.ShapeDtypeStruct((count, 2 * trk_dev, width), BF),
        ),
        in_specs=[pl.BlockSpec(memory_space=pltpu.SMEM)] + [vmem] * (2 + groups),
        out_specs=(vmem, vmem),
        scratch_shapes=[
            pltpu.VMEM((4, width, width), BF),
            pltpu.VMEM((groups, trk_dev * count, part), BF),
            pltpu.VMEM((groups, trk_dev * count, part), BF),
        ],
        compiler_params=pltpu.CompilerParams(vmem_limit_bytes=48 * 2**20),
    )(place, row, ln_gain[None], *w_parts)
    if narrow:
        wg = cut_blocks(wg, half_at, blocks_shape)
    total = wg[0].astype(F32)
    for k in range(1, groups):
        total = total + lax.ppermute(wg[k], "grp", ring(groups, k)).astype(F32)
    back = lax.all_to_all(cells, "trk", split_axis=0, concat_axis=0, tiled=True)
    spread = lax.all_to_all(
        total.astype(BF), "trk", split_axis=0, concat_axis=0, tiled=True, axis_index_groups=near
    )
    summed = jnp.sum(spread.astype(F32), 0)
    total = summed[0] + lax.ppermute(summed[1].astype(BF), "trk", ring(count, fan)).astype(F32)
    grad_fields = back[:, :trk_dev]
    gain_sum = jnp.sum(back[:, trk_dev : trk_dev + 2].astype(F32), (0, 1))
    gain_sum = lax.psum(gain_sum, "grp")
    factor = float(cell_count) ** (-0.5)
    return (grad_fields, total.transpose(0, 2, 1) * factor, gain_sum * factor)


def solution(mesh):
    in_specs = (P("grp", "trk", None), P("grp", "trk", None), P(), P(None, "grp", "trk"))
    out_specs = (P("grp", "trk", None), P(None, "grp", "trk"), P())
    return jax.shard_map(shards, mesh=mesh, in_specs=in_specs, out_specs=out_specs, check_vma=False)
```

time: 321 us -> 90.2 us (0.28)
  waiting for transfers between devices: 193 us -> 37.3 us
  blocking collectives: 42.1 us -> 20.8 us
  matrix products: 18.5 us -> 0 us
  between operations: 14.8 us -> 0.76 us
  starting transfers between devices: 28.8 us -> 17.9 us
  local copies, waits for them, and re-layouts: 12.4 us -> 4.06 us
  other arithmetic: 10 us -> 4.56 us
  Pallas kernels: 0 us -> 4.28 us
    unnamed x5 -> x0, waiting for transfers between devices: 85.3 us -> none
    all_gather x2 -> x0, waiting for transfers between devices: 65.3 us -> none  [the longest x1 60.5 us: shards(): w_part = lax.all_gather(weights, 'trk', axis=2, tiled=True)]
    psum x1, blocking collectives: 42.1 us -> 2.47 us  [shards(): gain_sum = lax.psum(gain_sum, 'grp')]
    dot_general x57 -> x0, matrix products: 18.5 us -> none  [the longest x3 5.94 us: project(): jnp.einsum('rti,ij->rtj', normed, w_in[index], preferred_element_type=jnp...]
    all_to_all x0 -> x1, blocking collectives: none -> 18.4 us  [shards(): lax.all_to_all(sent, 'trk', split_axis=0, concat_axis=0, tiled=True, axis...]
    all_to_all x7 -> x3, starting transfers between devices: 28.6 us -> 12.3 us  [the longest x1 5.15 us: shards(): row = lax.all_to_all(both, 'trk', split_axis=0, concat_axis=0, tiled=True)]
    reduce_scatter x1 -> x0, waiting for transfers between devices: 6.85 us -> none  [shards(): lax.psum_scatter(raw_grad.astype(jnp.bfloat16), 'grp', scatter_dimension=...]
    ppermute x0 -> x4, waiting for transfers between devices: none -> 6.33 us  [the longest x1 3.86 us: shards(): held = jnp.stack([own, lax.ppermute(own, 'trk', ring(count, fan))])]
  transfers between devices with their start and end apart: 11 -> 7, of which waited for: 11 -> 5; matrix products, arithmetic and copies ran while one was open for 6% -> 4% of each run, Pallas kernels for 0% -> 0%
where the time goes in v1:
time: 90.2 us; the launch traced here: 89.7 us
  waiting for transfers between devices  37.3 us (41%)
  blocking collectives  20.8 us (23%)
  starting transfers between devices  17.9 us (20%)
  other arithmetic  4.56 us (5%)
  Pallas kernels  4.28 us (5%)
  local copies, waits for them, and re-layouts  4.06 us (5%)
    all_to_all x1, blocking collectives, shards(): lax.all_to_all(sent, 'trk', split_axis=0, concat_axis=0, tiled=True, axis...  18.4 us
    all_to_all x1, waiting for transfers between devices, shards(): lax.all_to_all(total.astype(BF), 'trk', split_axis=0, concat_axis=0, tile...  11.3 us
    all_to_all x1, waiting for transfers between devices, shards(): row = lax.all_to_all(both, 'trk', split_axis=0, concat_axis=0, tiled=True)  10.4 us
    all_to_all x1, waiting for transfers between devices, shards(): back = lax.all_to_all(cells, 'trk', split_axis=0, concat_axis=0, tiled=True)  9.24 us
    all_to_all x1, starting transfers between devices, shards(): row = lax.all_to_all(both, 'trk', split_axis=0, concat_axis=0, tiled=True)  5.15 us
    pallas_call x1, Pallas kernels, shards(): pl.pallas_call(functools.partial(row_kernel, groups), out_shape=(jax.Shap...  4.28 us
    ppermute x1, starting transfers between devices, shards(): held = jnp.stack([own, lax.ppermute(own, 'trk', ring(count, fan))])  4.1 us
    ppermute x1, waiting for transfers between devices, shards(): held = jnp.stack([own, lax.ppermute(own, 'trk', ring(count, fan))])  3.86 us
  transfers between devices with their start and end apart: 7, of which 5 were waited for; matrix products, arithmetic and copies ran while one was open for 4% of the time, Pallas kernels for 0%

profile of v1, /device:TPU:0, one launch (start us, length us, event | category | flops | bytes accessed | tf_op | source)
XLA Modules:
  0.0 89.7 jit_solution(3391853390181360291)
XLA Ops:
  0.6 0.0 copy-start.4
  0.6 0.0 copy-start.5
  0.7 4.1 %collective-permute-start = (bf16[4,32,256]{2,1,0:T(8,128)(2,1)}, bf16[4,32,256]{2,1,0:T(8,128)(2,1)S(1)}, u32[]{:S(2)}, u32[]{:S(2)}) collective-permute-start(bf16[4,32,256]{2,1,0:T(8,128)(2,1)} %bitcast.25), channel_id=1, source_target_pairs={{0,8},{1,9},{2,10},{3,11},{4,12},{5,13},{6,14},{7,15},{8,0},{9,1},... | collective-permute-start | bytes 196616 | tf_op jit(solution)/shard_map/ppermute | solution.py:142
  4.8 3.9 %collective-permute-done = bf16[4,32,256]{2,1,0:T(8,128)(2,1)S(1)} collective-permute-done((bf16[4,32,256]{2,1,0:T(8,128)(2,1)}, bf16[4,32,256]{2,1,0:T(8,128)(2,1)S(1)}, u32[]{:S(2)}, u32[]{:S(2)}) %collective-permute-start) | collective-permute-done | bytes 65568 | tf_op jit(solution)/shard_map/ppermute | solution.py:142
  8.6 0.9 pad_maximum_fusion.1
  9.5 0.0 copy-start.3
  9.5 0.1 broadcast_in_dim.10
  9.6 18.4 %all_to_all.20.refs_0_ = bf16[8,2,4,32,256]{4,3,2,1,0:T(8,128)(2,1)S(1)} all-to-all(bf16[8,2,4,32,256]{4,3,2,1,0:T(8,128)(2,1)S(1)} %broadcast_in_dim.10), channel_id=1, replica_groups={{0,1,2,3,4,5,6,7},{8,9,10,11,12,13,14,15},{16,17,18,19,20,21,22,23},{24..., dimensions={0} | all-to-all | bytes 2097152 | tf_op jit(solution)/shard_map/all_to_all | solution.py:144
  28.0 0.0 collective-permute-start.1
  28.0 0.0 copy-done.4
  28.0 0.0 copy-done.5
  28.0 0.7 pad_maximum_fusion
  28.7 5.1 %all-to-all-start = ((bf16[16,16,512]{2,1,0:T(8,128)(2,1)}), bf16[16,16,512]{2,1,0:T(8,128)(2,1)S(1)}, u32[]{:S(2)}, u32[]{:S(2)}) async-start(bf16[16,16,512]{2,1,0:T(8,128)(2,1)} %pad_maximum_fusion), calls=%async_computation | async-start | bytes 524288 | tf_op jit(solution)/shard_map/all_to_all | solution.py:140
  33.9 0.1 pad_add_fusion.place
  33.9 10.4 %all-to-all-done.rows_ref = bf16[16,16,512]{2,1,0:T(8,128)(2,1)S(1)} async-done(((bf16[16,16,512]{2,1,0:T(8,128)(2,1)}), bf16[16,16,512]{2,1,0:T(8,128)(2,1)S(1)}, u32[]{:S(2)}, u32[]{:S(2)}) %all-to-all-start) | async-done | bytes 262176 | tf_op jit(solution)/shard_map/all_to_all | solution.py:140
  44.4 0.0 collective-permute-done.1.refs_1_
  44.4 0.0 copy-start
  44.4 1.0 %copy-done = bf16[8,2,4,32,256]{4,3,2,1,0:T(8,128)(2,1)} copy-done((bf16[8,2,4,32,256]{4,3,2,1,0:T(8,128)(2,1)}, bf16[8,2,4,32,256]{4,3,2,1,0:T(8,128)(2,1)S(1)}, u32[]{:S(2)}) %copy-start) | copy-done | bytes 1048600
  45.4 0.0 copy-done.3
  45.4 0.0 copy-start.1
  45.4 1.2 %copy-done.1 = bf16[8,2,4,32,256]{4,3,2,1,0:T(8,128)(2,1)S(1)} copy-done((bf16[8,2,4,32,256]{4,3,2,1,0:T(8,128)(2,1)S(1)}, bf16[8,2,4,32,256]{4,3,2,1,0:T(8,128)(2,1)}, u32[]{:S(2)}) %copy-start.1) | copy-done | bytes 1048600
  46.6 4.3 %shard_map.67 = (bf16[2,8,2,4,32,256]{5,4,3,2,1,0:T(8,128)(2,1)S(1)}, bf16[16,16,512]{2,1,0:T(8,128)(2,1)S(1)}) custom-call(s32[2]{0:T(128)S(1)} %pad_add_fusion.place, bf16[16,16,512]{2,1,0:T(8,128)(2,1)S(1)} %all-to-all-done.rows_ref, f32[1,512]{1,0:T(1,128)S(1)} %bitcast.24, bf16[8,2,4,32,256]{4,3,2,1,0:T(8,128)(2,1)S(1)} %all_to_all.20.refs_0_, ...), custom_call_target="tpu_custom_call" | custom-call | tf_op jit(solution)/shard_map/pallas_call | solution.py:154
  50.9 0.0 copy-start.2
  50.9 1.1 %slice_bitcast_fusion = bf16[8,2,4,32,256]{4,3,2,1,0:T(8,128)(2,1)} fusion(bf16[2,8,2,4,32,256]{5,4,3,2,1,0:T(8,128)(2,1)S(1)} %get-tuple-element.6), kind=kLoop, calls=%fused_computation.3 | loop fusion | bytes 2097152 | tf_op jit(solution)/shard_map/squeeze | solution.py:173
  52.0 0.0 collective-permute-start.2
  52.0 0.0 copy-done.2
  52.0 3.6 %all-to-all-start.2 = ((bf16[16,16,512]{2,1,0:T(8,128)(2,1)}), bf16[16,16,512]{2,1,0:T(8,128)(2,1)S(1)}, u32[]{:S(2)}, u32[]{:S(2)}) async-start(bf16[16,16,512]{2,1,0:T(8,128)(2,1)} %copy-done.2), calls=%async_computation.2 | async-start | bytes 524288 | tf_op jit(solution)/shard_map/all_to_all | solution.py:174
  55.5 0.0 collective-permute-done.2
  55.5 1.4 %fusion = bf16[8,2,4,32,256]{4,3,2,1,0:T(8,128)(2,1)} fusion(bf16[8,2,4,32,256]{4,3,2,1,0:T(8,128)(2,1)S(1)} %collective-permute-done.2, bf16[2,8,2,4,32,256]{5,4,3,2,1,0:T(8,128)(2,1)S(1)} %get-tuple-element.6), kind=kLoop, calls=%fused_computation.1 | loop fusion | flops 2097152 | bytes 3145728 | tf_op jit(solution)/shard_map/convert_element_type | solution.py:176
  57.0 9.2 %all-to-all-done.2 = bf16[16,16,512]{2,1,0:T(8,128)(2,1)S(1)} async-done(((bf16[16,16,512]{2,1,0:T(8,128)(2,1)}), bf16[16,16,512]{2,1,0:T(8,128)(2,1)S(1)}, u32[]{:S(2)}, u32[]{:S(2)}) %all-to-all-start.2) | async-done | bytes 262176 | tf_op jit(solution)/shard_map/all_to_all | solution.py:174
  66.2 3.6 %all-to-all-start.3 = ((bf16[8,2,4,32,256]{4,3,2,1,0:T(8,128)(2,1)}), bf16[8,2,4,32,256]{4,3,2,1,0:T(8,128)(2,1)S(1)}, u32[]{:S(2)}, u32[]{:S(2)}) async-start(bf16[8,2,4,32,256]{4,3,2,1,0:T(8,128)(2,1)} %fusion), calls=%async_computation.3 | async-start | bytes 2097152 | tf_op jit(solution)/shard_map/all_to_all | solution.py:175
  69.8 2.5 %psum.7 = f32[512]{0:T(512)S(1)} all-reduce(f32[512]{0:T(512)S(1)} %convert_reduce_fusion.1), channel_id=1, replica_groups=mesh['grp'=2,'trk'=16] {'grp'}, use_global_device_ids=true, to_apply=%region_2.3 | all-reduce | flops 512 | bytes 4096 | tf_op jit(solution)/shard_map/psum | solution.py:182
  72.3 11.3 %all-to-all-done.3 = bf16[8,2,4,32,256]{4,3,2,1,0:T(8,128)(2,1)S(1)} async-done(((bf16[8,2,4,32,256]{4,3,2,1,0:T(8,128)(2,1)}), bf16[8,2,4,32,256]{4,3,2,1,0:T(8,128)(2,1)S(1)}, u32[]{:S(2)}, u32[]{:S(2)}) %all-to-all-start.3) | async-done | bytes 1048608 | tf_op jit(solution)/shard_map/all_to_all | solution.py:175
  83.6 0.2 convert_reduce_fusion
  83.8 1.5 %collective-permute-start.3 = (bf16[4,32,256]{2,1,0:T(8,128)(2,1)S(1)}, bf16[4,32,256]{2,1,0:T(8,128)(2,1)S(1)}, u32[]{:S(2)}, u32[]{:S(2)}) collective-permute-start(bf16[4,32,256]{2,1,0:T(8,128)(2,1)S(1)} %fusion.4), channel_id=1, source_target_pairs={{0,8},{1,9},{2,10},{3,11},{4,12},{5,13},{6,14},{7,15},{8,0},{9,1},... | collective-permute-start | bytes 196616 | tf_op jit(solution)/shard_map/ppermute | solution.py:179
  85.3 0.6 broadcast_multiply_fusion
  85.9 0.7 slice.25
  86.6 2.5 %collective-permute-done.3 = bf16[4,32,256]{2,1,0:T(8,128)(2,1)S(1)} collective-permute-done((bf16[4,32,256]{2,1,0:T(8,128)(2,1)S(1)}, bf16[4,32,256]{2,1,0:T(8,128)(2,1)S(1)}, u32[]{:S(2)}, u32[]{:S(2)}) %collective-permute-start.3) | collective-permute-done | bytes 65568 | tf_op jit(solution)/shard_map/ppermute | solution.py:179
  89.0 0.7 fusion.3
  (2 shorter events, 0.1 us)
Async XLA Ops:
  0.6 27.3 %copy-start.4 = (bf16[16,8,512]{2,1,0:T(8,128)(2,1)S(1)}, bf16[16,8,512]{2,1,0:T(8,128)(2,1)}, u32[]{:S(2)}) copy-start(bf16[16,8,512]{2,1,0:T(8,128)(2,1)} %param.5) | copy-start | bytes 393220
  0.6 27.3 %copy-start.5 = (bf16[16,8,512]{2,1,0:T(8,128)(2,1)S(1)}, bf16[16,8,512]{2,1,0:T(8,128)(2,1)}, u32[]{:S(2)}) copy-start(bf16[16,8,512]{2,1,0:T(8,128)(2,1)} %param.4) | copy-start | bytes 393220
  0.7 8.0 %collective-permute-start = (bf16[4,32,256]{2,1,0:T(8,128)(2,1)}, bf16[4,32,256]{2,1,0:T(8,128)(2,1)S(1)}, u32[]{:S(2)}, u32[]{:S(2)}) collective-permute-start(bf16[4,32,256]{2,1,0:T(8,128)(2,1)} %bitcast.25), channel_id=1, source_target_pairs={{0,8},{1,9},{2,10},{3,11},{4,12},{5,13},{6,14},{7,15},{8,0},{9,1},... | collective-permute-start | bytes 196616 | tf_op jit(solution)/shard_map/ppermute | solution.py:142
  9.5 35.9 %copy-start.3 = (f32[512]{0:T(512)S(1)}, f32[512]{0:T(512)}, u32[]{:S(2)}) copy-start(f32[512]{0:T(512)} %param.6) | copy-start | bytes 6148
  28.0 16.4 %collective-permute-start.1 = (bf16[8,2,4,32,256]{4,3,2,1,0:T(8,128)(2,1)S(1)}, bf16[8,2,4,32,256]{4,3,2,1,0:T(8,128)(2,1)S(1)}, u32[]{:S(2)}, u32[]{:S(2)}) collective-permute-start(bf16[8,2,4,32,256]{4,3,2,1,0:T(8,128)(2,1)S(1)} %all_to_all.20.refs_0_), channel_id=1, source_target_pairs={{0,16},{16,0},{1,17},{17,1},{2,18},{18,2},{3,19},{19,3},{4,20},{20... | collective-permute-start | bytes 3145736 | tf_op jit(solution)/shard_map/ppermute | solution.py:147
  28.7 15.7 %all-to-all-start = ((bf16[16,16,512]{2,1,0:T(8,128)(2,1)}), bf16[16,16,512]{2,1,0:T(8,128)(2,1)S(1)}, u32[]{:S(2)}, u32[]{:S(2)}) async-start(bf16[16,16,512]{2,1,0:T(8,128)(2,1)} %pad_maximum_fusion), calls=%async_computation | async-start | bytes 524288 | tf_op jit(solution)/shard_map/all_to_all | solution.py:140
  44.4 1.0 %copy-start = (bf16[8,2,4,32,256]{4,3,2,1,0:T(8,128)(2,1)}, bf16[8,2,4,32,256]{4,3,2,1,0:T(8,128)(2,1)S(1)}, u32[]{:S(2)}) copy-start(bf16[8,2,4,32,256]{4,3,2,1,0:T(8,128)(2,1)S(1)} %collective-permute-done.1.refs_1_) | copy-start | bytes 3145732
  45.4 1.2 %copy-start.1 = (bf16[8,2,4,32,256]{4,3,2,1,0:T(8,128)(2,1)S(1)}, bf16[8,2,4,32,256]{4,3,2,1,0:T(8,128)(2,1)}, u32[]{:S(2)}) copy-start(bf16[8,2,4,32,256]{4,3,2,1,0:T(8,128)(2,1)} %copy-done) | copy-start | bytes 3145732
  50.9 1.1 %copy-start.2 = (bf16[16,16,512]{2,1,0:T(8,128)(2,1)}, bf16[16,16,512]{2,1,0:T(8,128)(2,1)S(1)}, u32[]{:S(2)}) copy-start(bf16[16,16,512]{2,1,0:T(8,128)(2,1)S(1)} %get-tuple-element.5) | copy-start | bytes 786436
  52.0 3.6 %collective-permute-start.2 = (bf16[8,2,4,32,256]{4,3,2,1,0:T(8,128)(2,1)}, bf16[8,2,4,32,256]{4,3,2,1,0:T(8,128)(2,1)S(1)}, u32[]{:S(2)}, u32[]{:S(2)}) collective-permute-start(bf16[8,2,4,32,256]{4,3,2,1,0:T(8,128)(2,1)} %slice_bitcast_fusion), channel_id=1, source_target_pairs={{0,16},{16,0},{1,17},{17,1},{2,18},{18,2},{3,19},{19,3},{4,20},{20... | collective-permute-start | bytes 3145736 | tf_op jit(solution)/shard_map/ppermute | solution.py:173
  52.0 14.2 %all-to-all-start.2 = ((bf16[16,16,512]{2,1,0:T(8,128)(2,1)}), bf16[16,16,512]{2,1,0:T(8,128)(2,1)S(1)}, u32[]{:S(2)}, u32[]{:S(2)}) async-start(bf16[16,16,512]{2,1,0:T(8,128)(2,1)} %copy-done.2), calls=%async_computation.2 | async-start | bytes 524288 | tf_op jit(solution)/shard_map/all_to_all | solution.py:174
  66.2 17.4 %all-to-all-start.3 = ((bf16[8,2,4,32,256]{4,3,2,1,0:T(8,128)(2,1)}), bf16[8,2,4,32,256]{4,3,2,1,0:T(8,128)(2,1)S(1)}, u32[]{:S(2)}, u32[]{:S(2)}) async-start(bf16[8,2,4,32,256]{4,3,2,1,0:T(8,128)(2,1)} %fusion), calls=%async_computation.3 | async-start | bytes 2097152 | tf_op jit(solution)/shard_map/all_to_all | solution.py:175
  83.8 5.2 %collective-permute-start.3 = (bf16[4,32,256]{2,1,0:T(8,128)(2,1)S(1)}, bf16[4,32,256]{2,1,0:T(8,128)(2,1)S(1)}, u32[]{:S(2)}, u32[]{:S(2)}) collective-permute-start(bf16[4,32,256]{2,1,0:T(8,128)(2,1)S(1)} %fusion.4), channel_id=1, source_target_pairs={{0,8},{1,9},{2,10},{3,11},{4,12},{5,13},{6,14},{7,15},{8,0},{9,1},... | collective-permute-start | bytes 196616 | tf_op jit(solution)/shard_map/ppermute | solution.py:179

commit v2 on v1

--- a/solution.py
+++ b/solution.py
@@ -16,28 +16,36 @@
     return lax.dot_general(a, b, (dims, ((), ())), preferred_element_type=F32)
 
 
-def row_kernel(groups, place, rows_ref, gain_ref, *refs):
-    w_refs, rest = refs[:groups], refs[groups:]
-    wg_ref, cells_ref, w_all, norm_s, att_s = rest
-    group, half_at = place[0], place[1]
+def row_kernel(groups, offsets, place, rows_ref, gain_ref, *refs):
+    w_refs, rest = refs[: groups * len(offsets)], refs[groups * len(offsets) :]
+    wg_refs, cells_ref, (w_all, norm_s, att_s, sems) = rest[:groups], rest[groups], rest[groups + 1 :]
+    group, track = place[0], place[1]
     senders, pair, _ = rows_ref.shape
     tracks = pair // 2
     width = gain_ref.shape[1]
     length = senders * tracks
-    fan, halves, _, cols, part = w_refs[0].shape
+    fan, halves, _, cols, part = wg_refs[0].shape
+    half_at = track // fan
+    copies = []
+    for step in range(groups):
+        owner = lax.rem(group - step + groups, groups)
+        lanes = pl.ds(pl.multiple_of(owner * part, part), part)
+        for at, held in enumerate(offsets):
+            for slot, offset in enumerate(held):
+                size = w_refs[0].shape[2]
+                begin = (track ^ offset) * size if len(offsets) > 1 else 0
+                rows = pl.ds(pl.multiple_of(begin, size), size)
+                copy = pltpu.make_async_copy(
+                    w_refs[step * len(offsets) + at].at[slot],
+                    w_all.at[:, rows, lanes],
+                    sems.at[len(copies)],
+                )
+                copy.start()
+                copies.append(copy)
     both = rows_ref[...].astype(F32)
     values = both[:, :tracks].reshape(length, width)
     upstream = both[:, tracks:].reshape(length, width)
     gain = gain_ref[...]
-    for step in range(groups):
-        owner = lax.rem(group - step + groups, groups)
-        lanes = pl.ds(pl.multiple_of(owner * part, part), part)
-        for far in range(halves):
-            base = lax.rem(half_at + far, halves) * (fan * cols)
-            for near in range(fan):
-                at = pl.ds(pl.multiple_of(base + near * cols, cols), cols)
-                for index in range(4):
-                    w_all[index, at, lanes] = w_refs[step][near, far, index]
     row_mean = jnp.mean(values, -1, keepdims=True)
     offset = values - row_mean
     row_var = jnp.mean(offset * offset, -1, keepdims=True)
@@ -45,6 +53,8 @@
     centred = offset * inv_std
     normed = (centred * gain).astype(BF)
     up = upstream.astype(BF)
+    for copy in copies:
+        copy.wait()
     projected = [dot(normed, w_all[index], ((1,), (1,))).astype(BF) for index in range(3)]
     grad_att = dot(up, w_all[3], ((1,), (0,))).astype(BF)
     size = width // HEADS
@@ -108,23 +118,42 @@
             for far in range(halves):
                 to = lax.rem(half_at + far, halves)
                 for near in range(fan):
-                    wg_ref[step, near, to, index] = block[far, near]
+                    wg_refs[step][near, to, index] = block[far, near]
 
 
 def ring(size, step):
     return [(i, (i + step) % size) for i in range(size)]
 
 
-def join_blocks(blocks, half_at):
-    fan, halves, four, cols, part = blocks.shape
-    blocks = jnp.where(half_at == 0, blocks, blocks[:, ::-1])
-    return blocks.transpose(2, 1, 0, 3, 4).reshape(1, 1, four, halves * fan * cols, part)
+def join_blocks(parts, offsets, track):
+    blocks = jnp.concatenate(parts)
+    order = [offset for held in offsets for offset in held]
+    where = [order.index(offset) for offset in range(len(order))]
+    blocks = jnp.take(blocks, jnp.array(where)[track ^ jnp.arange(len(order))], axis=0)
+    count, four, cols, part = blocks.shape
+    return blocks.transpose(1, 0, 2, 3).reshape(1, four, count * cols, part)
 
 
 def cut_blocks(joined, half_at, shape):
     fan, halves, four, cols, part = shape
-    blocks = joined.reshape(-1, four, halves, fan, cols, part).transpose(0, 3, 2, 1, 4, 5)
-    return jnp.where(half_at == 0, blocks, blocks[:, :, ::-1])
+    blocks = joined.reshape(four, halves, fan, cols, part).transpose(2, 1, 0, 3, 4)
+    return jnp.where(half_at == 0, blocks, blocks[:, ::-1])
+
+
+def gather_blocks(block, axis):
+    count = lax.axis_size(axis)
+
+    def swap(array, bits):
+        return lax.ppermute(array, axis, [(i, i ^ bits) for i in range(count)])
+
+    held, order, bit = block[None], [0], count // 2
+    while bit >= 4:
+        held = jnp.concatenate([held, swap(held, bit)])
+        order = order + [offset ^ bit for offset in order]
+        bit //= 2
+    close = range(2 * bit)
+    parts = [swap(held, bits) if bits else held for bits in close]
+    return parts, [[offset ^ bits for offset in order] for bits in close]
 
 
 def shards(fields, upstream, ln_gain, weights):
@@ -138,36 +167,37 @@
     half_at = track // fan
     both = jnp.concatenate([fields, upstream], 1)
     row = lax.all_to_all(both, "trk", split_axis=0, concat_axis=0, tiled=True)
-    own = weights.transpose(0, 2, 1)
-    held = jnp.stack([own, lax.ppermute(own, "trk", ring(count, fan))])
-    sent = jnp.broadcast_to(held[None], (fan,) + held.shape)
-    w_part = lax.all_to_all(
-        sent, "trk", split_axis=0, concat_axis=0, tiled=True, axis_index_groups=near
-    )
-    w_parts = [w_part] + [lax.ppermute(w_part, "grp", ring(groups, k)) for k in range(1, groups)]
-    blocks_shape = w_part.shape
+    parts, offsets = gather_blocks(weights.transpose(0, 2, 1), "trk")
+    blocks_shape = (fan, 2, 4, cols, part)
+    out_shape = blocks_shape
     narrow = cols % 16 != 0
     if narrow:
-        w_parts = [join_blocks(blocks, half_at) for blocks in w_parts]
-    place = jnp.stack([group, half_at]).astype(jnp.int32)
+        parts, offsets = [join_blocks(parts, offsets, track)], [[0]]
+        out_shape = (1, 1, 4, count * cols, part)
+    w_parts = [
+        lax.ppermute(held, "grp", ring(groups, k)) if k else held
+        for k in range(groups)
+        for held in parts
+    ]
+    place = jnp.stack([group, track]).astype(jnp.int32)
     vmem = pl.BlockSpec(memory_space=pltpu.VMEM)
-    wg, cells = pl.pallas_call(
-        functools.partial(row_kernel, groups),
-        out_shape=(
-            jax.ShapeDtypeStruct((groups,) + w_parts[0].shape, BF),
-            jax.ShapeDtypeStruct((count, 2 * trk_dev, width), BF),
-        ),
-        in_specs=[pl.BlockSpec(memory_space=pltpu.SMEM)] + [vmem] * (2 + groups),
-        out_specs=(vmem, vmem),
+    *wg, cells = pl.pallas_call(
+        functools.partial(row_kernel, groups, offsets),
+        out_shape=(jax.ShapeDtypeStruct(out_shape, BF),) * groups
+        + (jax.ShapeDtypeStruct((count, 2 * trk_dev, width), BF),),
+        in_specs=[pl.BlockSpec(memory_space=pltpu.SMEM), vmem, vmem]
+        + [pl.BlockSpec(memory_space=pl.ANY)] * len(w_parts),
+        out_specs=(vmem,) * (groups + 1),
         scratch_shapes=[
             pltpu.VMEM((4, width, width), BF),
             pltpu.VMEM((groups, trk_dev * count, part), BF),
             pltpu.VMEM((groups, trk_dev * count, part), BF),
+            pltpu.SemaphoreType.DMA((groups * sum(len(held) for held in offsets),)),
         ],
         compiler_params=pltpu.CompilerParams(vmem_limit_bytes=48 * 2**20),
     )(place, row, ln_gain[None], *w_parts)
     if narrow:
-        wg = cut_blocks(wg, half_at, blocks_shape)
+        wg = [cut_blocks(blocks, half_at, blocks_shape) for blocks in wg]
     total = wg[0].astype(F32)
     for k in range(1, groups):
         total = total + lax.ppermute(wg[k], "grp", ring(groups, k)).astype(F32)

time: 90.2 us -> 80.8 us (0.90)
  blocking collectives: 20.8 us -> 2.47 us
  starting transfers between devices: 17.9 us -> 24.8 us
  local copies, waits for them, and re-layouts: 4.06 us -> 1.38 us
  other arithmetic: 4.56 us -> 6.41 us
  Pallas kernels: 4.28 us -> 5.91 us
  waiting for transfers between devices: 37.3 us -> 38.6 us
    all_to_all x1 -> x0, blocking collectives: 18.4 us -> none  [shards(): lax.all_to_all(sent, 'trk', split_axis=0, concat_axis=0, tiled=True, axis...]
    ppermute x2 -> x9, starting transfers between devices: 4.1 us -> 9.46 us  [the longest x5 8.39 us: swap(): return lax.ppermute(array, axis, [(i, i ^ bits) for i in range(count)])]
    ppermute x2 -> x9, waiting for transfers between devices: 3.86 us -> 8.6 us  [the longest x5 8.17 us: swap(): return lax.ppermute(array, axis, [(i, i ^ bits) for i in range(count)])]
    all_to_all x1, waiting for transfers between devices: 10.4 us -> 6.9 us  [shards(): row = lax.all_to_all(both, 'trk', split_axis=0, concat_axis=0, tiled=True)]
    concatenate x0 -> x2, other arithmetic: none -> 1.72 us  [gather_blocks(): held = jnp.concatenate([held, swap(held, bit)])]
    pallas_call x1, Pallas kernels: 4.28 us -> 5.91 us  [shards(): pl.pallas_call(functools.partial(row_kernel, groups, offsets), out_shape=...]
    all_to_all x1, starting transfers between devices: 5.15 us -> 6.75 us  [shards(): row = lax.all_to_all(both, 'trk', split_axis=0, concat_axis=0, tiled=True)]
    unnamed x12 -> x4, local copies, waits for them, and re-layouts: 2.21 us -> 0.7 us
  transfers between devices with their start and end apart: 7 -> 14, of which waited for: 5 -> 7; matrix products, arithmetic and copies ran while one was open for 4% -> 6% of each run, Pallas kernels for 0% -> 0%
where the time goes in v2:
time: 80.8 us; the launch traced here: 80.3 us
  waiting for transfers between devices  38.6 us (48%)
  starting transfers between devices  24.8 us (31%)
  other arithmetic  6.41 us (8%)
  Pallas kernels  5.91 us (7%)
  blocking collectives  2.47 us (3%)
  local copies, waits for them, and re-layouts  1.38 us (2%)
    all_to_all x1, waiting for transfers between devices, shards(): lax.all_to_all(total.astype(BF), 'trk', split_axis=0, concat_axis=0, tile...  11.4 us
    all_to_all x1, waiting for transfers between devices, shards(): back = lax.all_to_all(cells, 'trk', split_axis=0, concat_axis=0, tiled=True)  9.22 us
    ppermute x5, starting transfers between devices, swap(): return lax.ppermute(array, axis, [(i, i ^ bits) for i in range(count)])  8.39 us
    ppermute x5, waiting for transfers between devices, swap(): return lax.ppermute(array, axis, [(i, i ^ bits) for i in range(count)])  8.17 us
    all_to_all x1, waiting for transfers between devices, shards(): row = lax.all_to_all(both, 'trk', split_axis=0, concat_axis=0, tiled=True)  6.9 us
    all_to_all x1, starting transfers between devices, shards(): row = lax.all_to_all(both, 'trk', split_axis=0, concat_axis=0, tiled=True)  6.75 us
    pallas_call x1, Pallas kernels, shards(): pl.pallas_call(functools.partial(row_kernel, groups, offsets), out_shape=...  5.91 us
    all_to_all x1, starting transfers between devices, shards(): lax.all_to_all(total.astype(BF), 'trk', split_axis=0, concat_axis=0, tile...  3.56 us
  transfers between devices with their start and end apart: 14, of which 7 were waited for; matrix products, arithmetic and copies ran while one was open for 6% of the time, Pallas kernels for 0%

profile of v2, /device:TPU:0, one launch (start us, length us, event | category | flops | bytes accessed | tf_op | source)
XLA Modules:
  0.0 80.3 jit_solution(11161118761633942090)
XLA Ops:
  0.6 0.0 copy-start.1
  0.6 4.1 %collective-permute-start = (bf16[1,4,32,256]{3,2,1,0:T(8,128)(2,1)}, bf16[1,4,32,256]{3,2,1,0:T(8,128)(2,1)S(1)}, u32[]{:S(2)}, u32[]{:S(2)}) collective-permute-start(bf16[1,4,32,256]{3,2,1,0:T(8,128)(2,1)} %bitcast.19), channel_id=1, source_target_pairs={{0,8},{1,9},{2,10},{3,11},{4,12},{5,13},{6,14},{7,15},{8,0},{9,1},... | collective-permute-start | bytes 196616 | tf_op jit(solution)/shard_map/ppermute | solution.py:147
  4.7 3.9 %collective-permute-done = bf16[1,4,32,256]{3,2,1,0:T(8,128)(2,1)S(1)} collective-permute-done((bf16[1,4,32,256]{3,2,1,0:T(8,128)(2,1)}, bf16[1,4,32,256]{3,2,1,0:T(8,128)(2,1)S(1)}, u32[]{:S(2)}, u32[]{:S(2)}) %collective-permute-start) | collective-permute-done | bytes 65568 | tf_op jit(solution)/shard_map/ppermute | solution.py:147
  8.6 0.9 %pad_maximum_fusion.2 = bf16[2,4,32,256]{3,2,1,0:T(8,128)(2,1)S(1)} fusion(bf16[1,4,32,256]{3,2,1,0:T(8,128)(2,1)S(1)} %collective-permute-done, bf16[1,4,32,256]{3,2,1,0:T(8,128)(2,1)} %bitcast.20), kind=kLoop, calls=%fused_computation.9 | loop fusion | flops 65536 | bytes 262144 | tf_op jit(solution)/shard_map/concatenate | solution.py:151
  9.5 0.7 collective-permute-start.1
  10.2 4.3 %collective-permute-done.1 = bf16[2,4,32,256]{3,2,1,0:T(8,128)(2,1)S(1)} collective-permute-done((bf16[2,4,32,256]{3,2,1,0:T(8,128)(2,1)S(1)}, bf16[2,4,32,256]{3,2,1,0:T(8,128)(2,1)S(1)}, u32[]{:S(2)}, u32[]{:S(2)}) %collective-permute-start.1) | collective-permute-done | bytes 131104 | tf_op jit(solution)/shard_map/ppermute | solution.py:147
  14.5 0.9 %pad_maximum_fusion.1.refs_0_ = bf16[4,4,32,256]{3,2,1,0:T(8,128)(2,1)S(1)} fusion(bf16[2,4,32,256]{3,2,1,0:T(8,128)(2,1)S(1)} %collective-permute-done.1, bf16[1,4,32,256]{3,2,1,0:T(8,128)(2,1)S(1)} %collective-permute-done, bf16[1,4,32,256]{3,2,1,0:T(8,128)(2,1)} %bitcast.21), kind=kLoop, calls=%fused_computation.3 | loop fusion | flops 262144 | bytes 524288 | tf_op jit(solution)/shard_map/concatenate | solution.py:151
  15.4 2.7 %collective-permute-start.4 = (bf16[4,4,32,256]{3,2,1,0:T(8,128)(2,1)S(1)}, bf16[4,4,32,256]{3,2,1,0:T(8,128)(2,1)S(1)}, u32[]{:S(2)}, u32[]{:S(2)}) collective-permute-start(bf16[4,4,32,256]{3,2,1,0:T(8,128)(2,1)S(1)} %pad_maximum_fusion.1.refs_0_), channel_id=1, source_target_pairs={{0,3},{1,2},{2,1},{3,0},{4,7},{5,6},{6,5},{7,4},{8,11},{9,10},{10,... | collective-permute-start | bytes 786440 | tf_op jit(solution)/shard_map/ppermute | solution.py:147
  18.1 0.5 collective-permute-start.3
  18.6 0.3 collective-permute-start.2
  18.9 1.7 %pad_maximum_fusion = bf16[16,16,512]{2,1,0:T(8,128)(2,1)} fusion(bf16[16,8,512]{2,1,0:T(8,128)(2,1)} %param.5, bf16[16,8,512]{2,1,0:T(8,128)(2,1)} %param.4), kind=kLoop, calls=%fused_computation.2 | loop fusion | flops 524288 | bytes 524288 | tf_op jit(solution)/shard_map/concatenate | solution.py:168
  20.6 6.7 %all-to-all-start = ((bf16[16,16,512]{2,1,0:T(8,128)(2,1)}), bf16[16,16,512]{2,1,0:T(8,128)(2,1)S(1)}, u32[]{:S(2)}, u32[]{:S(2)}) async-start(bf16[16,16,512]{2,1,0:T(8,128)(2,1)} %pad_maximum_fusion), calls=%async_computation | async-start | bytes 524288 | tf_op jit(solution)/shard_map/all_to_all | solution.py:169
  27.4 0.1 collective-permute-start.5
  27.5 0.0 collective-permute-done.4.refs_3_
  27.5 0.5 collective-permute-start.8
  28.0 0.0 collective-permute-done.3.refs_2_
  28.0 0.1 collective-permute-start.7
  28.0 0.0 collective-permute-done.2.refs_1_
  28.0 0.4 collective-permute-start.6
  28.5 0.1 pad_add_fusion.place
  28.5 0.4 collective-permute-done.5.refs_4_
  29.0 6.9 %all-to-all-done.rows_ref = bf16[16,16,512]{2,1,0:T(8,128)(2,1)S(1)} async-done(((bf16[16,16,512]{2,1,0:T(8,128)(2,1)}), bf16[16,16,512]{2,1,0:T(8,128)(2,1)S(1)}, u32[]{:S(2)}, u32[]{:S(2)}) %all-to-all-start) | async-done | bytes 262176 | tf_op jit(solution)/shard_map/all_to_all | solution.py:169
  35.9 0.0 collective-permute-done.8.refs_7_
  35.9 0.0 collective-permute-done.7.refs_6_
  35.9 0.0 collective-permute-done.6.refs_5_
  35.9 0.0 copy-done.1
  35.9 5.9 %shard_map.67 = (bf16[8,2,4,32,256]{4,3,2,1,0:T(8,128)(2,1)S(1)}, bf16[8,2,4,32,256]{4,3,2,1,0:T(8,128)(2,1)}, bf16[16,16,512]{2,1,0:T(8,128)(2,1)S(1)}) custom-call(s32[2]{0:T(128)S(1)} %pad_add_fusion.place, bf16[16,16,512]{2,1,0:T(8,128)(2,1)S(1)} %all-to-all-done.rows_ref, f32[1,512]{1,0:T(1,128)S(1)} %bitcast.18, ...), custom_call_target="tpu_custom_call" | custom-call | tf_op jit(solution)/shard_map/pallas_call | solution.py:184
  41.8 0.0 copy-start
  41.8 0.7 copy-done
  42.5 0.0 collective-permute-start.9
  42.5 3.5 %all-to-all-start.1 = ((bf16[16,16,512]{2,1,0:T(8,128)(2,1)}), bf16[16,16,512]{2,1,0:T(8,128)(2,1)S(1)}, u32[]{:S(2)}, u32[]{:S(2)}) async-start(bf16[16,16,512]{2,1,0:T(8,128)(2,1)} %copy-done), calls=%async_computation.1 | async-start | bytes 524288 | tf_op jit(solution)/shard_map/all_to_all | solution.py:204
  46.1 0.0 collective-permute-done.9
  46.1 1.4 %add_convert_fusion = bf16[8,2,4,32,256]{4,3,2,1,0:T(8,128)(2,1)} fusion(bf16[8,2,4,32,256]{4,3,2,1,0:T(8,128)(2,1)S(1)} %collective-permute-done.9, bf16[8,2,4,32,256]{4,3,2,1,0:T(8,128)(2,1)S(1)} %get-tuple-element.7), kind=kLoop, calls=%fused_computation.1 | loop fusion | flops 2097152 | bytes 3145728 | tf_op jit(solution)/shard_map/convert_element_type | solution.py:206
  47.5 9.2 %all-to-all-done.1 = bf16[16,16,512]{2,1,0:T(8,128)(2,1)S(1)} async-done(((bf16[16,16,512]{2,1,0:T(8,128)(2,1)}), bf16[16,16,512]{2,1,0:T(8,128)(2,1)S(1)}, u32[]{:S(2)}, u32[]{:S(2)}) %all-to-all-start.1) | async-done | bytes 262176 | tf_op jit(solution)/shard_map/all_to_all | solution.py:204
  56.7 3.6 %all-to-all-start.2 = ((bf16[8,2,4,32,256]{4,3,2,1,0:T(8,128)(2,1)}), bf16[8,2,4,32,256]{4,3,2,1,0:T(8,128)(2,1)S(1)}, u32[]{:S(2)}, u32[]{:S(2)}) async-start(bf16[8,2,4,32,256]{4,3,2,1,0:T(8,128)(2,1)} %add_convert_fusion), calls=%async_computation.2 | async-start | bytes 2097152 | tf_op jit(solution)/shard_map/all_to_all | solution.py:205
  60.4 2.5 %psum.7 = f32[512]{0:T(512)S(1)} all-reduce(f32[512]{0:T(512)S(1)} %convert_reduce_fusion.1), channel_id=1, replica_groups=mesh['grp'=2,'trk'=16] {'grp'}, use_global_device_ids=true, to_apply=%region_2.0 | all-reduce | flops 512 | bytes 4096 | tf_op jit(solution)/shard_map/psum | solution.py:212
  62.8 11.4 %all-to-all-done.2 = bf16[8,2,4,32,256]{4,3,2,1,0:T(8,128)(2,1)S(1)} async-done(((bf16[8,2,4,32,256]{4,3,2,1,0:T(8,128)(2,1)}), bf16[8,2,4,32,256]{4,3,2,1,0:T(8,128)(2,1)S(1)}, u32[]{:S(2)}, u32[]{:S(2)}) %all-to-all-start.2) | async-done | bytes 1048608 | tf_op jit(solution)/shard_map/all_to_all | solution.py:205
  74.2 0.2 convert_reduce_fusion
  74.4 1.5 %collective-permute-start.10 = (bf16[4,32,256]{2,1,0:T(8,128)(2,1)S(1)}, bf16[4,32,256]{2,1,0:T(8,128)(2,1)S(1)}, u32[]{:S(2)}, u32[]{:S(2)}) collective-permute-start(bf16[4,32,256]{2,1,0:T(8,128)(2,1)S(1)} %fusion.3), channel_id=1, source_target_pairs={{0,8},{1,9},{2,10},{3,11},{4,12},{5,13},{6,14},{7,15},{8,0},{9,1},... | collective-permute-start | bytes 196616 | tf_op jit(solution)/shard_map/ppermute | solution.py:209
  75.9 0.6 broadcast_multiply_fusion
  76.4 0.7 slice.17
  77.1 2.5 %collective-permute-done.10 = bf16[4,32,256]{2,1,0:T(8,128)(2,1)S(1)} collective-permute-done((bf16[4,32,256]{2,1,0:T(8,128)(2,1)S(1)}, bf16[4,32,256]{2,1,0:T(8,128)(2,1)S(1)}, u32[]{:S(2)}, u32[]{:S(2)}) %collective-permute-start.10) | collective-permute-done | bytes 65568 | tf_op jit(solution)/shard_map/ppermute | solution.py:209
  79.6 0.7 fusion.2
  (2 shorter events, 0.1 us)
Async XLA Ops:
  0.6 35.3 %copy-start.1 = (f32[512]{0:T(512)S(1)}, f32[512]{0:T(512)}, u32[]{:S(2)}) copy-start(f32[512]{0:T(512)} %param.6) | copy-start | bytes 6148
  0.6 8.0 %collective-permute-start = (bf16[1,4,32,256]{3,2,1,0:T(8,128)(2,1)}, bf16[1,4,32,256]{3,2,1,0:T(8,128)(2,1)S(1)}, u32[]{:S(2)}, u32[]{:S(2)}) collective-permute-start(bf16[1,4,32,256]{3,2,1,0:T(8,128)(2,1)} %bitcast.19), channel_id=1, source_target_pairs={{0,8},{1,9},{2,10},{3,11},{4,12},{5,13},{6,14},{7,15},{8,0},{9,1},... | collective-permute-start | bytes 196616 | tf_op jit(solution)/shard_map/ppermute | solution.py:147
  9.5 5.0 %collective-permute-start.1 = (bf16[2,4,32,256]{3,2,1,0:T(8,128)(2,1)S(1)}, bf16[2,4,32,256]{3,2,1,0:T(8,128)(2,1)S(1)}, u32[]{:S(2)}, u32[]{:S(2)}) collective-permute-start(bf16[2,4,32,256]{3,2,1,0:T(8,128)(2,1)S(1)} %pad_maximum_fusion.2), channel_id=1, source_target_pairs={{0,4},{1,5},{2,6},{3,7},{4,0},{5,1},{6,2},{7,3},{8,12},{9,13},{10,... | collective-permute-start | bytes 393224 | tf_op jit(solution)/shard_map/ppermute | solution.py:147
  15.4 12.1 %collective-permute-start.4 = (bf16[4,4,32,256]{3,2,1,0:T(8,128)(2,1)S(1)}, bf16[4,4,32,256]{3,2,1,0:T(8,128)(2,1)S(1)}, u32[]{:S(2)}, u32[]{:S(2)}) collective-permute-start(bf16[4,4,32,256]{3,2,1,0:T(8,128)(2,1)S(1)} %pad_maximum_fusion.1.refs_0_), channel_id=1, source_target_pairs={{0,3},{1,2},{2,1},{3,0},{4,7},{5,6},{6,5},{7,4},{8,11},{9,10},{10,... | collective-permute-start | bytes 786440 | tf_op jit(solution)/shard_map/ppermute | solution.py:147
  18.1 9.9 %collective-permute-start.3 = (bf16[4,4,32,256]{3,2,1,0:T(8,128)(2,1)S(1)}, bf16[4,4,32,256]{3,2,1,0:T(8,128)(2,1)S(1)}, u32[]{:S(2)}, u32[]{:S(2)}) collective-permute-start(bf16[4,4,32,256]{3,2,1,0:T(8,128)(2,1)S(1)} %pad_maximum_fusion.1.refs_0_), channel_id=1, source_target_pairs={{0,2},{1,3},{2,0},{3,1},{4,6},{5,7},{6,4},{7,5},{8,10},{9,11},{10,... | collective-permute-start | bytes 786440 | tf_op jit(solution)/shard_map/ppermute | solution.py:147
  18.6 9.5 %collective-permute-start.2 = (bf16[4,4,32,256]{3,2,1,0:T(8,128)(2,1)S(1)}, bf16[4,4,32,256]{3,2,1,0:T(8,128)(2,1)S(1)}, u32[]{:S(2)}, u32[]{:S(2)}) collective-permute-start(bf16[4,4,32,256]{3,2,1,0:T(8,128)(2,1)S(1)} %pad_maximum_fusion.1.refs_0_), channel_id=1, source_target_pairs={{0,1},{1,0},{2,3},{3,2},{4,5},{5,4},{6,7},{7,6},{8,9},{9,8},{10,11... | collective-permute-start | bytes 786440 | tf_op jit(solution)/shard_map/ppermute | solution.py:147
  20.6 15.3 %all-to-all-start = ((bf16[16,16,512]{2,1,0:T(8,128)(2,1)}), bf16[16,16,512]{2,1,0:T(8,128)(2,1)S(1)}, u32[]{:S(2)}, u32[]{:S(2)}) async-start(bf16[16,16,512]{2,1,0:T(8,128)(2,1)} %pad_maximum_fusion), calls=%async_computation | async-start | bytes 524288 | tf_op jit(solution)/shard_map/all_to_all | solution.py:169
  27.4 1.6 %collective-permute-start.5 = (bf16[4,4,32,256]{3,2,1,0:T(8,128)(2,1)S(1)}, bf16[4,4,32,256]{3,2,1,0:T(8,128)(2,1)S(1)}, u32[]{:S(2)}, u32[]{:S(2)}) collective-permute-start(bf16[4,4,32,256]{3,2,1,0:T(8,128)(2,1)S(1)} %pad_maximum_fusion.1.refs_0_), channel_id=1, source_target_pairs={{0,16},{16,0},{1,17},{17,1},{2,18},{18,2},{3,19},{19,3},{4,20},{20... | collective-permute-start | bytes 786440 | tf_op jit(solution)/shard_map/ppermute | solution.py:178
  27.5 8.4 %collective-permute-start.8 = (bf16[4,4,32,256]{3,2,1,0:T(8,128)(2,1)S(1)}, bf16[4,4,32,256]{3,2,1,0:T(8,128)(2,1)S(1)}, u32[]{:S(2)}, u32[]{:S(2)}) collective-permute-start(bf16[4,4,32,256]{3,2,1,0:T(8,128)(2,1)S(1)} %collective-permute-done.4.refs_3_), channel_id=1, source_target_pairs={{0,16},{16,0},{1,17},{17,1},{2,18},{18,2},{3,19},{19,3},{4,20},{20... | collective-permute-start | bytes 786440 | tf_op jit(solution)/shard_map/ppermute | solution.py:178
  28.0 7.9 %collective-permute-start.7 = (bf16[4,4,32,256]{3,2,1,0:T(8,128)(2,1)S(1)}, bf16[4,4,32,256]{3,2,1,0:T(8,128)(2,1)S(1)}, u32[]{:S(2)}, u32[]{:S(2)}) collective-permute-start(bf16[4,4,32,256]{3,2,1,0:T(8,128)(2,1)S(1)} %collective-permute-done.3.refs_2_), channel_id=1, source_target_pairs={{0,16},{16,0},{1,17},{17,1},{2,18},{18,2},{3,19},{19,3},{4,20},{20... | collective-permute-start | bytes 786440 | tf_op jit(solution)/shard_map/ppermute | solution.py:178
  28.0 7.8 %collective-permute-start.6 = (bf16[4,4,32,256]{3,2,1,0:T(8,128)(2,1)S(1)}, bf16[4,4,32,256]{3,2,1,0:T(8,128)(2,1)S(1)}, u32[]{:S(2)}, u32[]{:S(2)}) collective-permute-start(bf16[4,4,32,256]{3,2,1,0:T(8,128)(2,1)S(1)} %collective-permute-done.2.refs_1_), channel_id=1, source_target_pairs={{0,16},{16,0},{1,17},{17,1},{2,18},{18,2},{3,19},{19,3},{4,20},{20... | collective-permute-start | bytes 786440 | tf_op jit(solution)/shard_map/ppermute | solution.py:178
  41.8 0.7 copy-start
  42.5 3.5 %collective-permute-start.9 = (bf16[8,2,4,32,256]{4,3,2,1,0:T(8,128)(2,1)}, bf16[8,2,4,32,256]{4,3,2,1,0:T(8,128)(2,1)S(1)}, u32[]{:S(2)}, u32[]{:S(2)}) collective-permute-start(bf16[8,2,4,32,256]{4,3,2,1,0:T(8,128)(2,1)} %get-tuple-element.8), channel_id=1, source_target_pairs={{0,16},{16,0},{1,17},{17,1},{2,18},{18,2},{3,19},{19,3},{4,20},{20... | collective-permute-start | bytes 3145736 | tf_op jit(solution)/shard_map/ppermute | solution.py:203
  42.5 14.2 %all-to-all-start.1 = ((bf16[16,16,512]{2,1,0:T(8,128)(2,1)}), bf16[16,16,512]{2,1,0:T(8,128)(2,1)S(1)}, u32[]{:S(2)}, u32[]{:S(2)}) async-start(bf16[16,16,512]{2,1,0:T(8,128)(2,1)} %copy-done), calls=%async_computation.1 | async-start | bytes 524288 | tf_op jit(solution)/shard_map/all_to_all | solution.py:204
  56.7 17.4 %all-to-all-start.2 = ((bf16[8,2,4,32,256]{4,3,2,1,0:T(8,128)(2,1)}), bf16[8,2,4,32,256]{4,3,2,1,0:T(8,128)(2,1)S(1)}, u32[]{:S(2)}, u32[]{:S(2)}) async-start(bf16[8,2,4,32,256]{4,3,2,1,0:T(8,128)(2,1)} %add_convert_fusion), calls=%async_computation.2 | async-start | bytes 2097152 | tf_op jit(solution)/shard_map/all_to_all | solution.py:205
  74.4 5.2 %collective-permute-start.10 = (bf16[4,32,256]{2,1,0:T(8,128)(2,1)S(1)}, bf16[4,32,256]{2,1,0:T(8,128)(2,1)S(1)}, u32[]{:S(2)}, u32[]{:S(2)}) collective-permute-start(bf16[4,32,256]{2,1,0:T(8,128)(2,1)S(1)} %fusion.3), channel_id=1, source_target_pairs={{0,8},{1,9},{2,10},{3,11},{4,12},{5,13},{6,14},{7,15},{8,0},{9,1},... | collective-permute-start | bytes 196616 | tf_op jit(solution)/shard_map/ppermute | solution.py:209

commit v3 on v2

--- a/solution.py
+++ b/solution.py
@@ -14,6 +14,14 @@
 
 def dot(a, b, dims):
     return lax.dot_general(a, b, (dims, ((), ())), preferred_element_type=F32)
+
+
+def send_slot(offset, count):
+    slot, bit = offset & 3, 4
+    while bit < count:
+        slot = slot * 2 + (offset // bit) % 2
+        bit *= 2
+    return slot
 
 
 def row_kernel(groups, offsets, place, rows_ref, gain_ref, *refs):
@@ -24,8 +32,7 @@
     tracks = pair // 2
     width = gain_ref.shape[1]
     length = senders * tracks
-    fan, halves, _, cols, part = wg_refs[0].shape
-    half_at = track // fan
+    count, _, cols, part = wg_refs[0].shape
     copies = []
     for step in range(groups):
         owner = lax.rem(group - step + groups, groups)
@@ -114,15 +121,18 @@
                 block = dot(grads[index], norm_part, ((0,), (0,))).astype(BF)
             else:
                 block = dot(up, att_part, ((0,), (0,))).astype(BF)
-            block = block.reshape(halves, fan, cols, part)
-            for far in range(halves):
-                to = lax.rem(half_at + far, halves)
-                for near in range(fan):
-                    wg_refs[step][near, to, index] = block[far, near]
+            block = block.reshape(count, cols, part)
+            for to in range(count):
+                slot = send_slot(track ^ to, count) if count > 1 else 0
+                wg_refs[step][slot, index] = block[to]
 
 
 def ring(size, step):
     return [(i, (i + step) % size) for i in range(size)]
+
+
+def swap(array, axis, bits):
+    return lax.ppermute(array, axis, [(i, i ^ bits) for i in range(lax.axis_size(axis))])
 
 
 def join_blocks(parts, offsets, track):
@@ -134,26 +144,40 @@
     return blocks.transpose(1, 0, 2, 3).reshape(1, four, count * cols, part)
 
 
-def cut_blocks(joined, half_at, shape):
-    fan, halves, four, cols, part = shape
-    blocks = joined.reshape(four, halves, fan, cols, part).transpose(2, 1, 0, 3, 4)
-    return jnp.where(half_at == 0, blocks, blocks[:, ::-1])
-
-
-def gather_blocks(block, axis):
+def cut_blocks(joined, count, track):
+    _, four, width, part = joined.shape
+    blocks = joined.reshape(four, count, width // count, part).transpose(1, 0, 2, 3)
+    slots = [send_slot(offset, count) for offset in range(count)]
+    order = [slots.index(slot) for slot in range(count)]
+    return jnp.take(blocks, track ^ jnp.array(order), axis=0)
+
+
+def gather_blocks(block, axis, other):
     count = lax.axis_size(axis)
-
-    def swap(array, bits):
-        return lax.ppermute(array, axis, [(i, i ^ bits) for i in range(count)])
-
     held, order, bit = block[None], [0], count // 2
     while bit >= 4:
-        held = jnp.concatenate([held, swap(held, bit)])
+        moved = swap(held, axis, bit)
+        if len(order) == 1:
+            moved, other = lax.optimization_barrier((moved, other))
+        held = jnp.concatenate([held, moved])
         order = order + [offset ^ bit for offset in order]
         bit //= 2
     close = range(2 * bit)
-    parts = [swap(held, bits) if bits else held for bits in close]
-    return parts, [[offset ^ bits for offset in order] for bits in close]
+    parts = [swap(held, axis, bits) if bits else held for bits in close]
+    return parts, [[offset ^ bits for offset in order] for bits in close], other
+
+
+def scatter_sum(blocks, axis):
+    count = lax.axis_size(axis)
+    blocks = blocks.reshape((4, count // 4) + blocks.shape[1:])
+    moved = [swap(blocks[bits], axis, bits) for bits in (1, 2, 3)]
+    total = blocks[0].astype(F32) + sum(block.astype(F32) for block in moved)
+    bit = 4
+    while bit < count:
+        half = total.shape[0] // 2
+        total = total[:half] + swap(total[half:].astype(BF), axis, bit).astype(F32)
+        bit *= 2
+    return total[0]
 
 
 def shards(fields, upstream, ln_gain, weights):
@@ -161,19 +185,15 @@
     rows_dev, trk_dev, width = fields.shape
     _, part, cols = weights.shape
     cell_count = rows_dev * groups * trk_dev * count
-    fan = count // 2
-    near = [[half * fan + i for i in range(fan)] for half in range(2)]
     group, track = lax.axis_index("grp"), lax.axis_index("trk")
-    half_at = track // fan
     both = jnp.concatenate([fields, upstream], 1)
+    parts, offsets, both = gather_blocks(weights.transpose(0, 2, 1), "trk", both)
     row = lax.all_to_all(both, "trk", split_axis=0, concat_axis=0, tiled=True)
-    parts, offsets = gather_blocks(weights.transpose(0, 2, 1), "trk")
-    blocks_shape = (fan, 2, 4, cols, part)
-    out_shape = blocks_shape
+    out_shape = (count, 4, cols, part)
     narrow = cols % 16 != 0
     if narrow:
         parts, offsets = [join_blocks(parts, offsets, track)], [[0]]
-        out_shape = (1, 1, 4, count * cols, part)
+        out_shape = (1, 4, count * cols, part)
     w_parts = [
         lax.ppermute(held, "grp", ring(groups, k)) if k else held
         for k in range(groups)
@@ -197,19 +217,18 @@
         compiler_params=pltpu.CompilerParams(vmem_limit_bytes=48 * 2**20),
     )(place, row, ln_gain[None], *w_parts)
     if narrow:
-        wg = [cut_blocks(blocks, half_at, blocks_shape) for blocks in wg]
+        wg = [cut_blocks(blocks, count, track) for blocks in wg]
+    back = lax.all_to_all(cells, "trk", split_axis=0, concat_axis=0, tiled=True)
     total = wg[0].astype(F32)
     for k in range(1, groups):
         total = total + lax.ppermute(wg[k], "grp", ring(groups, k)).astype(F32)
-    back = lax.all_to_all(cells, "trk", split_axis=0, concat_axis=0, tiled=True)
-    spread = lax.all_to_all(
-        total.astype(BF), "trk", split_axis=0, concat_axis=0, tiled=True, axis_index_groups=near
-    )
-    summed = jnp.sum(spread.astype(F32), 0)
-    total = summed[0] + lax.ppermute(summed[1].astype(BF), "trk", ring(count, fan)).astype(F32)
+    total = scatter_sum(total.astype(BF), "trk")
     grad_fields = back[:, :trk_dev]
     gain_sum = jnp.sum(back[:, trk_dev : trk_dev + 2].astype(F32), (0, 1))
-    gain_sum = lax.psum(gain_sum, "grp")
+    if groups == 2:
+        gain_sum = gain_sum + lax.ppermute(gain_sum, "grp", ring(2, 1))
+    else:
+        gain_sum = jnp.sum(lax.all_gather(gain_sum, "grp"), 0)
     factor = float(cell_count) ** (-0.5)
     return (grad_fields, total.transpose(0, 2, 1) * factor, gain_sum * factor)
 

time: 80.8 us -> 73.5 us (0.910)
  waiting for transfers between devices: 38.6 us -> 32.2 us
  starting transfers between devices: 24.8 us -> 28.4 us
  blocking collectives: 2.47 us -> 0 us
  other arithmetic: 6.41 us -> 5.42 us
    ppermute x6 -> x11, waiting for transfers between devices: 10.7 us -> 24.2 us  [the longest x10 24.2 us: swap(): lax.ppermute(array, axis, [(i, i ^ bits) for i in range(lax.axis_size(axi...]
    all_to_all x1 -> x0, waiting for transfers between devices: 11.4 us -> none  [shards(): lax.all_to_all(total.astype(BF), 'trk', split_axis=0, concat_axis=0, tile...]
    all_to_all x1, waiting for transfers between devices: 9.22 us -> 0.01 us  [shards(): back = lax.all_to_all(cells, 'trk', split_axis=0, concat_axis=0, tiled=True)]
    ppermute x6 -> x11, starting transfers between devices: 9.86 us -> 15.7 us  [the longest x10 15.7 us: swap(): lax.ppermute(array, axis, [(i, i ^ bits) for i in range(lax.axis_size(axi...]
    all_to_all x1 -> x0, starting transfers between devices: 3.56 us -> none  [shards(): lax.all_to_all(total.astype(BF), 'trk', split_axis=0, concat_axis=0, tile...]
    ppermute x1, waiting for transfers between devices: 0.01 us -> 2.65 us  [shards(): total = total + lax.ppermute(wg[k], 'grp', ring(groups, k)).astype(F32)]
    psum x1 -> x0, blocking collectives: 2.47 us -> none  [shards(): gain_sum = lax.psum(gain_sum, 'grp')]
    all_to_all x1, waiting for transfers between devices: 6.9 us -> 5.42 us  [shards(): row = lax.all_to_all(both, 'trk', split_axis=0, concat_axis=0, tiled=True)]
  transfers between devices with their start and end apart: 14 -> 18, of which waited for: 7 -> 11; matrix products, arithmetic and copies ran while one was open for 6% -> 4% of each run, Pallas kernels for 0% -> 0%
where the time goes in v3:
time: 73.5 us; the launch traced here: 73 us
  waiting for transfers between devices  32.2 us (44%)
  starting transfers between devices  28.4 us (39%)
  other arithmetic  5.42 us (7%)
  Pallas kernels  5.42 us (7%)
  between operations  0.77 us (1%)
  local copies, waits for them, and re-layouts  0.75 us (1%)
    ppermute x10, waiting for transfers between devices, swap(): lax.ppermute(array, axis, [(i, i ^ bits) for i in range(lax.axis_size(axi...  24.2 us
    ppermute x10, starting transfers between devices, swap(): lax.ppermute(array, axis, [(i, i ^ bits) for i in range(lax.axis_size(axi...  15.7 us
    all_to_all x1, starting transfers between devices, shards(): row = lax.all_to_all(both, 'trk', split_axis=0, concat_axis=0, tiled=True)  6.75 us
    pallas_call x1, Pallas kernels, shards(): pl.pallas_call(functools.partial(row_kernel, groups, offsets), out_shape=...  5.42 us
    all_to_all x1, waiting for transfers between devices, shards(): row = lax.all_to_all(both, 'trk', split_axis=0, concat_axis=0, tiled=True)  5.42 us
    all_to_all x1, starting transfers between devices, shards(): back = lax.all_to_all(cells, 'trk', split_axis=0, concat_axis=0, tiled=True)  4.96 us
    ppermute x1, waiting for transfers between devices, shards(): total = total + lax.ppermute(wg[k], 'grp', ring(groups, k)).astype(F32)  2.65 us
    concatenate x2, other arithmetic, gather_blocks(): held = jnp.concatenate([held, moved])  1.72 us
  transfers between devices with their start and end apart: 18, of which 11 were waited for; matrix products, arithmetic and copies ran while one was open for 4% of the time, Pallas kernels for 0%

profile of v3, /device:TPU:0, one launch (start us, length us, event | category | flops | bytes accessed | tf_op | source)
XLA Modules:
  0.0 73.0 jit_solution(7009836320655700922)
XLA Ops:
  0.6 0.0 copy-start
  0.6 4.1 %collective-permute-start = (bf16[1,4,32,256]{3,2,1,0:T(8,128)(2,1)}, bf16[1,4,32,256]{3,2,1,0:T(8,128)(2,1)S(1)}, u32[]{:S(2)}, u32[]{:S(2)}) collective-permute-start(bf16[1,4,32,256]{3,2,1,0:T(8,128)(2,1)} %bitcast.11), channel_id=1, source_target_pairs={{0,8},{1,9},{2,10},{3,11},{4,12},{5,13},{6,14},{7,15},{8,0},{9,1},... | collective-permute-start | bytes 196616 | tf_op jit(solution)/shard_map/ppermute | solution.py:135
  4.7 1.7 %pad_maximum_fusion = bf16[16,16,512]{2,1,0:T(8,128)(2,1)} fusion(bf16[16,8,512]{2,1,0:T(8,128)(2,1)} %param.5, bf16[16,8,512]{2,1,0:T(8,128)(2,1)} %param.4), kind=kLoop, calls=%fused_computation.4 | loop fusion | flops 524288 | bytes 524288 | tf_op jit(solution)/shard_map/concatenate | solution.py:189
  6.4 2.2 %collective-permute-done = bf16[1,4,32,256]{3,2,1,0:T(8,128)(2,1)S(1)} collective-permute-done((bf16[1,4,32,256]{3,2,1,0:T(8,128)(2,1)}, bf16[1,4,32,256]{3,2,1,0:T(8,128)(2,1)S(1)}, u32[]{:S(2)}, u32[]{:S(2)}) %collective-permute-start) | collective-permute-done | bytes 65568 | tf_op jit(solution)/shard_map/ppermute | solution.py:135
  8.6 0.9 %pad_maximum_fusion.2 = bf16[2,4,32,256]{3,2,1,0:T(8,128)(2,1)S(1)} fusion(bf16[1,4,32,256]{3,2,1,0:T(8,128)(2,1)S(1)} %collective-permute-done, bf16[1,4,32,256]{3,2,1,0:T(8,128)(2,1)} %bitcast.12), kind=kLoop, calls=%fused_computation.10 | loop fusion | flops 65536 | bytes 262144 | tf_op jit(solution)/shard_map/concatenate | solution.py:162
  9.5 0.7 %collective-permute-start.1 = (bf16[2,4,32,256]{3,2,1,0:T(8,128)(2,1)S(1)}, bf16[2,4,32,256]{3,2,1,0:T(8,128)(2,1)S(1)}, u32[]{:S(2)}, u32[]{:S(2)}) collective-permute-start(bf16[2,4,32,256]{3,2,1,0:T(8,128)(2,1)S(1)} %pad_maximum_fusion.2), channel_id=1, source_target_pairs={{0,4},{1,5},{2,6},{3,7},{4,0},{5,1},{6,2},{7,3},{8,12},{9,13},{10,... | collective-permute-start | bytes 393224 | tf_op jit(solution)/shard_map/ppermute | solution.py:135
  10.2 4.3 %collective-permute-done.1 = bf16[2,4,32,256]{3,2,1,0:T(8,128)(2,1)S(1)} collective-permute-done((bf16[2,4,32,256]{3,2,1,0:T(8,128)(2,1)S(1)}, bf16[2,4,32,256]{3,2,1,0:T(8,128)(2,1)S(1)}, u32[]{:S(2)}, u32[]{:S(2)}) %collective-permute-start.1) | collective-permute-done | bytes 131104 | tf_op jit(solution)/shard_map/ppermute | solution.py:135
  14.5 0.9 %pad_maximum_fusion.1.refs_0_ = bf16[4,4,32,256]{3,2,1,0:T(8,128)(2,1)S(1)} fusion(bf16[2,4,32,256]{3,2,1,0:T(8,128)(2,1)S(1)} %collective-permute-done.1, bf16[1,4,32,256]{3,2,1,0:T(8,128)(2,1)S(1)} %collective-permute-done, bf16[1,4,32,256]{3,2,1,0:T(8,128)(2,1)} %bitcast.13), kind=kLoop, calls=%fused_computation.5 | loop fusion | flops 262144 | bytes 524288 | tf_op jit(solution)/shard_map/concatenate | solution.py:162
  15.4 2.7 %collective-permute-start.4 = (bf16[4,4,32,256]{3,2,1,0:T(8,128)(2,1)S(1)}, bf16[4,4,32,256]{3,2,1,0:T(8,128)(2,1)S(1)}, u32[]{:S(2)}, u32[]{:S(2)}) collective-permute-start(bf16[4,4,32,256]{3,2,1,0:T(8,128)(2,1)S(1)} %pad_maximum_fusion.1.refs_0_), channel_id=1, source_target_pairs={{0,3},{1,2},{2,1},{3,0},{4,7},{5,6},{6,5},{7,4},{8,11},{9,10},{10,... | collective-permute-start | bytes 786440 | tf_op jit(solution)/shard_map/ppermute | solution.py:135
  18.1 0.5 collective-permute-start.3
  18.6 0.3 collective-permute-start.2
  18.9 6.7 %all-to-all-start = ((bf16[16,16,512]{2,1,0:T(8,128)(2,1)}), bf16[16,16,512]{2,1,0:T(8,128)(2,1)S(1)}, u32[]{:S(2)}, u32[]{:S(2)}) async-start(bf16[16,16,512]{2,1,0:T(8,128)(2,1)} %pad_maximum_fusion), calls=%async_computation | async-start | bytes 524288 | tf_op jit(solution)/shard_map/all_to_all | solution.py:191
  25.7 0.1 collective-permute-start.5
  25.8 0.0 collective-permute-done.4.refs_3_
  25.8 0.5 collective-permute-start.8
  26.3 1.9 %collective-permute-done.3.refs_2_ = bf16[4,4,32,256]{3,2,1,0:T(8,128)(2,1)S(1)} collective-permute-done((bf16[4,4,32,256]{3,2,1,0:T(8,128)(2,1)S(1)}, bf16[4,4,32,256]{3,2,1,0:T(8,128)(2,1)S(1)}, u32[]{:S(2)}, u32[]{:S(2)}) %collective-permute-start.3) | collective-permute-done | bytes 262176 | tf_op jit(solution)/shard_map/ppermute | solution.py:135
  28.2 0.0 collective-permute-start.7
  28.2 0.1 collective-permute-done.2.refs_1_
  28.3 0.4 collective-permute-start.6
  28.7 0.1 pad_add_fusion.place
  28.8 0.0 collective-permute-done.5.refs_4_
  28.8 5.4 %all-to-all-done.rows_ref = bf16[16,16,512]{2,1,0:T(8,128)(2,1)S(1)} async-done(((bf16[16,16,512]{2,1,0:T(8,128)(2,1)}), bf16[16,16,512]{2,1,0:T(8,128)(2,1)S(1)}, u32[]{:S(2)}, u32[]{:S(2)}) %all-to-all-start) | async-done | bytes 262176 | tf_op jit(solution)/shard_map/all_to_all | solution.py:191
  34.2 0.0 collective-permute-done.8.refs_7_
  34.2 0.0 collective-permute-done.7.refs_6_
  34.2 0.0 collective-permute-done.6.refs_5_
  34.2 0.0 copy-done
  34.2 5.4 %shard_map.67 = (bf16[16,4,32,256]{3,2,1,0:T(8,128)(2,1)S(1)}, bf16[16,4,32,256]{3,2,1,0:T(8,128)(2,1)S(1)}, bf16[16,16,512]{2,1,0:T(8,128)(2,1)}) custom-call(s32[2]{0:T(128)S(1)} %pad_add_fusion.place, bf16[16,16,512]{2,1,0:T(8,128)(2,1)S(1)} %all-to-all-done.rows_ref, f32[1,512]{1,0:T(1,128)S(1)} %bitcast.10, ...), custom_call_target="tpu_custom_call" | custom-call | tf_op jit(solution)/shard_map/pallas_call | solution.py:204
  39.6 0.1 collective-permute-start.9
  39.7 2.6 %collective-permute-done.9 = bf16[16,4,32,256]{3,2,1,0:T(8,128)(2,1)S(1)} collective-permute-done((bf16[16,4,32,256]{3,2,1,0:T(8,128)(2,1)S(1)}, bf16[16,4,32,256]{3,2,1,0:T(8,128)(2,1)S(1)}, u32[]{:S(2)}, u32[]{:S(2)}) %collective-permute-start.9) | collective-permute-done | bytes 1048608 | tf_op jit(solution)/shard_map/ppermute | solution.py:224
  42.4 0.4 add_convert_fusion
  42.8 0.1 fusion.2
  42.9 1.5 %collective-permute-start.10 = (bf16[4,4,32,256]{3,2,1,0:T(8,128)(2,1)S(1)}, bf16[4,4,32,256]{3,2,1,0:T(8,128)(2,1)S(1)}, u32[]{:S(2)}, u32[]{:S(2)}) collective-permute-start(bf16[4,4,32,256]{3,2,1,0:T(8,128)(2,1)S(1)} %get-tuple-element.13), channel_id=1, source_target_pairs={{0,1},{1,0},{2,3},{3,2},{4,5},{5,4},{6,7},{7,6},{8,9},{9,8},{10,11... | collective-permute-start | bytes 786440 | tf_op jit(solution)/shard_map/ppermute | solution.py:135
  44.4 0.8 %collective-permute-start.12 = (bf16[4,4,32,256]{3,2,1,0:T(8,128)(2,1)S(1)}, bf16[4,4,32,256]{3,2,1,0:T(8,128)(2,1)S(1)}, u32[]{:S(2)}, u32[]{:S(2)}) collective-permute-start(bf16[4,4,32,256]{3,2,1,0:T(8,128)(2,1)S(1)} %get-tuple-element.14), channel_id=1, source_target_pairs={{0,3},{1,2},{2,1},{3,0},{4,7},{5,6},{6,5},{7,4},{8,11},{9,10},{10,... | collective-permute-start | bytes 786440 | tf_op jit(solution)/shard_map/ppermute | solution.py:135
  45.1 1.3 %collective-permute-start.11 = (bf16[4,4,32,256]{3,2,1,0:T(8,128)(2,1)S(1)}, bf16[4,4,32,256]{3,2,1,0:T(8,128)(2,1)S(1)}, u32[]{:S(2)}, u32[]{:S(2)}) collective-permute-start(bf16[4,4,32,256]{3,2,1,0:T(8,128)(2,1)S(1)} %get-tuple-element.15), channel_id=1, source_target_pairs={{0,2},{1,3},{2,0},{3,1},{4,6},{5,7},{6,4},{7,5},{8,10},{9,11},{10,... | collective-permute-start | bytes 786440 | tf_op jit(solution)/shard_map/ppermute | solution.py:135
  46.4 5.0 %all-to-all-start.1 = ((bf16[16,16,512]{2,1,0:T(8,128)(2,1)}), bf16[16,16,512]{2,1,0:T(8,128)(2,1)S(1)}, u32[]{:S(2)}, u32[]{:S(2)}) async-start(bf16[16,16,512]{2,1,0:T(8,128)(2,1)} %get-tuple-element.10), calls=%async_computation.1 | async-start | bytes 524288 | tf_op jit(solution)/shard_map/all_to_all | solution.py:221
  51.4 0.7 collective-permute-done.10
  52.1 7.0 %collective-permute-done.12 = bf16[4,4,32,256]{3,2,1,0:T(8,128)(2,1)S(1)} collective-permute-done((bf16[4,4,32,256]{3,2,1,0:T(8,128)(2,1)S(1)}, bf16[4,4,32,256]{3,2,1,0:T(8,128)(2,1)S(1)}, u32[]{:S(2)}, u32[]{:S(2)}) %collective-permute-start.12) | collective-permute-done | bytes 262176 | tf_op jit(solution)/shard_map/ppermute | solution.py:135
  59.1 2.1 %collective-permute-done.11 = bf16[4,4,32,256]{3,2,1,0:T(8,128)(2,1)S(1)} collective-permute-done((bf16[4,4,32,256]{3,2,1,0:T(8,128)(2,1)S(1)}, bf16[4,4,32,256]{3,2,1,0:T(8,128)(2,1)S(1)}, u32[]{:S(2)}, u32[]{:S(2)}) %collective-permute-start.11) | collective-permute-done | bytes 262176 | tf_op jit(solution)/shard_map/ppermute | solution.py:135
  61.2 0.2 add_add_fusion
  61.4 1.1 %collective-permute-start.13 = (bf16[2,4,32,256]{3,2,1,0:T(8,128)(2,1)S(1)}, bf16[2,4,32,256]{3,2,1,0:T(8,128)(2,1)S(1)}, u32[]{:S(2)}, u32[]{:S(2)}) collective-permute-start(bf16[2,4,32,256]{3,2,1,0:T(8,128)(2,1)S(1)} %slice.66), channel_id=1, source_target_pairs={{0,4},{1,5},{2,6},{3,7},{4,0},{5,1},{6,2},{7,3},{8,12},{9,13},{10,... | collective-permute-start | bytes 393224 | tf_op jit(solution)/shard_map/ppermute | solution.py:135
  62.5 0.0 all-to-all-done.1
  62.5 0.1 collective-permute-start.15
  62.6 0.7 slice.46
  63.3 3.1 %collective-permute-done.13 = bf16[2,4,32,256]{3,2,1,0:T(8,128)(2,1)S(1)} collective-permute-done((bf16[2,4,32,256]{3,2,1,0:T(8,128)(2,1)S(1)}, bf16[2,4,32,256]{3,2,1,0:T(8,128)(2,1)S(1)}, u32[]{:S(2)}, u32[]{:S(2)}) %collective-permute-start.13) | collective-permute-done | bytes 131104 | tf_op jit(solution)/shard_map/ppermute | solution.py:135
  66.4 2.6 %collective-permute-start.14 = (bf16[1,4,32,256]{3,2,1,0:T(8,128)(2,1)S(1)}, bf16[1,4,32,256]{3,2,1,0:T(8,128)(2,1)S(1)}, u32[]{:S(2)}, u32[]{:S(2)}) collective-permute-start(bf16[1,4,32,256]{3,2,1,0:T(8,128)(2,1)S(1)} %slice.67), channel_id=1, source_target_pairs={{0,8},{1,9},{2,10},{3,11},{4,12},{5,13},{6,14},{7,15},{8,0},{9,1},... | collective-permute-start | bytes 196616 | tf_op jit(solution)/shard_map/ppermute | solution.py:135
  69.0 0.0 collective-permute-done.15
  69.0 0.6 add_multiply_fusion
  69.6 2.8 %collective-permute-done.14 = bf16[1,4,32,256]{3,2,1,0:T(8,128)(2,1)S(1)} collective-permute-done((bf16[1,4,32,256]{3,2,1,0:T(8,128)(2,1)S(1)}, bf16[1,4,32,256]{3,2,1,0:T(8,128)(2,1)S(1)}, u32[]{:S(2)}, u32[]{:S(2)}) %collective-permute-start.14) | collective-permute-done | bytes 65568 | tf_op jit(solution)/shard_map/ppermute | solution.py:135
  72.4 0.7 fusion.1
  (4 shorter events, 0.1 us)
Async XLA Ops:
  0.6 33.6 %copy-start = (f32[512]{0:T(512)S(1)}, f32[512]{0:T(512)}, u32[]{:S(2)}) copy-start(f32[512]{0:T(512)} %param.6) | copy-start | bytes 6148
  0.6 8.0 %collective-permute-start = (bf16[1,4,32,256]{3,2,1,0:T(8,128)(2,1)}, bf16[1,4,32,256]{3,2,1,0:T(8,128)(2,1)S(1)}, u32[]{:S(2)}, u32[]{:S(2)}) collective-permute-start(bf16[1,4,32,256]{3,2,1,0:T(8,128)(2,1)} %bitcast.11), channel_id=1, source_target_pairs={{0,8},{1,9},{2,10},{3,11},{4,12},{5,13},{6,14},{7,15},{8,0},{9,1},... | collective-permute-start | bytes 196616 | tf_op jit(solution)/shard_map/ppermute | solution.py:135
  9.5 5.0 %collective-permute-start.1 = (bf16[2,4,32,256]{3,2,1,0:T(8,128)(2,1)S(1)}, bf16[2,4,32,256]{3,2,1,0:T(8,128)(2,1)S(1)}, u32[]{:S(2)}, u32[]{:S(2)}) collective-permute-start(bf16[2,4,32,256]{3,2,1,0:T(8,128)(2,1)S(1)} %pad_maximum_fusion.2), channel_id=1, source_target_pairs={{0,4},{1,5},{2,6},{3,7},{4,0},{5,1},{6,2},{7,3},{8,12},{9,13},{10,... | collective-permute-start | bytes 393224 | tf_op jit(solution)/shard_map/ppermute | solution.py:135
  15.4 10.4 %collective-permute-start.4 = (bf16[4,4,32,256]{3,2,1,0:T(8,128)(2,1)S(1)}, bf16[4,4,32,256]{3,2,1,0:T(8,128)(2,1)S(1)}, u32[]{:S(2)}, u32[]{:S(2)}) collective-permute-start(bf16[4,4,32,256]{3,2,1,0:T(8,128)(2,1)S(1)} %pad_maximum_fusion.1.refs_0_), channel_id=1, source_target_pairs={{0,3},{1,2},{2,1},{3,0},{4,7},{5,6},{6,5},{7,4},{8,11},{9,10},{10,... | collective-permute-start | bytes 786440 | tf_op jit(solution)/shard_map/ppermute | solution.py:135
  18.1 10.1 %collective-permute-start.3 = (bf16[4,4,32,256]{3,2,1,0:T(8,128)(2,1)S(1)}, bf16[4,4,32,256]{3,2,1,0:T(8,128)(2,1)S(1)}, u32[]{:S(2)}, u32[]{:S(2)}) collective-permute-start(bf16[4,4,32,256]{3,2,1,0:T(8,128)(2,1)S(1)} %pad_maximum_fusion.1.refs_0_), channel_id=1, source_target_pairs={{0,2},{1,3},{2,0},{3,1},{4,6},{5,7},{6,4},{7,5},{8,10},{9,11},{10,... | collective-permute-start | bytes 786440 | tf_op jit(solution)/shard_map/ppermute | solution.py:135
  18.6 9.7 %collective-permute-start.2 = (bf16[4,4,32,256]{3,2,1,0:T(8,128)(2,1)S(1)}, bf16[4,4,32,256]{3,2,1,0:T(8,128)(2,1)S(1)}, u32[]{:S(2)}, u32[]{:S(2)}) collective-permute-start(bf16[4,4,32,256]{3,2,1,0:T(8,128)(2,1)S(1)} %pad_maximum_fusion.1.refs_0_), channel_id=1, source_target_pairs={{0,1},{1,0},{2,3},{3,2},{4,5},{5,4},{6,7},{7,6},{8,9},{9,8},{10,11... | collective-permute-start | bytes 786440 | tf_op jit(solution)/shard_map/ppermute | solution.py:135
  18.9 15.3 %all-to-all-start = ((bf16[16,16,512]{2,1,0:T(8,128)(2,1)}), bf16[16,16,512]{2,1,0:T(8,128)(2,1)S(1)}, u32[]{:S(2)}, u32[]{:S(2)}) async-start(bf16[16,16,512]{2,1,0:T(8,128)(2,1)} %pad_maximum_fusion), calls=%async_computation | async-start | bytes 524288 | tf_op jit(solution)/shard_map/all_to_all | solution.py:191
  25.7 3.1 %collective-permute-start.5 = (bf16[4,4,32,256]{3,2,1,0:T(8,128)(2,1)S(1)}, bf16[4,4,32,256]{3,2,1,0:T(8,128)(2,1)S(1)}, u32[]{:S(2)}, u32[]{:S(2)}) collective-permute-start(bf16[4,4,32,256]{3,2,1,0:T(8,128)(2,1)S(1)} %pad_maximum_fusion.1.refs_0_), channel_id=1, source_target_pairs={{0,16},{16,0},{1,17},{17,1},{2,18},{18,2},{3,19},{19,3},{4,20},{20... | collective-permute-start | bytes 786440 | tf_op jit(solution)/shard_map/ppermute | solution.py:198
  25.8 8.4 %collective-permute-start.8 = (bf16[4,4,32,256]{3,2,1,0:T(8,128)(2,1)S(1)}, bf16[4,4,32,256]{3,2,1,0:T(8,128)(2,1)S(1)}, u32[]{:S(2)}, u32[]{:S(2)}) collective-permute-start(bf16[4,4,32,256]{3,2,1,0:T(8,128)(2,1)S(1)} %collective-permute-done.4.refs_3_), channel_id=1, source_target_pairs={{0,16},{16,0},{1,17},{17,1},{2,18},{18,2},{3,19},{19,3},{4,20},{20... | collective-permute-start | bytes 786440 | tf_op jit(solution)/shard_map/ppermute | solution.py:198
  28.2 6.0 %collective-permute-start.7 = (bf16[4,4,32,256]{3,2,1,0:T(8,128)(2,1)S(1)}, bf16[4,4,32,256]{3,2,1,0:T(8,128)(2,1)S(1)}, u32[]{:S(2)}, u32[]{:S(2)}) collective-permute-start(bf16[4,4,32,256]{3,2,1,0:T(8,128)(2,1)S(1)} %collective-permute-done.3.refs_2_), channel_id=1, source_target_pairs={{0,16},{16,0},{1,17},{17,1},{2,18},{18,2},{3,19},{19,3},{4,20},{20... | collective-permute-start | bytes 786440 | tf_op jit(solution)/shard_map/ppermute | solution.py:198
  28.3 5.9 %collective-permute-start.6 = (bf16[4,4,32,256]{3,2,1,0:T(8,128)(2,1)S(1)}, bf16[4,4,32,256]{3,2,1,0:T(8,128)(2,1)S(1)}, u32[]{:S(2)}, u32[]{:S(2)}) collective-permute-start(bf16[4,4,32,256]{3,2,1,0:T(8,128)(2,1)S(1)} %collective-permute-done.2.refs_1_), channel_id=1, source_target_pairs={{0,16},{16,0},{1,17},{17,1},{2,18},{18,2},{3,19},{19,3},{4,20},{20... | collective-permute-start | bytes 786440 | tf_op jit(solution)/shard_map/ppermute | solution.py:198
  39.6 2.7 %collective-permute-start.9 = (bf16[16,4,32,256]{3,2,1,0:T(8,128)(2,1)S(1)}, bf16[16,4,32,256]{3,2,1,0:T(8,128)(2,1)S(1)}, u32[]{:S(2)}, u32[]{:S(2)}) collective-permute-start(bf16[16,4,32,256]{3,2,1,0:T(8,128)(2,1)S(1)} %get-tuple-element.12), channel_id=1, source_target_pairs={{0,16},{16,0},{1,17},{17,1},{2,18},{18,2},{3,19},{19,3},{4,20},{20... | collective-permute-start | bytes 3145736 | tf_op jit(solution)/shard_map/ppermute | solution.py:224
  42.9 9.2 %collective-permute-start.10 = (bf16[4,4,32,256]{3,2,1,0:T(8,128)(2,1)S(1)}, bf16[4,4,32,256]{3,2,1,0:T(8,128)(2,1)S(1)}, u32[]{:S(2)}, u32[]{:S(2)}) collective-permute-start(bf16[4,4,32,256]{3,2,1,0:T(8,128)(2,1)S(1)} %get-tuple-element.13), channel_id=1, source_target_pairs={{0,1},{1,0},{2,3},{3,2},{4,5},{5,4},{6,7},{7,6},{8,9},{9,8},{10,11... | collective-permute-start | bytes 786440 | tf_op jit(solution)/shard_map/ppermute | solution.py:135
  44.4 14.7 %collective-permute-start.12 = (bf16[4,4,32,256]{3,2,1,0:T(8,128)(2,1)S(1)}, bf16[4,4,32,256]{3,2,1,0:T(8,128)(2,1)S(1)}, u32[]{:S(2)}, u32[]{:S(2)}) collective-permute-start(bf16[4,4,32,256]{3,2,1,0:T(8,128)(2,1)S(1)} %get-tuple-element.14), channel_id=1, source_target_pairs={{0,3},{1,2},{2,1},{3,0},{4,7},{5,6},{6,5},{7,4},{8,11},{9,10},{10,... | collective-permute-start | bytes 786440 | tf_op jit(solution)/shard_map/ppermute | solution.py:135
  45.1 16.0 %collective-permute-start.11 = (bf16[4,4,32,256]{3,2,1,0:T(8,128)(2,1)S(1)}, bf16[4,4,32,256]{3,2,1,0:T(8,128)(2,1)S(1)}, u32[]{:S(2)}, u32[]{:S(2)}) collective-permute-start(bf16[4,4,32,256]{3,2,1,0:T(8,128)(2,1)S(1)} %get-tuple-element.15), channel_id=1, source_target_pairs={{0,2},{1,3},{2,0},{3,1},{4,6},{5,7},{6,4},{7,5},{8,10},{9,11},{10,... | collective-permute-start | bytes 786440 | tf_op jit(solution)/shard_map/ppermute | solution.py:135
  46.4 16.1 %all-to-all-start.1 = ((bf16[16,16,512]{2,1,0:T(8,128)(2,1)}), bf16[16,16,512]{2,1,0:T(8,128)(2,1)S(1)}, u32[]{:S(2)}, u32[]{:S(2)}) async-start(bf16[16,16,512]{2,1,0:T(8,128)(2,1)} %get-tuple-element.10), calls=%async_computation.1 | async-start | bytes 524288 | tf_op jit(solution)/shard_map/all_to_all | solution.py:221
  61.4 5.0 %collective-permute-start.13 = (bf16[2,4,32,256]{3,2,1,0:T(8,128)(2,1)S(1)}, bf16[2,4,32,256]{3,2,1,0:T(8,128)(2,1)S(1)}, u32[]{:S(2)}, u32[]{:S(2)}) collective-permute-start(bf16[2,4,32,256]{3,2,1,0:T(8,128)(2,1)S(1)} %slice.66), channel_id=1, source_target_pairs={{0,4},{1,5},{2,6},{3,7},{4,0},{5,1},{6,2},{7,3},{8,12},{9,13},{10,... | collective-permute-start | bytes 393224 | tf_op jit(solution)/shard_map/ppermute | solution.py:135
  62.5 6.5 %collective-permute-start.15 = (f32[512]{0:T(512)S(1)}, f32[512]{0:T(512)S(1)}, u32[]{:S(2)}, u32[]{:S(2)}) collective-permute-start(f32[512]{0:T(512)S(1)} %convert_reduce_fusion), channel_id=1, source_target_pairs={{0,16},{16,0},{1,17},{17,1},{2,18},{18,2},{3,19},{19,3},{4,20},{20... | collective-permute-start | bytes 6152 | tf_op jit(solution)/shard_map/ppermute | solution.py:229
  66.4 5.9 %collective-permute-start.14 = (bf16[1,4,32,256]{3,2,1,0:T(8,128)(2,1)S(1)}, bf16[1,4,32,256]{3,2,1,0:T(8,128)(2,1)S(1)}, u32[]{:S(2)}, u32[]{:S(2)}) collective-permute-start(bf16[1,4,32,256]{3,2,1,0:T(8,128)(2,1)S(1)} %slice.67), channel_id=1, source_target_pairs={{0,8},{1,9},{2,10},{3,11},{4,12},{5,13},{6,14},{7,15},{8,0},{9,1},... | collective-permute-start | bytes 196616 | tf_op jit(solution)/shard_map/ppermute | solution.py:135

commit v4 on v3

--- a/solution.py
+++ b/solution.py
@@ -155,22 +155,23 @@
 def gather_blocks(block, axis, other):
     count = lax.axis_size(axis)
     held, order, bit = block[None], [0], count // 2
-    while bit >= 4:
-        moved = swap(held, axis, bit)
-        if len(order) == 1:
-            moved, other = lax.optimization_barrier((moved, other))
-        held = jnp.concatenate([held, moved])
+    while bit > 8:
+        held = jnp.concatenate([held, swap(held, axis, bit)])
         order = order + [offset ^ bit for offset in order]
         bit //= 2
-    close = range(2 * bit)
-    parts = [swap(held, axis, bits) if bits else held for bits in close]
-    return parts, [[offset ^ bits for offset in order] for bits in close], other
+    far = [bits for bits in (8, 4, 12) if bits < 2 * bit]
+    moved = [swap(held, axis, bits) for bits in far]
+    moved[0], other = lax.optimization_barrier((moved[0], other))
+    held = jnp.concatenate([held] + moved)
+    order = order + [offset ^ bits for bits in far for offset in order]
+    parts = [swap(held, axis, bits) if bits else held for bits in range(4)]
+    return parts, [[offset ^ bits for offset in order] for bits in range(4)], other
 
 
 def scatter_sum(blocks, axis):
     count = lax.axis_size(axis)
     blocks = blocks.reshape((4, count // 4) + blocks.shape[1:])
-    moved = [swap(blocks[bits], axis, bits) for bits in (1, 2, 3)]
+    moved = [swap(blocks[bits], axis, bits) for bits in (1, 3, 2)]
     total = blocks[0].astype(F32) + sum(block.astype(F32) for block in moved)
     bit = 4
     while bit < count:

time: 73.5 us -> 67.5 us (0.918)
  waiting for transfers between devices: 32.2 us -> 27 us
  other arithmetic: 5.42 us -> 4.57 us
    all_to_all x1, waiting for transfers between devices: 5.42 us -> 1.45 us  [shards(): row = lax.all_to_all(both, 'trk', split_axis=0, concat_axis=0, tiled=True)]
    ppermute x10 -> x11, starting transfers between devices: 15.7 us -> 17.3 us  [swap(): lax.ppermute(array, axis, [(i, i ^ bits) for i in range(lax.axis_size(axi...]
    all_to_all x1, starting transfers between devices: 6.75 us -> 5.42 us  [shards(): row = lax.all_to_all(both, 'trk', split_axis=0, concat_axis=0, tiled=True)]
    ppermute x10 -> x11, waiting for transfers between devices: 24.2 us -> 22.9 us  [swap(): lax.ppermute(array, axis, [(i, i ^ bits) for i in range(lax.axis_size(axi...]
    concatenate x2 -> x1, other arithmetic: 1.72 us -> 0.88 us  [gather_blocks(): held = jnp.concatenate([held] + moved)]
  transfers between devices with their start and end apart: 18 -> 19, of which waited for: 11 -> 11; matrix products, arithmetic and copies ran while one was open for 4% -> 5% of each run, Pallas kernels for 0% -> 0%
where the time goes in v4:
time: 67.5 us; the launch traced here: 67.1 us
  starting transfers between devices  28.6 us (42%)
  waiting for transfers between devices  27 us (40%)
  Pallas kernels  5.42 us (8%)
  other arithmetic  4.57 us (7%)
  between operations  0.76 us (1%)
  local copies, waits for them, and re-layouts  0.75 us (1%)
    ppermute x11, waiting for transfers between devices, swap(): lax.ppermute(array, axis, [(i, i ^ bits) for i in range(lax.axis_size(axi...  22.9 us
    ppermute x11, starting transfers between devices, swap(): lax.ppermute(array, axis, [(i, i ^ bits) for i in range(lax.axis_size(axi...  17.3 us
    all_to_all x1, starting transfers between devices, shards(): back = lax.all_to_all(cells, 'trk', split_axis=0, concat_axis=0, tiled=True)  5.47 us
    all_to_all x1, starting transfers between devices, shards(): row = lax.all_to_all(both, 'trk', split_axis=0, concat_axis=0, tiled=True)  5.42 us
    pallas_call x1, Pallas kernels, shards(): pl.pallas_call(functools.partial(row_kernel, groups, offsets), out_shape=...  5.42 us
    ppermute x1, waiting for transfers between devices, shards(): total = total + lax.ppermute(wg[k], 'grp', ring(groups, k)).astype(F32)  2.65 us
    concatenate x1, other arithmetic, shards(): both = jnp.concatenate([fields, upstream], 1)  1.69 us
    all_to_all x1, waiting for transfers between devices, shards(): row = lax.all_to_all(both, 'trk', split_axis=0, concat_axis=0, tiled=True)  1.45 us
  transfers between devices with their start and end apart: 19, of which 11 were waited for; matrix products, arithmetic and copies ran while one was open for 5% of the time, Pallas kernels for 0%

profile of v4, /device:TPU:0, one launch (start us, length us, event | category | flops | bytes accessed | tf_op | source)
XLA Modules:
  0.0 67.1 jit_solution(5605680979448704917)
XLA Ops:
  0.6 0.0 copy-start
  0.6 5.1 %collective-permute-start.2 = (bf16[1,4,32,256]{3,2,1,0:T(8,128)(2,1)}, bf16[1,4,32,256]{3,2,1,0:T(8,128)(2,1)S(1)}, u32[]{:S(2)}, u32[]{:S(2)}) collective-permute-start(bf16[1,4,32,256]{3,2,1,0:T(8,128)(2,1)} %bitcast.11), channel_id=1, source_target_pairs={{0,12},{1,13},{2,14},{3,15},{4,8},{5,9},{6,10},{7,11},{8,4},{9,5},... | collective-permute-start | bytes 196616 | tf_op jit(solution)/shard_map/ppermute | solution.py:135
  5.8 0.0 collective-permute-start.1
  5.8 0.6 collective-permute-start
  6.4 1.7 %pad_maximum_fusion = bf16[16,16,512]{2,1,0:T(8,128)(2,1)} fusion(bf16[16,8,512]{2,1,0:T(8,128)(2,1)} %param.5, bf16[16,8,512]{2,1,0:T(8,128)(2,1)} %param.4), kind=kLoop, calls=%fused_computation.4 | loop fusion | flops 524288 | bytes 524288 | tf_op jit(solution)/shard_map/concatenate | solution.py:190
  8.1 3.5 %collective-permute-done = bf16[1,4,32,256]{3,2,1,0:T(8,128)(2,1)S(1)} collective-permute-done((bf16[1,4,32,256]{3,2,1,0:T(8,128)(2,1)}, bf16[1,4,32,256]{3,2,1,0:T(8,128)(2,1)S(1)}, u32[]{:S(2)}, u32[]{:S(2)}) %collective-permute-start) | collective-permute-done | bytes 65568 | tf_op jit(solution)/shard_map/ppermute | solution.py:135
  11.6 0.0 collective-permute-done.2
  11.6 0.0 collective-permute-done.1
  11.6 0.9 %pad_maximum_fusion.1.refs_0_ = bf16[4,4,32,256]{3,2,1,0:T(8,128)(2,1)S(1)} fusion(bf16[1,4,32,256]{3,2,1,0:T(8,128)(2,1)S(1)} %collective-permute-done.2, bf16[1,4,32,256]{3,2,1,0:T(8,128)(2,1)S(1)} %collective-permute-done.1, bf16[1,4,32,256]{3,2,1,0:T(8,128)(2,1)S(1)} %collective-permute-done, bf16[1,4,32,256]{3,2,1,0:T(8,128)(2,1)} %bitcast.14), kind=kLoop, calls=%fused_computation.5 | loop fusion | flops 393216 | bytes 524288 | tf_op jit(solution)/shard_map/concatenate | solution.py:165
  12.5 2.5 %collective-permute-start.5 = (bf16[4,4,32,256]{3,2,1,0:T(8,128)(2,1)S(1)}, bf16[4,4,32,256]{3,2,1,0:T(8,128)(2,1)S(1)}, u32[]{:S(2)}, u32[]{:S(2)}) collective-permute-start(bf16[4,4,32,256]{3,2,1,0:T(8,128)(2,1)S(1)} %pad_maximum_fusion.1.refs_0_), channel_id=1, source_target_pairs={{0,3},{1,2},{2,1},{3,0},{4,7},{5,6},{6,5},{7,4},{8,11},{9,10},{10,... | collective-permute-start | bytes 786440 | tf_op jit(solution)/shard_map/ppermute | solution.py:135
  15.0 0.5 collective-permute-start.4
  15.5 0.5 collective-permute-start.3
  16.0 5.4 %all-to-all-start = ((bf16[16,16,512]{2,1,0:T(8,128)(2,1)}), bf16[16,16,512]{2,1,0:T(8,128)(2,1)S(1)}, u32[]{:S(2)}, u32[]{:S(2)}) async-start(bf16[16,16,512]{2,1,0:T(8,128)(2,1)} %pad_maximum_fusion), calls=%async_computation | async-start | bytes 524288 | tf_op jit(solution)/shard_map/all_to_all | solution.py:192
  21.5 0.1 collective-permute-start.6
  21.6 1.2 %collective-permute-done.5.refs_3_ = bf16[4,4,32,256]{3,2,1,0:T(8,128)(2,1)S(1)} collective-permute-done((bf16[4,4,32,256]{3,2,1,0:T(8,128)(2,1)S(1)}, bf16[4,4,32,256]{3,2,1,0:T(8,128)(2,1)S(1)}, u32[]{:S(2)}, u32[]{:S(2)}) %collective-permute-start.5) | collective-permute-done | bytes 262176 | tf_op jit(solution)/shard_map/ppermute | solution.py:135
  22.7 0.0 collective-permute-start.9
  22.7 5.2 %collective-permute-done.4.refs_2_ = bf16[4,4,32,256]{3,2,1,0:T(8,128)(2,1)S(1)} collective-permute-done((bf16[4,4,32,256]{3,2,1,0:T(8,128)(2,1)S(1)}, bf16[4,4,32,256]{3,2,1,0:T(8,128)(2,1)S(1)}, u32[]{:S(2)}, u32[]{:S(2)}) %collective-permute-start.4) | collective-permute-done | bytes 262176 | tf_op jit(solution)/shard_map/ppermute | solution.py:135
  27.9 0.0 collective-permute-start.8
  27.9 0.2 collective-permute-done.3.refs_1_
  28.2 0.3 collective-permute-start.7
  28.4 0.1 pad_add_fusion.place
  28.5 0.0 collective-permute-done.6.refs_4_
  28.5 1.4 %all-to-all-done.rows_ref = bf16[16,16,512]{2,1,0:T(8,128)(2,1)S(1)} async-done(((bf16[16,16,512]{2,1,0:T(8,128)(2,1)}), bf16[16,16,512]{2,1,0:T(8,128)(2,1)S(1)}, u32[]{:S(2)}, u32[]{:S(2)}) %all-to-all-start) | async-done | bytes 262176 | tf_op jit(solution)/shard_map/all_to_all | solution.py:192
  30.0 0.0 collective-permute-done.9.refs_7_
  30.0 0.0 collective-permute-done.8.refs_6_
  30.0 0.0 collective-permute-done.7.refs_5_
  30.0 0.0 copy-done
  30.0 5.4 %shard_map.67 = (bf16[16,4,32,256]{3,2,1,0:T(8,128)(2,1)S(1)}, bf16[16,4,32,256]{3,2,1,0:T(8,128)(2,1)S(1)}, bf16[16,16,512]{2,1,0:T(8,128)(2,1)}) custom-call(s32[2]{0:T(128)S(1)} %pad_add_fusion.place, bf16[16,16,512]{2,1,0:T(8,128)(2,1)S(1)} %all-to-all-done.rows_ref, f32[1,512]{1,0:T(1,128)S(1)} %bitcast.10, ...), custom_call_target="tpu_custom_call" | custom-call | tf_op jit(solution)/shard_map/pallas_call | solution.py:205
  35.4 0.1 collective-permute-start.10
  35.5 2.6 %collective-permute-done.10 = bf16[16,4,32,256]{3,2,1,0:T(8,128)(2,1)S(1)} collective-permute-done((bf16[16,4,32,256]{3,2,1,0:T(8,128)(2,1)S(1)}, bf16[16,4,32,256]{3,2,1,0:T(8,128)(2,1)S(1)}, u32[]{:S(2)}, u32[]{:S(2)}) %collective-permute-start.10) | collective-permute-done | bytes 1048608 | tf_op jit(solution)/shard_map/ppermute | solution.py:225
  38.1 0.4 add_convert_fusion
  38.6 0.1 fusion.2
  38.7 1.7 %collective-permute-start.11 = (bf16[4,4,32,256]{3,2,1,0:T(8,128)(2,1)S(1)}, bf16[4,4,32,256]{3,2,1,0:T(8,128)(2,1)S(1)}, u32[]{:S(2)}, u32[]{:S(2)}) collective-permute-start(bf16[4,4,32,256]{3,2,1,0:T(8,128)(2,1)S(1)} %get-tuple-element.13), channel_id=1, source_target_pairs={{0,1},{1,0},{2,3},{3,2},{4,5},{5,4},{6,7},{7,6},{8,9},{9,8},{10,11... | collective-permute-start | bytes 786440 | tf_op jit(solution)/shard_map/ppermute | solution.py:135
  40.3 0.7 %collective-permute-start.13 = (bf16[4,4,32,256]{3,2,1,0:T(8,128)(2,1)S(1)}, bf16[4,4,32,256]{3,2,1,0:T(8,128)(2,1)S(1)}, u32[]{:S(2)}, u32[]{:S(2)}) collective-permute-start(bf16[4,4,32,256]{3,2,1,0:T(8,128)(2,1)S(1)} %get-tuple-element.14), channel_id=1, source_target_pairs={{0,2},{1,3},{2,0},{3,1},{4,6},{5,7},{6,4},{7,5},{8,10},{9,11},{10,... | collective-permute-start | bytes 786440 | tf_op jit(solution)/shard_map/ppermute | solution.py:135
  41.1 1.1 %collective-permute-start.12 = (bf16[4,4,32,256]{3,2,1,0:T(8,128)(2,1)S(1)}, bf16[4,4,32,256]{3,2,1,0:T(8,128)(2,1)S(1)}, u32[]{:S(2)}, u32[]{:S(2)}) collective-permute-start(bf16[4,4,32,256]{3,2,1,0:T(8,128)(2,1)S(1)} %get-tuple-element.15), channel_id=1, source_target_pairs={{0,3},{1,2},{2,1},{3,0},{4,7},{5,6},{6,5},{7,4},{8,11},{9,10},{10,... | collective-permute-start | bytes 786440 | tf_op jit(solution)/shard_map/ppermute | solution.py:135
  42.2 5.5 %all-to-all-start.1 = ((bf16[16,16,512]{2,1,0:T(8,128)(2,1)}), bf16[16,16,512]{2,1,0:T(8,128)(2,1)S(1)}, u32[]{:S(2)}, u32[]{:S(2)}) async-start(bf16[16,16,512]{2,1,0:T(8,128)(2,1)} %get-tuple-element.10), calls=%async_computation.1 | async-start | bytes 524288 | tf_op jit(solution)/shard_map/all_to_all | solution.py:222
  47.7 0.2 collective-permute-done.11
  47.9 6.7 %collective-permute-done.13 = bf16[4,4,32,256]{3,2,1,0:T(8,128)(2,1)S(1)} collective-permute-done((bf16[4,4,32,256]{3,2,1,0:T(8,128)(2,1)S(1)}, bf16[4,4,32,256]{3,2,1,0:T(8,128)(2,1)S(1)}, u32[]{:S(2)}, u32[]{:S(2)}) %collective-permute-start.13) | collective-permute-done | bytes 262176 | tf_op jit(solution)/shard_map/ppermute | solution.py:135
  54.6 1.4 %collective-permute-done.12 = bf16[4,4,32,256]{3,2,1,0:T(8,128)(2,1)S(1)} collective-permute-done((bf16[4,4,32,256]{3,2,1,0:T(8,128)(2,1)S(1)}, bf16[4,4,32,256]{3,2,1,0:T(8,128)(2,1)S(1)}, u32[]{:S(2)}, u32[]{:S(2)}) %collective-permute-start.12) | collective-permute-done | bytes 262176 | tf_op jit(solution)/shard_map/ppermute | solution.py:135
  55.9 0.2 add_add_fusion
  56.1 1.9 %collective-permute-start.14 = (bf16[2,4,32,256]{3,2,1,0:T(8,128)(2,1)S(1)}, bf16[2,4,32,256]{3,2,1,0:T(8,128)(2,1)S(1)}, u32[]{:S(2)}, u32[]{:S(2)}) collective-permute-start(bf16[2,4,32,256]{3,2,1,0:T(8,128)(2,1)S(1)} %slice.66), channel_id=1, source_target_pairs={{0,4},{1,5},{2,6},{3,7},{4,0},{5,1},{6,2},{7,3},{8,12},{9,13},{10,... | collective-permute-start | bytes 393224 | tf_op jit(solution)/shard_map/ppermute | solution.py:135
  58.0 0.0 all-to-all-done.1
  58.0 0.1 collective-permute-start.16
  58.1 0.7 slice.46
  58.8 2.4 %collective-permute-done.14 = bf16[2,4,32,256]{3,2,1,0:T(8,128)(2,1)S(1)} collective-permute-done((bf16[2,4,32,256]{3,2,1,0:T(8,128)(2,1)S(1)}, bf16[2,4,32,256]{3,2,1,0:T(8,128)(2,1)S(1)}, u32[]{:S(2)}, u32[]{:S(2)}) %collective-permute-start.14) | collective-permute-done | bytes 131104 | tf_op jit(solution)/shard_map/ppermute | solution.py:135
  61.2 2.6 %collective-permute-start.15 = (bf16[1,4,32,256]{3,2,1,0:T(8,128)(2,1)S(1)}, bf16[1,4,32,256]{3,2,1,0:T(8,128)(2,1)S(1)}, u32[]{:S(2)}, u32[]{:S(2)}) collective-permute-start(bf16[1,4,32,256]{3,2,1,0:T(8,128)(2,1)S(1)} %slice.67), channel_id=1, source_target_pairs={{0,8},{1,9},{2,10},{3,11},{4,12},{5,13},{6,14},{7,15},{8,0},{9,1},... | collective-permute-start | bytes 196616 | tf_op jit(solution)/shard_map/ppermute | solution.py:135
  63.8 0.0 collective-permute-done.16
  63.8 0.6 add_multiply_fusion
  64.4 2.1 %collective-permute-done.15 = bf16[1,4,32,256]{3,2,1,0:T(8,128)(2,1)S(1)} collective-permute-done((bf16[1,4,32,256]{3,2,1,0:T(8,128)(2,1)S(1)}, bf16[1,4,32,256]{3,2,1,0:T(8,128)(2,1)S(1)}, u32[]{:S(2)}, u32[]{:S(2)}) %collective-permute-start.15) | collective-permute-done | bytes 65568 | tf_op jit(solution)/shard_map/ppermute | solution.py:135
  66.4 0.7 fusion.1
  (4 shorter events, 0.1 us)
Async XLA Ops:
  0.6 29.4 %copy-start = (f32[512]{0:T(512)S(1)}, f32[512]{0:T(512)}, u32[]{:S(2)}) copy-start(f32[512]{0:T(512)} %param.6) | copy-start | bytes 6148
  0.6 11.0 %collective-permute-start.2 = (bf16[1,4,32,256]{3,2,1,0:T(8,128)(2,1)}, bf16[1,4,32,256]{3,2,1,0:T(8,128)(2,1)S(1)}, u32[]{:S(2)}, u32[]{:S(2)}) collective-permute-start(bf16[1,4,32,256]{3,2,1,0:T(8,128)(2,1)} %bitcast.11), channel_id=1, source_target_pairs={{0,12},{1,13},{2,14},{3,15},{4,8},{5,9},{6,10},{7,11},{8,4},{9,5},... | collective-permute-start | bytes 196616 | tf_op jit(solution)/shard_map/ppermute | solution.py:135
  5.8 5.9 %collective-permute-start.1 = (bf16[1,4,32,256]{3,2,1,0:T(8,128)(2,1)}, bf16[1,4,32,256]{3,2,1,0:T(8,128)(2,1)S(1)}, u32[]{:S(2)}, u32[]{:S(2)}) collective-permute-start(bf16[1,4,32,256]{3,2,1,0:T(8,128)(2,1)} %bitcast.12), channel_id=1, source_target_pairs={{0,4},{1,5},{2,6},{3,7},{4,0},{5,1},{6,2},{7,3},{8,12},{9,13},{10,... | collective-permute-start | bytes 196616 | tf_op jit(solution)/shard_map/ppermute | solution.py:135
  5.8 5.8 %collective-permute-start = (bf16[1,4,32,256]{3,2,1,0:T(8,128)(2,1)}, bf16[1,4,32,256]{3,2,1,0:T(8,128)(2,1)S(1)}, u32[]{:S(2)}, u32[]{:S(2)}) collective-permute-start(bf16[1,4,32,256]{3,2,1,0:T(8,128)(2,1)} %bitcast.13), channel_id=1, source_target_pairs={{0,8},{1,9},{2,10},{3,11},{4,12},{5,13},{6,14},{7,15},{8,0},{9,1},... | collective-permute-start | bytes 196616 | tf_op jit(solution)/shard_map/ppermute | solution.py:135
  12.5 10.2 %collective-permute-start.5 = (bf16[4,4,32,256]{3,2,1,0:T(8,128)(2,1)S(1)}, bf16[4,4,32,256]{3,2,1,0:T(8,128)(2,1)S(1)}, u32[]{:S(2)}, u32[]{:S(2)}) collective-permute-start(bf16[4,4,32,256]{3,2,1,0:T(8,128)(2,1)S(1)} %pad_maximum_fusion.1.refs_0_), channel_id=1, source_target_pairs={{0,3},{1,2},{2,1},{3,0},{4,7},{5,6},{6,5},{7,4},{8,11},{9,10},{10,... | collective-permute-start | bytes 786440 | tf_op jit(solution)/shard_map/ppermute | solution.py:135
  15.0 12.9 %collective-permute-start.4 = (bf16[4,4,32,256]{3,2,1,0:T(8,128)(2,1)S(1)}, bf16[4,4,32,256]{3,2,1,0:T(8,128)(2,1)S(1)}, u32[]{:S(2)}, u32[]{:S(2)}) collective-permute-start(bf16[4,4,32,256]{3,2,1,0:T(8,128)(2,1)S(1)} %pad_maximum_fusion.1.refs_0_), channel_id=1, source_target_pairs={{0,2},{1,3},{2,0},{3,1},{4,6},{5,7},{6,4},{7,5},{8,10},{9,11},{10,... | collective-permute-start | bytes 786440 | tf_op jit(solution)/shard_map/ppermute | solution.py:135
  15.5 12.7 %collective-permute-start.3 = (bf16[4,4,32,256]{3,2,1,0:T(8,128)(2,1)S(1)}, bf16[4,4,32,256]{3,2,1,0:T(8,128)(2,1)S(1)}, u32[]{:S(2)}, u32[]{:S(2)}) collective-permute-start(bf16[4,4,32,256]{3,2,1,0:T(8,128)(2,1)S(1)} %pad_maximum_fusion.1.refs_0_), channel_id=1, source_target_pairs={{0,1},{1,0},{2,3},{3,2},{4,5},{5,4},{6,7},{7,6},{8,9},{9,8},{10,11... | collective-permute-start | bytes 786440 | tf_op jit(solution)/shard_map/ppermute | solution.py:135
  16.0 13.9 %all-to-all-start = ((bf16[16,16,512]{2,1,0:T(8,128)(2,1)}), bf16[16,16,512]{2,1,0:T(8,128)(2,1)S(1)}, u32[]{:S(2)}, u32[]{:S(2)}) async-start(bf16[16,16,512]{2,1,0:T(8,128)(2,1)} %pad_maximum_fusion), calls=%async_computation | async-start | bytes 524288 | tf_op jit(solution)/shard_map/all_to_all | solution.py:192
  21.5 7.1 %collective-permute-start.6 = (bf16[4,4,32,256]{3,2,1,0:T(8,128)(2,1)S(1)}, bf16[4,4,32,256]{3,2,1,0:T(8,128)(2,1)S(1)}, u32[]{:S(2)}, u32[]{:S(2)}) collective-permute-start(bf16[4,4,32,256]{3,2,1,0:T(8,128)(2,1)S(1)} %pad_maximum_fusion.1.refs_0_), channel_id=1, source_target_pairs={{0,16},{16,0},{1,17},{17,1},{2,18},{18,2},{3,19},{19,3},{4,20},{20... | collective-permute-start | bytes 786440 | tf_op jit(solution)/shard_map/ppermute | solution.py:199
  22.7 7.3 %collective-permute-start.9 = (bf16[4,4,32,256]{3,2,1,0:T(8,128)(2,1)S(1)}, bf16[4,4,32,256]{3,2,1,0:T(8,128)(2,1)S(1)}, u32[]{:S(2)}, u32[]{:S(2)}) collective-permute-start(bf16[4,4,32,256]{3,2,1,0:T(8,128)(2,1)S(1)} %collective-permute-done.5.refs_3_), channel_id=1, source_target_pairs={{0,16},{16,0},{1,17},{17,1},{2,18},{18,2},{3,19},{19,3},{4,20},{20... | collective-permute-start | bytes 786440 | tf_op jit(solution)/shard_map/ppermute | solution.py:199
  27.9 2.0 %collective-permute-start.8 = (bf16[4,4,32,256]{3,2,1,0:T(8,128)(2,1)S(1)}, bf16[4,4,32,256]{3,2,1,0:T(8,128)(2,1)S(1)}, u32[]{:S(2)}, u32[]{:S(2)}) collective-permute-start(bf16[4,4,32,256]{3,2,1,0:T(8,128)(2,1)S(1)} %collective-permute-done.4.refs_2_), channel_id=1, source_target_pairs={{0,16},{16,0},{1,17},{17,1},{2,18},{18,2},{3,19},{19,3},{4,20},{20... | collective-permute-start | bytes 786440 | tf_op jit(solution)/shard_map/ppermute | solution.py:199
  28.2 1.8 %collective-permute-start.7 = (bf16[4,4,32,256]{3,2,1,0:T(8,128)(2,1)S(1)}, bf16[4,4,32,256]{3,2,1,0:T(8,128)(2,1)S(1)}, u32[]{:S(2)}, u32[]{:S(2)}) collective-permute-start(bf16[4,4,32,256]{3,2,1,0:T(8,128)(2,1)S(1)} %collective-permute-done.3.refs_1_), channel_id=1, source_target_pairs={{0,16},{16,0},{1,17},{17,1},{2,18},{18,2},{3,19},{19,3},{4,20},{20... | collective-permute-start | bytes 786440 | tf_op jit(solution)/shard_map/ppermute | solution.py:199
  35.4 2.7 %collective-permute-start.10 = (bf16[16,4,32,256]{3,2,1,0:T(8,128)(2,1)S(1)}, bf16[16,4,32,256]{3,2,1,0:T(8,128)(2,1)S(1)}, u32[]{:S(2)}, u32[]{:S(2)}) collective-permute-start(bf16[16,4,32,256]{3,2,1,0:T(8,128)(2,1)S(1)} %get-tuple-element.12), channel_id=1, source_target_pairs={{0,16},{16,0},{1,17},{17,1},{2,18},{18,2},{3,19},{19,3},{4,20},{20... | collective-permute-start | bytes 3145736 | tf_op jit(solution)/shard_map/ppermute | solution.py:225
  38.7 9.2 %collective-permute-start.11 = (bf16[4,4,32,256]{3,2,1,0:T(8,128)(2,1)S(1)}, bf16[4,4,32,256]{3,2,1,0:T(8,128)(2,1)S(1)}, u32[]{:S(2)}, u32[]{:S(2)}) collective-permute-start(bf16[4,4,32,256]{3,2,1,0:T(8,128)(2,1)S(1)} %get-tuple-element.13), channel_id=1, source_target_pairs={{0,1},{1,0},{2,3},{3,2},{4,5},{5,4},{6,7},{7,6},{8,9},{9,8},{10,11... | collective-permute-start | bytes 786440 | tf_op jit(solution)/shard_map/ppermute | solution.py:135
  40.3 14.3 %collective-permute-start.13 = (bf16[4,4,32,256]{3,2,1,0:T(8,128)(2,1)S(1)}, bf16[4,4,32,256]{3,2,1,0:T(8,128)(2,1)S(1)}, u32[]{:S(2)}, u32[]{:S(2)}) collective-permute-start(bf16[4,4,32,256]{3,2,1,0:T(8,128)(2,1)S(1)} %get-tuple-element.14), channel_id=1, source_target_pairs={{0,2},{1,3},{2,0},{3,1},{4,6},{5,7},{6,4},{7,5},{8,10},{9,11},{10,... | collective-permute-start | bytes 786440 | tf_op jit(solution)/shard_map/ppermute | solution.py:135
  41.1 14.9 %collective-permute-start.12 = (bf16[4,4,32,256]{3,2,1,0:T(8,128)(2,1)S(1)}, bf16[4,4,32,256]{3,2,1,0:T(8,128)(2,1)S(1)}, u32[]{:S(2)}, u32[]{:S(2)}) collective-permute-start(bf16[4,4,32,256]{3,2,1,0:T(8,128)(2,1)S(1)} %get-tuple-element.15), channel_id=1, source_target_pairs={{0,3},{1,2},{2,1},{3,0},{4,7},{5,6},{6,5},{7,4},{8,11},{9,10},{10,... | collective-permute-start | bytes 786440 | tf_op jit(solution)/shard_map/ppermute | solution.py:135
  42.2 15.8 %all-to-all-start.1 = ((bf16[16,16,512]{2,1,0:T(8,128)(2,1)}), bf16[16,16,512]{2,1,0:T(8,128)(2,1)S(1)}, u32[]{:S(2)}, u32[]{:S(2)}) async-start(bf16[16,16,512]{2,1,0:T(8,128)(2,1)} %get-tuple-element.10), calls=%async_computation.1 | async-start | bytes 524288 | tf_op jit(solution)/shard_map/all_to_all | solution.py:222
  56.1 5.0 %collective-permute-start.14 = (bf16[2,4,32,256]{3,2,1,0:T(8,128)(2,1)S(1)}, bf16[2,4,32,256]{3,2,1,0:T(8,128)(2,1)S(1)}, u32[]{:S(2)}, u32[]{:S(2)}) collective-permute-start(bf16[2,4,32,256]{3,2,1,0:T(8,128)(2,1)S(1)} %slice.66), channel_id=1, source_target_pairs={{0,4},{1,5},{2,6},{3,7},{4,0},{5,1},{6,2},{7,3},{8,12},{9,13},{10,... | collective-permute-start | bytes 393224 | tf_op jit(solution)/shard_map/ppermute | solution.py:135
  58.0 5.7 %collective-permute-start.16 = (f32[512]{0:T(512)S(1)}, f32[512]{0:T(512)S(1)}, u32[]{:S(2)}, u32[]{:S(2)}) collective-permute-start(f32[512]{0:T(512)S(1)} %convert_reduce_fusion), channel_id=1, source_target_pairs={{0,16},{16,0},{1,17},{17,1},{2,18},{18,2},{3,19},{19,3},{4,20},{20... | collective-permute-start | bytes 6152 | tf_op jit(solution)/shard_map/ppermute | solution.py:230
  61.2 5.2 %collective-permute-start.15 = (bf16[1,4,32,256]{3,2,1,0:T(8,128)(2,1)S(1)}, bf16[1,4,32,256]{3,2,1,0:T(8,128)(2,1)S(1)}, u32[]{:S(2)}, u32[]{:S(2)}) collective-permute-start(bf16[1,4,32,256]{3,2,1,0:T(8,128)(2,1)S(1)} %slice.67), channel_id=1, source_target_pairs={{0,8},{1,9},{2,10},{3,11},{4,12},{5,13},{6,14},{7,15},{8,0},{9,1},... | collective-permute-start | bytes 196616 | tf_op jit(solution)/shard_map/ppermute | solution.py:135

commit v5 on v4

--- a/solution.py
+++ b/solution.py
@@ -26,29 +26,24 @@
 
 def row_kernel(groups, offsets, place, rows_ref, gain_ref, *refs):
     w_refs, rest = refs[: groups * len(offsets)], refs[groups * len(offsets) :]
-    wg_refs, cells_ref, (w_all, norm_s, att_s, sems) = rest[:groups], rest[groups], rest[groups + 1 :]
+    wg_refs, cells_ref, (w_all, norm_s, att_s) = rest[:groups], rest[groups], rest[groups + 1 :]
     group, track = place[0], place[1]
     senders, pair, _ = rows_ref.shape
     tracks = pair // 2
     width = gain_ref.shape[1]
     length = senders * tracks
     count, _, cols, part = wg_refs[0].shape
-    copies = []
     for step in range(groups):
         owner = lax.rem(group - step + groups, groups)
         lanes = pl.ds(pl.multiple_of(owner * part, part), part)
         for at, held in enumerate(offsets):
+            w_ref = w_refs[step * len(offsets) + at]
+            size = w_ref.shape[2]
             for slot, offset in enumerate(held):
-                size = w_refs[0].shape[2]
                 begin = (track ^ offset) * size if len(offsets) > 1 else 0
                 rows = pl.ds(pl.multiple_of(begin, size), size)
-                copy = pltpu.make_async_copy(
-                    w_refs[step * len(offsets) + at].at[slot],
-                    w_all.at[:, rows, lanes],
-                    sems.at[len(copies)],
-                )
-                copy.start()
-                copies.append(copy)
+                for index in range(4):
+                    w_all[index, rows, lanes] = w_ref[slot, index]
     both = rows_ref[...].astype(F32)
     values = both[:, :tracks].reshape(length, width)
     upstream = both[:, tracks:].reshape(length, width)
@@ -60,8 +55,6 @@
     centred = offset * inv_std
     normed = (centred * gain).astype(BF)
     up = upstream.astype(BF)
-    for copy in copies:
-        copy.wait()
     projected = [dot(normed, w_all[index], ((1,), (1,))).astype(BF) for index in range(3)]
     grad_att = dot(up, w_all[3], ((1,), (0,))).astype(BF)
     size = width // HEADS
@@ -103,13 +96,11 @@
     )
     cells = upstream + branch.astype(BF).astype(F32)
     high = gain_term.astype(BF).astype(F32)
-    low = gain_term - high
-    which = lax.broadcasted_iota(jnp.int32, (tracks, width), 0)
-    extra = jnp.where(which == 0, high, jnp.where(which == 1, low, 0.0))
-    extra = jnp.broadcast_to(extra[None], (senders, tracks, width))
-    cells_ref[...] = jnp.concatenate(
-        [cells.reshape(senders, tracks, width), extra], 1
-    ).astype(BF)
+    terms = jnp.concatenate([high, gain_term - high], 1)
+    lanes = 2 * width // tracks
+    terms = jnp.concatenate([terms[:, at * lanes : (at + 1) * lanes] for at in range(tracks)], 0)
+    terms = jnp.broadcast_to(terms[None], (senders, tracks, lanes)).reshape(length, lanes)
+    cells_ref[...] = jnp.concatenate([cells, terms], 1).astype(BF)
     for at in range(groups):
         norm_s[at] = normed[:, at * part : (at + 1) * part]
         att_s[at] = attended[:, at * part : (at + 1) * part]
@@ -174,11 +165,12 @@
     moved = [swap(blocks[bits], axis, bits) for bits in (1, 3, 2)]
     total = blocks[0].astype(F32) + sum(block.astype(F32) for block in moved)
     bit = 4
-    while bit < count:
+    while total.shape[0] > 4:
         half = total.shape[0] // 2
         total = total[:half] + swap(total[half:].astype(BF), axis, bit).astype(F32)
         bit *= 2
-    return total[0]
+    low = total.astype(BF)
+    return [total[0]] + [swap(low[at], axis, bits * bit) for at, bits in ((1, 2), (2, 1), (3, 3))]
 
 
 def shards(fields, upstream, ln_gain, weights):
@@ -205,15 +197,13 @@
     *wg, cells = pl.pallas_call(
         functools.partial(row_kernel, groups, offsets),
         out_shape=(jax.ShapeDtypeStruct(out_shape, BF),) * groups
-        + (jax.ShapeDtypeStruct((count, 2 * trk_dev, width), BF),),
-        in_specs=[pl.BlockSpec(memory_space=pltpu.SMEM), vmem, vmem]
-        + [pl.BlockSpec(memory_space=pl.ANY)] * len(w_parts),
+        + (jax.ShapeDtypeStruct((count * trk_dev, width + 2 * width // trk_dev), BF),),
+        in_specs=[pl.BlockSpec(memory_space=pltpu.SMEM)] + [vmem] * (2 + len(w_parts)),
         out_specs=(vmem,) * (groups + 1),
         scratch_shapes=[
             pltpu.VMEM((4, width, width), BF),
             pltpu.VMEM((groups, trk_dev * count, part), BF),
             pltpu.VMEM((groups, trk_dev * count, part), BF),
-            pltpu.SemaphoreType.DMA((groups * sum(len(held) for held in offsets),)),
         ],
         compiler_params=pltpu.CompilerParams(vmem_limit_bytes=48 * 2**20),
     )(place, row, ln_gain[None], *w_parts)
@@ -223,13 +213,16 @@
     total = wg[0].astype(F32)
     for k in range(1, groups):
         total = total + lax.ppermute(wg[k], "grp", ring(groups, k)).astype(F32)
-    total = scatter_sum(total.astype(BF), "trk")
-    grad_fields = back[:, :trk_dev]
-    gain_sum = jnp.sum(back[:, trk_dev : trk_dev + 2].astype(F32), (0, 1))
+    terms = scatter_sum(total.astype(BF), "trk")
+    terms[3], back = lax.optimization_barrier((terms[3], back))
+    grad_fields = back[:, :width].reshape(count, trk_dev, width)
+    gain_sum = jnp.sum(back[:, width:].astype(F32).reshape(count, 2, width), (0, 1))
     if groups == 2:
         gain_sum = gain_sum + lax.ppermute(gain_sum, "grp", ring(2, 1))
     else:
         gain_sum = jnp.sum(lax.all_gather(gain_sum, "grp"), 0)
+    terms[1], terms[2], grad_fields, gain_sum = lax.optimization_barrier((terms[1], terms[2], grad_fields, gain_sum))
+    total = sum(term.astype(F32) for term in terms)
     factor = float(cell_count) ** (-0.5)
     return (grad_fields, total.transpose(0, 2, 1) * factor, gain_sum * factor)
 

time: 67.5 us -> 64.8 us (0.960)
  waiting for transfers between devices: 27 us -> 24.9 us
  Pallas kernels: 5.42 us -> 4.72 us
    ppermute x11 -> x12, waiting for transfers between devices: 22.9 us -> 20.3 us  [swap(): lax.ppermute(array, axis, [(i, i ^ bits) for i in range(lax.axis_size(axi...]
    pallas_call x1, Pallas kernels: 5.42 us -> 4.72 us  [shards(): pl.pallas_call(functools.partial(row_kernel, groups, offsets), out_shape=...]
    reshape x0 -> x2, local copies, waits for them, and re-layouts: none -> 0.7 us  [the longest x1 0.66 us: shards(): grad_fields = back[:, :width].reshape(count, trk_dev, width)]
    slice x3 -> x0, local copies, waits for them, and re-layouts: 0.69 us -> none  [the longest x1 0.66 us: shards(): grad_fields = back[:, :trk_dev]]
    ppermute x11 -> x12, starting transfers between devices: 17.3 us -> 17.3 us  [swap(): lax.ppermute(array, axis, [(i, i ^ bits) for i in range(lax.axis_size(axi...]
  transfers between devices with their start and end apart: 19 -> 20, of which waited for: 11 -> 12; matrix products, arithmetic and copies ran while one was open for 5% -> 4% of each run, Pallas kernels for 0% -> 0%
where the time goes in v5:
time: 64.8 us; the launch traced here: 64.4 us
  starting transfers between devices  28.6 us (44%)
  waiting for transfers between devices  24.9 us (38%)
  Pallas kernels  4.72 us (7%)
  other arithmetic  4.59 us (7%)
  local copies, waits for them, and re-layouts  0.77 us (1%)
  between operations  0.74 us (1%)
    ppermute x12, waiting for transfers between devices, swap(): lax.ppermute(array, axis, [(i, i ^ bits) for i in range(lax.axis_size(axi...  20.3 us
    ppermute x12, starting transfers between devices, swap(): lax.ppermute(array, axis, [(i, i ^ bits) for i in range(lax.axis_size(axi...  17.3 us
    all_to_all x1, starting transfers between devices, shards(): back = lax.all_to_all(cells, 'trk', split_axis=0, concat_axis=0, tiled=True)  5.47 us
    all_to_all x1, starting transfers between devices, shards(): row = lax.all_to_all(both, 'trk', split_axis=0, concat_axis=0, tiled=True)  5.42 us
    pallas_call x1, Pallas kernels, shards(): pl.pallas_call(functools.partial(row_kernel, groups, offsets), out_shape=...  4.72 us
    ppermute x1, waiting for transfers between devices, shards(): total = total + lax.ppermute(wg[k], 'grp', ring(groups, k)).astype(F32)  2.66 us
    concatenate x1, other arithmetic, shards(): both = jnp.concatenate([fields, upstream], 1)  1.71 us
    all_to_all x1, waiting for transfers between devices, shards(): row = lax.all_to_all(both, 'trk', split_axis=0, concat_axis=0, tiled=True)  1.45 us
  transfers between devices with their start and end apart: 20, of which 12 were waited for; matrix products, arithmetic and copies ran while one was open for 4% of the time, Pallas kernels for 0%

profile of v5, /device:TPU:0, one launch (start us, length us, event | category | flops | bytes accessed | tf_op | source)
XLA Modules:
  0.0 64.4 jit_solution(16100047527673272991)
XLA Ops:
  0.6 0.0 copy-start
  0.6 5.1 %collective-permute-start.2 = (bf16[1,4,32,256]{3,2,1,0:T(8,128)(2,1)}, bf16[1,4,32,256]{3,2,1,0:T(8,128)(2,1)S(1)}, u32[]{:S(2)}, u32[]{:S(2)}) collective-permute-start(bf16[1,4,32,256]{3,2,1,0:T(8,128)(2,1)} %bitcast.33), channel_id=1, source_target_pairs={{0,12},{1,13},{2,14},{3,15},{4,8},{5,9},{6,10},{7,11},{8,4},{9,5},... | collective-permute-start | bytes 196616 | tf_op jit(solution)/shard_map/ppermute | solution.py:126
  5.8 0.0 collective-permute-start.1
  5.8 0.6 collective-permute-start
  6.4 1.7 %pad_maximum_fusion = bf16[16,16,512]{2,1,0:T(8,128)(2,1)} fusion(bf16[16,8,512]{2,1,0:T(8,128)(2,1)} %param.5, bf16[16,8,512]{2,1,0:T(8,128)(2,1)} %param.4), kind=kLoop, calls=%fused_computation.2 | loop fusion | flops 524288 | bytes 524288 | tf_op jit(solution)/shard_map/concatenate | solution.py:182
  8.1 3.5 %collective-permute-done = bf16[1,4,32,256]{3,2,1,0:T(8,128)(2,1)S(1)} collective-permute-done((bf16[1,4,32,256]{3,2,1,0:T(8,128)(2,1)}, bf16[1,4,32,256]{3,2,1,0:T(8,128)(2,1)S(1)}, u32[]{:S(2)}, u32[]{:S(2)}) %collective-permute-start) | collective-permute-done | bytes 65568 | tf_op jit(solution)/shard_map/ppermute | solution.py:126
  11.6 0.0 collective-permute-done.2
  11.6 0.0 collective-permute-done.1
  11.6 0.9 %pad_maximum_fusion.1.refs_0_ = bf16[4,4,32,256]{3,2,1,0:T(8,128)(2,1)S(1)} fusion(bf16[1,4,32,256]{3,2,1,0:T(8,128)(2,1)S(1)} %collective-permute-done.2, bf16[1,4,32,256]{3,2,1,0:T(8,128)(2,1)S(1)} %collective-permute-done.1, bf16[1,4,32,256]{3,2,1,0:T(8,128)(2,1)S(1)} %collective-permute-done, bf16[1,4,32,256]{3,2,1,0:T(8,128)(2,1)} %bitcast.36), kind=kLoop, calls=%fused_computation.3 | loop fusion | flops 393216 | bytes 524288 | tf_op jit(solution)/shard_map/concatenate | solution.py:156
  12.5 2.5 %collective-permute-start.5 = (bf16[4,4,32,256]{3,2,1,0:T(8,128)(2,1)S(1)}, bf16[4,4,32,256]{3,2,1,0:T(8,128)(2,1)S(1)}, u32[]{:S(2)}, u32[]{:S(2)}) collective-permute-start(bf16[4,4,32,256]{3,2,1,0:T(8,128)(2,1)S(1)} %pad_maximum_fusion.1.refs_0_), channel_id=1, source_target_pairs={{0,3},{1,2},{2,1},{3,0},{4,7},{5,6},{6,5},{7,4},{8,11},{9,10},{10,... | collective-permute-start | bytes 786440 | tf_op jit(solution)/shard_map/ppermute | solution.py:126
  15.0 0.5 collective-permute-start.4
  15.5 0.5 collective-permute-start.3
  16.0 5.4 %all-to-all-start = ((bf16[16,16,512]{2,1,0:T(8,128)(2,1)}), bf16[16,16,512]{2,1,0:T(8,128)(2,1)S(1)}, u32[]{:S(2)}, u32[]{:S(2)}) async-start(bf16[16,16,512]{2,1,0:T(8,128)(2,1)} %pad_maximum_fusion), calls=%async_computation | async-start | bytes 524288 | tf_op jit(solution)/shard_map/all_to_all | solution.py:184
  21.5 0.1 collective-permute-start.6
  21.6 1.2 %collective-permute-done.5.refs_3_ = bf16[4,4,32,256]{3,2,1,0:T(8,128)(2,1)S(1)} collective-permute-done((bf16[4,4,32,256]{3,2,1,0:T(8,128)(2,1)S(1)}, bf16[4,4,32,256]{3,2,1,0:T(8,128)(2,1)S(1)}, u32[]{:S(2)}, u32[]{:S(2)}) %collective-permute-start.5) | collective-permute-done | bytes 262176 | tf_op jit(solution)/shard_map/ppermute | solution.py:126
  22.7 0.0 collective-permute-start.9
  22.7 5.2 %collective-permute-done.4.refs_2_ = bf16[4,4,32,256]{3,2,1,0:T(8,128)(2,1)S(1)} collective-permute-done((bf16[4,4,32,256]{3,2,1,0:T(8,128)(2,1)S(1)}, bf16[4,4,32,256]{3,2,1,0:T(8,128)(2,1)S(1)}, u32[]{:S(2)}, u32[]{:S(2)}) %collective-permute-start.4) | collective-permute-done | bytes 262176 | tf_op jit(solution)/shard_map/ppermute | solution.py:126
  27.9 0.0 collective-permute-start.8
  27.9 0.2 collective-permute-done.3.refs_1_
  28.2 0.3 collective-permute-start.7
  28.4 0.1 pad_add_fusion.place
  28.5 0.0 collective-permute-done.6.refs_4_
  28.5 1.4 %all-to-all-done.rows_ref = bf16[16,16,512]{2,1,0:T(8,128)(2,1)S(1)} async-done(((bf16[16,16,512]{2,1,0:T(8,128)(2,1)}), bf16[16,16,512]{2,1,0:T(8,128)(2,1)S(1)}, u32[]{:S(2)}, u32[]{:S(2)}) %all-to-all-start) | async-done | bytes 262176 | tf_op jit(solution)/shard_map/all_to_all | solution.py:184
  30.0 0.0 collective-permute-done.9.refs_7_
  30.0 0.0 collective-permute-done.8.refs_6_
  30.0 0.0 collective-permute-done.7.refs_5_
  30.0 0.0 copy-done
  30.0 4.7 %shard_map.67 = (bf16[16,4,32,256]{3,2,1,0:T(8,128)(2,1)S(1)}, bf16[16,4,32,256]{3,2,1,0:T(8,128)(2,1)S(1)}, bf16[128,640]{1,0:T(8,128)(2,1)}) custom-call(s32[2]{0:T(128)S(1)} %pad_add_fusion.place, bf16[16,16,512]{2,1,0:T(8,128)(2,1)S(1)} %all-to-all-done.rows_ref, f32[1,512]{1,0:T(1,128)S(1)} %bitcast.30, ...), custom_call_target="tpu_custom_call" | custom-call | tf_op jit(solution)/shard_map/pallas_call | solution.py:197
  34.7 0.0 collective-permute-start.10
  34.7 2.7 %collective-permute-done.10 = bf16[16,4,32,256]{3,2,1,0:T(8,128)(2,1)S(1)} collective-permute-done((bf16[16,4,32,256]{3,2,1,0:T(8,128)(2,1)S(1)}, bf16[16,4,32,256]{3,2,1,0:T(8,128)(2,1)S(1)}, u32[]{:S(2)}, u32[]{:S(2)}) %collective-permute-start.10) | collective-permute-done | bytes 1048608 | tf_op jit(solution)/shard_map/ppermute | solution.py:215
  37.4 0.4 add_convert_fusion
  37.8 0.1 fusion.6
  37.9 1.7 %collective-permute-start.11 = (bf16[4,4,32,256]{3,2,1,0:T(8,128)(2,1)S(1)}, bf16[4,4,32,256]{3,2,1,0:T(8,128)(2,1)S(1)}, u32[]{:S(2)}, u32[]{:S(2)}) collective-permute-start(bf16[4,4,32,256]{3,2,1,0:T(8,128)(2,1)S(1)} %get-tuple-element.27), channel_id=1, source_target_pairs={{0,1},{1,0},{2,3},{3,2},{4,5},{5,4},{6,7},{7,6},{8,9},{9,8},{10,11... | collective-permute-start | bytes 786440 | tf_op jit(solution)/shard_map/ppermute | solution.py:126
  39.5 0.8 %collective-permute-start.13 = (bf16[4,4,32,256]{3,2,1,0:T(8,128)(2,1)S(1)}, bf16[4,4,32,256]{3,2,1,0:T(8,128)(2,1)S(1)}, u32[]{:S(2)}, u32[]{:S(2)}) collective-permute-start(bf16[4,4,32,256]{3,2,1,0:T(8,128)(2,1)S(1)} %get-tuple-element.28), channel_id=1, source_target_pairs={{0,2},{1,3},{2,0},{3,1},{4,6},{5,7},{6,4},{7,5},{8,10},{9,11},{10,... | collective-permute-start | bytes 786440 | tf_op jit(solution)/shard_map/ppermute | solution.py:126
  40.3 1.1 %collective-permute-start.12 = (bf16[4,4,32,256]{3,2,1,0:T(8,128)(2,1)S(1)}, bf16[4,4,32,256]{3,2,1,0:T(8,128)(2,1)S(1)}, u32[]{:S(2)}, u32[]{:S(2)}) collective-permute-start(bf16[4,4,32,256]{3,2,1,0:T(8,128)(2,1)S(1)} %get-tuple-element.29), channel_id=1, source_target_pairs={{0,3},{1,2},{2,1},{3,0},{4,7},{5,6},{6,5},{7,4},{8,11},{9,10},{10,... | collective-permute-start | bytes 786440 | tf_op jit(solution)/shard_map/ppermute | solution.py:126
  41.4 5.5 %all-to-all-start.1 = ((bf16[16,8,640]{2,1,0:T(8,128)(2,1)}), bf16[16,8,640]{2,1,0:T(8,128)(2,1)S(1)}, u32[]{:S(2)}, u32[]{:S(2)}) async-start(bf16[16,8,640]{2,1,0:T(8,128)(2,1)} %bitcast.9), calls=%async_computation.1 | async-start | bytes 327680 | tf_op jit(solution)/shard_map/all_to_all | solution.py:212
  46.9 0.2 collective-permute-done.11
  47.1 6.6 %collective-permute-done.13 = bf16[4,4,32,256]{3,2,1,0:T(8,128)(2,1)S(1)} collective-permute-done((bf16[4,4,32,256]{3,2,1,0:T(8,128)(2,1)S(1)}, bf16[4,4,32,256]{3,2,1,0:T(8,128)(2,1)S(1)}, u32[]{:S(2)}, u32[]{:S(2)}) %collective-permute-start.13) | collective-permute-done | bytes 262176 | tf_op jit(solution)/shard_map/ppermute | solution.py:126
  53.7 1.0 %collective-permute-done.12 = bf16[4,4,32,256]{3,2,1,0:T(8,128)(2,1)S(1)} collective-permute-done((bf16[4,4,32,256]{3,2,1,0:T(8,128)(2,1)S(1)}, bf16[4,4,32,256]{3,2,1,0:T(8,128)(2,1)S(1)}, u32[]{:S(2)}, u32[]{:S(2)}) %collective-permute-start.12) | collective-permute-done | bytes 262176 | tf_op jit(solution)/shard_map/ppermute | solution.py:126
  54.7 0.2 fusion.5
  55.0 2.8 %collective-permute-start.16 = (bf16[4,32,256]{2,1,0:T(8,128)(2,1)S(1)}, bf16[4,32,256]{2,1,0:T(8,128)(2,1)S(1)}, u32[]{:S(2)}, u32[]{:S(2)}) collective-permute-start(bf16[4,32,256]{2,1,0:T(8,128)(2,1)S(1)} %get-tuple-element.30), channel_id=1, source_target_pairs={{0,12},{1,13},{2,14},{3,15},{4,8},{5,9},{6,10},{7,11},{8,4},{9,5},... | collective-permute-start | bytes 196616 | tf_op jit(solution)/shard_map/ppermute | solution.py:126
  57.8 0.0 collective-permute-start.15
  57.8 1.6 %collective-permute-start.14 = (bf16[4,32,256]{2,1,0:T(8,128)(2,1)S(1)}, bf16[4,32,256]{2,1,0:T(8,128)(2,1)S(1)}, u32[]{:S(2)}, u32[]{:S(2)}) collective-permute-start(bf16[4,32,256]{2,1,0:T(8,128)(2,1)S(1)} %get-tuple-element.32), channel_id=1, source_target_pairs={{0,8},{1,9},{2,10},{3,11},{4,12},{5,13},{6,14},{7,15},{8,0},{9,1},... | collective-permute-start | bytes 196616 | tf_op jit(solution)/shard_map/ppermute | solution.py:126
  59.4 0.0 all-to-all-done.1
  59.4 1.8 %collective-permute-done.16 = bf16[4,32,256]{2,1,0:T(8,128)(2,1)S(1)} collective-permute-done((bf16[4,32,256]{2,1,0:T(8,128)(2,1)S(1)}, bf16[4,32,256]{2,1,0:T(8,128)(2,1)S(1)}, u32[]{:S(2)}, u32[]{:S(2)}) %collective-permute-start.16) | collective-permute-done | bytes 65568 | tf_op jit(solution)/shard_map/ppermute | solution.py:126
  61.3 0.1 collective-permute-start.17
  61.3 0.7 %slice_bitcast_fusion.1 = bf16[16,8,512]{2,1,0:T(8,128)(2,1)} fusion(bf16[128,640]{1,0:T(8,128)(2,1)S(1)} %bitcast.32), kind=kLoop, calls=%fused_computation.10 | loop fusion | bytes 262144 | tf_op jit(solution)/shard_map/reshape | solution.py:218
  62.0 0.5 collective-permute-done.17
  62.5 0.0 collective-permute-done.15
  62.5 0.6 collective-permute-done.14
  63.1 0.6 broadcast_multiply_fusion
  63.7 0.7 %fusion.4 = f32[4,256,32]{1,2,0:T(8,128)} fusion(f32[4,4,32,256]{3,2,1,0:T(8,128)S(1)} %get-tuple-element.26, bf16[4,32,256]{2,1,0:T(8,128)(2,1)S(1)} %collective-permute-done.16, bf16[4,32,256]{2,1,0:T(8,128)(2,1)S(1)} %collective-permute-done.15, bf16[4,32,256]{2,1,0:T(8,128)(2,1)S(1)} %collective-permute-done.14), kind=kLoop, calls=%fused_computation.9 | loop fusion | flops 229376 | bytes 458752 | tf_op jit(solution)/shard_map/mul | solution.py:227
  (5 shorter events, 0.1 us)
Async XLA Ops:
  0.6 29.4 %copy-start = (f32[512]{0:T(512)S(1)}, f32[512]{0:T(512)}, u32[]{:S(2)}) copy-start(f32[512]{0:T(512)} %param.6) | copy-start | bytes 6148
  0.6 11.0 %collective-permute-start.2 = (bf16[1,4,32,256]{3,2,1,0:T(8,128)(2,1)}, bf16[1,4,32,256]{3,2,1,0:T(8,128)(2,1)S(1)}, u32[]{:S(2)}, u32[]{:S(2)}) collective-permute-start(bf16[1,4,32,256]{3,2,1,0:T(8,128)(2,1)} %bitcast.33), channel_id=1, source_target_pairs={{0,12},{1,13},{2,14},{3,15},{4,8},{5,9},{6,10},{7,11},{8,4},{9,5},... | collective-permute-start | bytes 196616 | tf_op jit(solution)/shard_map/ppermute | solution.py:126
  5.8 5.9 %collective-permute-start.1 = (bf16[1,4,32,256]{3,2,1,0:T(8,128)(2,1)}, bf16[1,4,32,256]{3,2,1,0:T(8,128)(2,1)S(1)}, u32[]{:S(2)}, u32[]{:S(2)}) collective-permute-start(bf16[1,4,32,256]{3,2,1,0:T(8,128)(2,1)} %bitcast.34), channel_id=1, source_target_pairs={{0,4},{1,5},{2,6},{3,7},{4,0},{5,1},{6,2},{7,3},{8,12},{9,13},{10,... | collective-permute-start | bytes 196616 | tf_op jit(solution)/shard_map/ppermute | solution.py:126
  5.8 5.8 %collective-permute-start = (bf16[1,4,32,256]{3,2,1,0:T(8,128)(2,1)}, bf16[1,4,32,256]{3,2,1,0:T(8,128)(2,1)S(1)}, u32[]{:S(2)}, u32[]{:S(2)}) collective-permute-start(bf16[1,4,32,256]{3,2,1,0:T(8,128)(2,1)} %bitcast.35), channel_id=1, source_target_pairs={{0,8},{1,9},{2,10},{3,11},{4,12},{5,13},{6,14},{7,15},{8,0},{9,1},... | collective-permute-start | bytes 196616 | tf_op jit(solution)/shard_map/ppermute | solution.py:126
  12.5 10.2 %collective-permute-start.5 = (bf16[4,4,32,256]{3,2,1,0:T(8,128)(2,1)S(1)}, bf16[4,4,32,256]{3,2,1,0:T(8,128)(2,1)S(1)}, u32[]{:S(2)}, u32[]{:S(2)}) collective-permute-start(bf16[4,4,32,256]{3,2,1,0:T(8,128)(2,1)S(1)} %pad_maximum_fusion.1.refs_0_), channel_id=1, source_target_pairs={{0,3},{1,2},{2,1},{3,0},{4,7},{5,6},{6,5},{7,4},{8,11},{9,10},{10,... | collective-permute-start | bytes 786440 | tf_op jit(solution)/shard_map/ppermute | solution.py:126
  15.0 12.9 %collective-permute-start.4 = (bf16[4,4,32,256]{3,2,1,0:T(8,128)(2,1)S(1)}, bf16[4,4,32,256]{3,2,1,0:T(8,128)(2,1)S(1)}, u32[]{:S(2)}, u32[]{:S(2)}) collective-permute-start(bf16[4,4,32,256]{3,2,1,0:T(8,128)(2,1)S(1)} %pad_maximum_fusion.1.refs_0_), channel_id=1, source_target_pairs={{0,2},{1,3},{2,0},{3,1},{4,6},{5,7},{6,4},{7,5},{8,10},{9,11},{10,... | collective-permute-start | bytes 786440 | tf_op jit(solution)/shard_map/ppermute | solution.py:126
  15.5 12.7 %collective-permute-start.3 = (bf16[4,4,32,256]{3,2,1,0:T(8,128)(2,1)S(1)}, bf16[4,4,32,256]{3,2,1,0:T(8,128)(2,1)S(1)}, u32[]{:S(2)}, u32[]{:S(2)}) collective-permute-start(bf16[4,4,32,256]{3,2,1,0:T(8,128)(2,1)S(1)} %pad_maximum_fusion.1.refs_0_), channel_id=1, source_target_pairs={{0,1},{1,0},{2,3},{3,2},{4,5},{5,4},{6,7},{7,6},{8,9},{9,8},{10,11... | collective-permute-start | bytes 786440 | tf_op jit(solution)/shard_map/ppermute | solution.py:126
  16.0 13.9 %all-to-all-start = ((bf16[16,16,512]{2,1,0:T(8,128)(2,1)}), bf16[16,16,512]{2,1,0:T(8,128)(2,1)S(1)}, u32[]{:S(2)}, u32[]{:S(2)}) async-start(bf16[16,16,512]{2,1,0:T(8,128)(2,1)} %pad_maximum_fusion), calls=%async_computation | async-start | bytes 524288 | tf_op jit(solution)/shard_map/all_to_all | solution.py:184
  21.5 7.1 %collective-permute-start.6 = (bf16[4,4,32,256]{3,2,1,0:T(8,128)(2,1)S(1)}, bf16[4,4,32,256]{3,2,1,0:T(8,128)(2,1)S(1)}, u32[]{:S(2)}, u32[]{:S(2)}) collective-permute-start(bf16[4,4,32,256]{3,2,1,0:T(8,128)(2,1)S(1)} %pad_maximum_fusion.1.refs_0_), channel_id=1, source_target_pairs={{0,16},{16,0},{1,17},{17,1},{2,18},{18,2},{3,19},{19,3},{4,20},{20... | collective-permute-start | bytes 786440 | tf_op jit(solution)/shard_map/ppermute | solution.py:191
  22.7 7.3 %collective-permute-start.9 = (bf16[4,4,32,256]{3,2,1,0:T(8,128)(2,1)S(1)}, bf16[4,4,32,256]{3,2,1,0:T(8,128)(2,1)S(1)}, u32[]{:S(2)}, u32[]{:S(2)}) collective-permute-start(bf16[4,4,32,256]{3,2,1,0:T(8,128)(2,1)S(1)} %collective-permute-done.5.refs_3_), channel_id=1, source_target_pairs={{0,16},{16,0},{1,17},{17,1},{2,18},{18,2},{3,19},{19,3},{4,20},{20... | collective-permute-start | bytes 786440 | tf_op jit(solution)/shard_map/ppermute | solution.py:191
  27.9 2.0 %collective-permute-start.8 = (bf16[4,4,32,256]{3,2,1,0:T(8,128)(2,1)S(1)}, bf16[4,4,32,256]{3,2,1,0:T(8,128)(2,1)S(1)}, u32[]{:S(2)}, u32[]{:S(2)}) collective-permute-start(bf16[4,4,32,256]{3,2,1,0:T(8,128)(2,1)S(1)} %collective-permute-done.4.refs_2_), channel_id=1, source_target_pairs={{0,16},{16,0},{1,17},{17,1},{2,18},{18,2},{3,19},{19,3},{4,20},{20... | collective-permute-start | bytes 786440 | tf_op jit(solution)/shard_map/ppermute | solution.py:191
  28.2 1.8 %collective-permute-start.7 = (bf16[4,4,32,256]{3,2,1,0:T(8,128)(2,1)S(1)}, bf16[4,4,32,256]{3,2,1,0:T(8,128)(2,1)S(1)}, u32[]{:S(2)}, u32[]{:S(2)}) collective-permute-start(bf16[4,4,32,256]{3,2,1,0:T(8,128)(2,1)S(1)} %collective-permute-done.3.refs_1_), channel_id=1, source_target_pairs={{0,16},{16,0},{1,17},{17,1},{2,18},{18,2},{3,19},{19,3},{4,20},{20... | collective-permute-start | bytes 786440 | tf_op jit(solution)/shard_map/ppermute | solution.py:191
  34.7 2.7 %collective-permute-start.10 = (bf16[16,4,32,256]{3,2,1,0:T(8,128)(2,1)S(1)}, bf16[16,4,32,256]{3,2,1,0:T(8,128)(2,1)S(1)}, u32[]{:S(2)}, u32[]{:S(2)}) collective-permute-start(bf16[16,4,32,256]{3,2,1,0:T(8,128)(2,1)S(1)} %get-tuple-element.17), channel_id=1, source_target_pairs={{0,16},{16,0},{1,17},{17,1},{2,18},{18,2},{3,19},{19,3},{4,20},{20... | collective-permute-start | bytes 3145736 | tf_op jit(solution)/shard_map/ppermute | solution.py:215
  37.9 9.2 %collective-permute-start.11 = (bf16[4,4,32,256]{3,2,1,0:T(8,128)(2,1)S(1)}, bf16[4,4,32,256]{3,2,1,0:T(8,128)(2,1)S(1)}, u32[]{:S(2)}, u32[]{:S(2)}) collective-permute-start(bf16[4,4,32,256]{3,2,1,0:T(8,128)(2,1)S(1)} %get-tuple-element.27), channel_id=1, source_target_pairs={{0,1},{1,0},{2,3},{3,2},{4,5},{5,4},{6,7},{7,6},{8,9},{9,8},{10,11... | collective-permute-start | bytes 786440 | tf_op jit(solution)/shard_map/ppermute | solution.py:126
  39.5 14.2 %collective-permute-start.13 = (bf16[4,4,32,256]{3,2,1,0:T(8,128)(2,1)S(1)}, bf16[4,4,32,256]{3,2,1,0:T(8,128)(2,1)S(1)}, u32[]{:S(2)}, u32[]{:S(2)}) collective-permute-start(bf16[4,4,32,256]{3,2,1,0:T(8,128)(2,1)S(1)} %get-tuple-element.28), channel_id=1, source_target_pairs={{0,2},{1,3},{2,0},{3,1},{4,6},{5,7},{6,4},{7,5},{8,10},{9,11},{10,... | collective-permute-start | bytes 786440 | tf_op jit(solution)/shard_map/ppermute | solution.py:126
  40.3 14.4 %collective-permute-start.12 = (bf16[4,4,32,256]{3,2,1,0:T(8,128)(2,1)S(1)}, bf16[4,4,32,256]{3,2,1,0:T(8,128)(2,1)S(1)}, u32[]{:S(2)}, u32[]{:S(2)}) collective-permute-start(bf16[4,4,32,256]{3,2,1,0:T(8,128)(2,1)S(1)} %get-tuple-element.29), channel_id=1, source_target_pairs={{0,3},{1,2},{2,1},{3,0},{4,7},{5,6},{6,5},{7,4},{8,11},{9,10},{10,... | collective-permute-start | bytes 786440 | tf_op jit(solution)/shard_map/ppermute | solution.py:126
  41.4 18.0 %all-to-all-start.1 = ((bf16[16,8,640]{2,1,0:T(8,128)(2,1)}), bf16[16,8,640]{2,1,0:T(8,128)(2,1)S(1)}, u32[]{:S(2)}, u32[]{:S(2)}) async-start(bf16[16,8,640]{2,1,0:T(8,128)(2,1)} %bitcast.9), calls=%async_computation.1 | async-start | bytes 327680 | tf_op jit(solution)/shard_map/all_to_all | solution.py:212
  55.0 6.2 %collective-permute-start.16 = (bf16[4,32,256]{2,1,0:T(8,128)(2,1)S(1)}, bf16[4,32,256]{2,1,0:T(8,128)(2,1)S(1)}, u32[]{:S(2)}, u32[]{:S(2)}) collective-permute-start(bf16[4,32,256]{2,1,0:T(8,128)(2,1)S(1)} %get-tuple-element.30), channel_id=1, source_target_pairs={{0,12},{1,13},{2,14},{3,15},{4,8},{5,9},{6,10},{7,11},{8,4},{9,5},... | collective-permute-start | bytes 196616 | tf_op jit(solution)/shard_map/ppermute | solution.py:126
  57.8 4.7 %collective-permute-start.15 = (bf16[4,32,256]{2,1,0:T(8,128)(2,1)S(1)}, bf16[4,32,256]{2,1,0:T(8,128)(2,1)S(1)}, u32[]{:S(2)}, u32[]{:S(2)}) collective-permute-start(bf16[4,32,256]{2,1,0:T(8,128)(2,1)S(1)} %get-tuple-element.31), channel_id=1, source_target_pairs={{0,4},{1,5},{2,6},{3,7},{4,0},{5,1},{6,2},{7,3},{8,12},{9,13},{10,... | collective-permute-start | bytes 196616 | tf_op jit(solution)/shard_map/ppermute | solution.py:126
  57.8 5.3 %collective-permute-start.14 = (bf16[4,32,256]{2,1,0:T(8,128)(2,1)S(1)}, bf16[4,32,256]{2,1,0:T(8,128)(2,1)S(1)}, u32[]{:S(2)}, u32[]{:S(2)}) collective-permute-start(bf16[4,32,256]{2,1,0:T(8,128)(2,1)S(1)} %get-tuple-element.32), channel_id=1, source_target_pairs={{0,8},{1,9},{2,10},{3,11},{4,12},{5,13},{6,14},{7,15},{8,0},{9,1},... | collective-permute-start | bytes 196616 | tf_op jit(solution)/shard_map/ppermute | solution.py:126
  61.3 1.2 %collective-permute-start.17 = (f32[512]{0:T(512)S(1)}, f32[512]{0:T(512)S(1)}, u32[]{:S(2)}, u32[]{:S(2)}) collective-permute-start(f32[512]{0:T(512)S(1)} %reduce_sum.9), channel_id=1, source_target_pairs={{0,16},{16,0},{1,17},{17,1},{2,18},{18,2},{3,19},{19,3},{4,20},{20... | collective-permute-start | bytes 6152 | tf_op jit(solution)/shard_map/ppermute | solution.py:221

commit v6 on v5

--- a/solution.py
+++ b/solution.py
@@ -24,36 +24,65 @@
     return slot
 
 
-def row_kernel(groups, offsets, place, rows_ref, gain_ref, *refs):
-    w_refs, rest = refs[: groups * len(offsets)], refs[groups * len(offsets) :]
-    wg_refs, cells_ref, (w_all, norm_s, att_s) = rest[:groups], rest[groups], rest[groups + 1 :]
-    group, track = place[0], place[1]
-    senders, pair, _ = rows_ref.shape
-    tracks = pair // 2
-    width = gain_ref.shape[1]
-    length = senders * tracks
-    count, _, cols, part = wg_refs[0].shape
+def join_weights(groups, offsets, group, track, w_refs, w_all):
     for step in range(groups):
-        owner = lax.rem(group - step + groups, groups)
-        lanes = pl.ds(pl.multiple_of(owner * part, part), part)
         for at, held in enumerate(offsets):
             w_ref = w_refs[step * len(offsets) + at]
-            size = w_ref.shape[2]
+            _, _, size, part = w_ref.shape
+            owner = lax.rem(group - step + groups, groups)
+            lanes = pl.ds(pl.multiple_of(owner * part, part), part)
             for slot, offset in enumerate(held):
                 begin = (track ^ offset) * size if len(offsets) > 1 else 0
                 rows = pl.ds(pl.multiple_of(begin, size), size)
                 for index in range(4):
                     w_all[index, rows, lanes] = w_ref[slot, index]
+
+
+def read_row(rows_ref):
+    senders, pair, width = rows_ref.shape
+    tracks = pair // 2
     both = rows_ref[...].astype(F32)
-    values = both[:, :tracks].reshape(length, width)
-    upstream = both[:, tracks:].reshape(length, width)
-    gain = gain_ref[...]
+    return [both[:, at : at + tracks].reshape(senders * tracks, width) for at in (0, tracks)]
+
+
+def normalize(values, gain):
     row_mean = jnp.mean(values, -1, keepdims=True)
     offset = values - row_mean
     row_var = jnp.mean(offset * offset, -1, keepdims=True)
     inv_std = lax.rsqrt(row_var + 1e-05)
     centred = offset * inv_std
-    normed = (centred * gain).astype(BF)
+    return (centred * gain).astype(BF), centred, inv_std
+
+
+def write_grads(track, wg_ref, grads, up, norm_part, att_part):
+    count, _, cols, part = wg_ref.shape
+    for index in range(4):
+        if index < 3:
+            block = dot(grads[index], norm_part, ((0,), (0,))).astype(BF)
+        else:
+            block = dot(up, att_part, ((0,), (0,))).astype(BF)
+        block = block.reshape(count, cols, part)
+        for to in range(count):
+            slot = send_slot(track ^ to, count) if count > 1 else 0
+            wg_ref[slot, index] = block[to]
+
+
+def pick(array, group, groups, scratch):
+    part = array.shape[1] // groups
+    for at in range(groups):
+        scratch[at] = array[:, at * part : (at + 1) * part]
+    return scratch[group]
+
+
+def attend_kernel(groups, offsets, place, rows_ref, gain_ref, *refs):
+    held = groups * len(offsets)
+    w_refs, wg_refs, refs = refs[:held], refs[held : held + groups - 1], refs[held + groups - 1 :]
+    grads_ref, att_ref, w_all, same_gain_ref, norm_s, att_s = refs
+    group, track = place[0], place[1]
+    join_weights(groups, offsets, group, track, w_refs, w_all)
+    values, upstream = read_row(rows_ref)
+    length, width = values.shape
+    normed, _, _ = normalize(values, gain_ref[...][:1])
     up = upstream.astype(BF)
     projected = [dot(normed, w_all[index], ((1,), (1,))).astype(BF) for index in range(3)]
     grad_att = dot(up, w_all[3], ((1,), (0,))).astype(BF)
@@ -86,6 +115,30 @@
         pieces[3].append(jnp.where(first, out2[:length], out2[length:]).astype(BF))
     grads = [jnp.concatenate(piece, 1) for piece in pieces[:3]]
     attended = jnp.concatenate(pieces[3], 1)
+    for step in range(1, groups):
+        owner = lax.rem(group + step, groups)
+        write_grads(
+            track,
+            wg_refs[step - 1],
+            grads,
+            up,
+            pick(normed, owner, groups, norm_s),
+            pick(attended, owner, groups, att_s),
+        )
+    for index in range(3):
+        grads_ref[index] = grads[index]
+    att_ref[...] = attended
+    same_gain_ref[...] = gain_ref[...][:1]
+
+
+def cells_kernel(groups, place, rows_ref, gain_ref, w_all, grads_ref, att_ref, wg_ref, cells_ref, norm_s, att_s):
+    group, track = place[0], place[1]
+    values, upstream = read_row(rows_ref)
+    senders, tracks = rows_ref.shape[0], rows_ref.shape[1] // 2
+    length, width = values.shape
+    gain = gain_ref[...]
+    normed, centred, inv_std = normalize(values, gain)
+    grads = [grads_ref[index] for index in range(3)]
     grad_normed = sum(dot(grads[index], w_all[index], ((1,), (0,))) for index in range(3))
     gain_term = jnp.sum(grad_normed * centred, 0, keepdims=True)
     scaled = grad_normed * gain
@@ -101,21 +154,14 @@
     terms = jnp.concatenate([terms[:, at * lanes : (at + 1) * lanes] for at in range(tracks)], 0)
     terms = jnp.broadcast_to(terms[None], (senders, tracks, lanes)).reshape(length, lanes)
     cells_ref[...] = jnp.concatenate([cells, terms], 1).astype(BF)
-    for at in range(groups):
-        norm_s[at] = normed[:, at * part : (at + 1) * part]
-        att_s[at] = attended[:, at * part : (at + 1) * part]
-    for step in range(groups):
-        owner = lax.rem(group + step, groups)
-        norm_part, att_part = norm_s[owner], att_s[owner]
-        for index in range(4):
-            if index < 3:
-                block = dot(grads[index], norm_part, ((0,), (0,))).astype(BF)
-            else:
-                block = dot(up, att_part, ((0,), (0,))).astype(BF)
-            block = block.reshape(count, cols, part)
-            for to in range(count):
-                slot = send_slot(track ^ to, count) if count > 1 else 0
-                wg_refs[step][slot, index] = block[to]
+    write_grads(
+        track,
+        wg_ref,
+        grads,
+        upstream.astype(BF),
+        pick(normed, group, groups, norm_s),
+        pick(att_ref[...], group, groups, att_s),
+    )
 
 
 def ring(size, step):
@@ -180,6 +226,9 @@
     cell_count = rows_dev * groups * trk_dev * count
     group, track = lax.axis_index("grp"), lax.axis_index("trk")
     both = jnp.concatenate([fields, upstream], 1)
+    gain = jnp.broadcast_to(ln_gain, (8, width))
+    place = jnp.stack([group, track]).astype(jnp.int32)
+    place, gain, both = lax.optimization_barrier((place, gain, both))
     parts, offsets, both = gather_blocks(weights.transpose(0, 2, 1), "trk", both)
     row = lax.all_to_all(both, "trk", split_axis=0, concat_axis=0, tiled=True)
     out_shape = (count, 4, cols, part)
@@ -192,21 +241,40 @@
         for k in range(groups)
         for held in parts
     ]
-    place = jnp.stack([group, track]).astype(jnp.int32)
     vmem = pl.BlockSpec(memory_space=pltpu.VMEM)
-    *wg, cells = pl.pallas_call(
-        functools.partial(row_kernel, groups, offsets),
-        out_shape=(jax.ShapeDtypeStruct(out_shape, BF),) * groups
-        + (jax.ShapeDtypeStruct((count * trk_dev, width + 2 * width // trk_dev), BF),),
-        in_specs=[pl.BlockSpec(memory_space=pltpu.SMEM)] + [vmem] * (2 + len(w_parts)),
-        out_specs=(vmem,) * (groups + 1),
-        scratch_shapes=[
-            pltpu.VMEM((4, width, width), BF),
-            pltpu.VMEM((groups, trk_dev * count, part), BF),
-            pltpu.VMEM((groups, trk_dev * count, part), BF),
-        ],
+    smem = pl.BlockSpec(memory_space=pltpu.SMEM)
+    length = trk_dev * count
+    wg_shape = jax.ShapeDtypeStruct(out_shape, BF)
+    scratch = [pltpu.VMEM((groups, length, part), BF)] * 2
+    *wg, grads, attended, w_all, gain = pl.pallas_call(
+        functools.partial(attend_kernel, groups, offsets),
+        out_shape=(wg_shape,) * (groups - 1)
+        + (
+            jax.ShapeDtypeStruct((3, length, width), BF),
+            jax.ShapeDtypeStruct((length, width), BF),
+            jax.ShapeDtypeStruct((4, width, width), BF),
+            jax.ShapeDtypeStruct((1, width), F32),
+        ),
+        in_specs=[smem] + [vmem] * (2 + len(w_parts)),
+        out_specs=(vmem,) * (groups + 3),
+        scratch_shapes=scratch,
         compiler_params=pltpu.CompilerParams(vmem_limit_bytes=48 * 2**20),
-    )(place, row, ln_gain[None], *w_parts)
+    )(place, row, gain, *w_parts)
+    own, cells = pl.pallas_call(
+        functools.partial(cells_kernel, groups),
+        out_shape=(
+            wg_shape,
+            jax.ShapeDtypeStruct((length, width + 2 * width // trk_dev), BF),
+        ),
+        in_specs=[smem] + [vmem] * 5,
+        out_specs=(vmem, vmem),
+        scratch_shapes=scratch,
+        compiler_params=pltpu.CompilerParams(vmem_limit_bytes=48 * 2**20),
+        cost_estimate=pl.CostEstimate(
+            flops=10 * length * width * width, bytes_accessed=16 * width * width, transcendentals=0
+        ),
+    )(place, row, gain, w_all, grads, attended)
+    wg = [own] + list(wg)
     if narrow:
         wg = [cut_blocks(blocks, count, track) for blocks in wg]
     back = lax.all_to_all(cells, "trk", split_axis=0, concat_axis=0, tiled=True)
@@ -221,10 +289,13 @@
         gain_sum = gain_sum + lax.ppermute(gain_sum, "grp", ring(2, 1))
     else:
         gain_sum = jnp.sum(lax.all_gather(gain_sum, "grp"), 0)
-    terms[1], terms[2], grad_fields, gain_sum = lax.optimization_barrier((terms[1], terms[2], grad_fields, gain_sum))
+    factor = float(cell_count) ** (-0.5)
+    gain_sum = gain_sum * factor
+    terms[1], terms[2], grad_fields, gain_sum = lax.optimization_barrier(
+        (terms[1], terms[2], grad_fields, gain_sum)
+    )
     total = sum(term.astype(F32) for term in terms)
-    factor = float(cell_count) ** (-0.5)
-    return (grad_fields, total.transpose(0, 2, 1) * factor, gain_sum * factor)
+    return (grad_fields, total.transpose(0, 2, 1) * factor, gain_sum)
 
 
 def solution(mesh):

time: 64.8 us -> 63.3 us (0.977)
  waiting for transfers between devices: 24.9 us -> 21.8 us
  Pallas kernels: 4.72 us -> 5.62 us
  local copies, waits for them, and re-layouts: 0.77 us -> 1.45 us
    ppermute x1, waiting for transfers between devices: 2.66 us -> 0.77 us  [shards(): total = total + lax.ppermute(wg[k], 'grp', ring(groups, k)).astype(F32)]
    ppermute x12, waiting for transfers between devices: 20.3 us -> 19 us  [swap(): lax.ppermute(array, axis, [(i, i ^ bits) for i in range(lax.axis_size(axi...]
    pallas_call x1 -> x2, Pallas kernels: 4.72 us -> 5.62 us  [the longest x1 3.74 us: shards(): pl.pallas_call(functools.partial(attend_kernel, groups, offsets), out_sha...]
    broadcast_in_dim x0 -> x1, local copies, waits for them, and re-layouts: none -> 0.68 us  [shards(): gain = jnp.broadcast_to(ln_gain, (8, width))]
  transfers between devices with their start and end apart: 20 -> 20, of which waited for: 12 -> 11; matrix products, arithmetic and copies ran while one was open for 4% -> 6% of each run, Pallas kernels for 0% -> 3%
where the time goes in v6:
time: 63.3 us; the launch traced here: 62.9 us
  starting transfers between devices  28.7 us (45%)
  waiting for transfers between devices  21.8 us (34%)
  Pallas kernels  5.62 us (9%)
  other arithmetic  4.57 us (7%)
  local copies, waits for them, and re-layouts  1.45 us (2%)
  between operations  0.74 us (1%)
    ppermute x12, waiting for transfers between devices, swap(): lax.ppermute(array, axis, [(i, i ^ bits) for i in range(lax.axis_size(axi...  19 us
    ppermute x12, starting transfers between devices, swap(): lax.ppermute(array, axis, [(i, i ^ bits) for i in range(lax.axis_size(axi...  17.3 us
    all_to_all x1, starting transfers between devices, shards(): back = lax.all_to_all(cells, 'trk', split_axis=0, concat_axis=0, tiled=True)  5.48 us
    all_to_all x1, starting transfers between devices, shards(): row = lax.all_to_all(both, 'trk', split_axis=0, concat_axis=0, tiled=True)  5.42 us
    pallas_call x1, Pallas kernels, shards(): pl.pallas_call(functools.partial(attend_kernel, groups, offsets), out_sha...  3.74 us
    pallas_call x1, Pallas kernels, shards(): pl.pallas_call(functools.partial(cells_kernel, groups), out_shape=(wg_sha...  1.88 us
    concatenate x1, other arithmetic, shards(): both = jnp.concatenate([fields, upstream], 1)  1.71 us
    all_to_all x1, waiting for transfers between devices, shards(): row = lax.all_to_all(both, 'trk', split_axis=0, concat_axis=0, tiled=True)  1.52 us
  transfers between devices with their start and end apart: 20, of which 11 were waited for; matrix products, arithmetic and copies ran while one was open for 6% of the time, Pallas kernels for 3%

profile of v6, /device:TPU:0, one launch (start us, length us, event | category | flops | bytes accessed | tf_op | source)
XLA Modules:
  0.0 62.9 jit_solution(17065685488490539212)
XLA Ops:
  0.6 5.1 %collective-permute-start.2 = (bf16[1,4,32,256]{3,2,1,0:T(8,128)(2,1)}, bf16[1,4,32,256]{3,2,1,0:T(8,128)(2,1)S(1)}, u32[]{:S(2)}, u32[]{:S(2)}) collective-permute-start(bf16[1,4,32,256]{3,2,1,0:T(8,128)(2,1)} %bitcast.31), channel_id=1, source_target_pairs={{0,12},{1,13},{2,14},{3,15},{4,8},{5,9},{6,10},{7,11},{8,4},{9,5},... | collective-permute-start | bytes 196616 | tf_op jit(solution)/shard_map/ppermute | solution.py:172
  5.7 0.0 collective-permute-start.1
  5.7 0.6 %collective-permute-start = (bf16[1,4,32,256]{3,2,1,0:T(8,128)(2,1)}, bf16[1,4,32,256]{3,2,1,0:T(8,128)(2,1)S(1)}, u32[]{:S(2)}, u32[]{:S(2)}) collective-permute-start(bf16[1,4,32,256]{3,2,1,0:T(8,128)(2,1)} %bitcast.33), channel_id=1, source_target_pairs={{0,8},{1,9},{2,10},{3,11},{4,12},{5,13},{6,14},{7,15},{8,0},{9,1},... | collective-permute-start | bytes 196616 | tf_op jit(solution)/shard_map/ppermute | solution.py:172
  6.4 1.7 %pad_maximum_fusion = bf16[16,16,512]{2,1,0:T(8,128)(2,1)} fusion(bf16[16,8,512]{2,1,0:T(8,128)(2,1)} %param.5, bf16[16,8,512]{2,1,0:T(8,128)(2,1)} %param.4), kind=kLoop, calls=%fused_computation.2 | loop fusion | flops 524288 | bytes 524288 | tf_op jit(solution)/shard_map/concatenate | solution.py:228
  8.1 0.1 pad_add_fusion.place
  8.2 0.7 %broadcast_in_dim.6.gain_ref = f32[8,512]{1,0:T(8,128)S(1)} broadcast(f32[512]{0:T(512)} %param.6), dimensions={1} | broadcast | bytes 18432 | tf_op jit(solution)/shard_map/broadcast_in_dim | solution.py:229
  8.9 2.7 %collective-permute-done = bf16[1,4,32,256]{3,2,1,0:T(8,128)(2,1)S(1)} collective-permute-done((bf16[1,4,32,256]{3,2,1,0:T(8,128)(2,1)}, bf16[1,4,32,256]{3,2,1,0:T(8,128)(2,1)S(1)}, u32[]{:S(2)}, u32[]{:S(2)}) %collective-permute-start) | collective-permute-done | bytes 65568 | tf_op jit(solution)/shard_map/ppermute | solution.py:172
  11.6 0.0 collective-permute-done.2
  11.6 0.0 collective-permute-done.1
  11.6 0.9 %pad_maximum_fusion.1.refs_0_ = bf16[4,4,32,256]{3,2,1,0:T(8,128)(2,1)S(1)} fusion(bf16[1,4,32,256]{3,2,1,0:T(8,128)(2,1)S(1)} %collective-permute-done.2, bf16[1,4,32,256]{3,2,1,0:T(8,128)(2,1)S(1)} %collective-permute-done.1, bf16[1,4,32,256]{3,2,1,0:T(8,128)(2,1)S(1)} %collective-permute-done, bf16[1,4,32,256]{3,2,1,0:T(8,128)(2,1)} %bitcast.34), kind=kLoop, calls=%fused_computation.3 | loop fusion | flops 393216 | bytes 524288 | tf_op jit(solution)/shard_map/concatenate | solution.py:202
  12.5 2.5 %collective-permute-start.5 = (bf16[4,4,32,256]{3,2,1,0:T(8,128)(2,1)S(1)}, bf16[4,4,32,256]{3,2,1,0:T(8,128)(2,1)S(1)}, u32[]{:S(2)}, u32[]{:S(2)}) collective-permute-start(bf16[4,4,32,256]{3,2,1,0:T(8,128)(2,1)S(1)} %pad_maximum_fusion.1.refs_0_), channel_id=1, source_target_pairs={{0,3},{1,2},{2,1},{3,0},{4,7},{5,6},{6,5},{7,4},{8,11},{9,10},{10,... | collective-permute-start | bytes 786440 | tf_op jit(solution)/shard_map/ppermute | solution.py:172
  15.0 0.5 collective-permute-start.4
  15.5 0.5 collective-permute-start.3
  16.0 5.4 %all-to-all-start = ((bf16[16,16,512]{2,1,0:T(8,128)(2,1)}), bf16[16,16,512]{2,1,0:T(8,128)(2,1)S(1)}, u32[]{:S(2)}, u32[]{:S(2)}) async-start(bf16[16,16,512]{2,1,0:T(8,128)(2,1)} %pad_maximum_fusion), calls=%async_computation | async-start | bytes 524288 | tf_op jit(solution)/shard_map/all_to_all | solution.py:233
  21.5 0.1 collective-permute-start.6
  21.5 1.2 %collective-permute-done.5.refs_3_ = bf16[4,4,32,256]{3,2,1,0:T(8,128)(2,1)S(1)} collective-permute-done((bf16[4,4,32,256]{3,2,1,0:T(8,128)(2,1)S(1)}, bf16[4,4,32,256]{3,2,1,0:T(8,128)(2,1)S(1)}, u32[]{:S(2)}, u32[]{:S(2)}) %collective-permute-start.5) | collective-permute-done | bytes 262176 | tf_op jit(solution)/shard_map/ppermute | solution.py:172
  22.7 0.0 collective-permute-start.9
  22.7 5.2 %collective-permute-done.4.refs_2_ = bf16[4,4,32,256]{3,2,1,0:T(8,128)(2,1)S(1)} collective-permute-done((bf16[4,4,32,256]{3,2,1,0:T(8,128)(2,1)S(1)}, bf16[4,4,32,256]{3,2,1,0:T(8,128)(2,1)S(1)}, u32[]{:S(2)}, u32[]{:S(2)}) %collective-permute-start.4) | collective-permute-done | bytes 262176 | tf_op jit(solution)/shard_map/ppermute | solution.py:172
  27.9 0.0 collective-permute-start.8
  27.9 0.2 collective-permute-done.3.refs_1_
  28.2 0.3 collective-permute-start.7
  28.4 0.0 collective-permute-done.6.refs_4_
  28.4 1.5 %all-to-all-done.rows_ref = bf16[16,16,512]{2,1,0:T(8,128)(2,1)S(1)} async-done(((bf16[16,16,512]{2,1,0:T(8,128)(2,1)}), bf16[16,16,512]{2,1,0:T(8,128)(2,1)S(1)}, u32[]{:S(2)}, u32[]{:S(2)}) %all-to-all-start) | async-done | bytes 262176 | tf_op jit(solution)/shard_map/all_to_all | solution.py:233
  30.0 0.0 collective-permute-done.9.refs_7_
  30.0 0.0 collective-permute-done.8.refs_6_
  30.0 0.0 collective-permute-done.7.refs_5_
  30.0 3.7 %shard_map.67 = (bf16[16,4,32,256]{3,2,1,0:T(8,128)(2,1)S(1)}, bf16[3,128,512]{2,1,0:T(8,128)(2,1)S(1)}, bf16[128,512]{1,0:T(8,128)(2,1)S(1)}, bf16[4,512,512]{2,1,0:T(8,128)(2,1)S(1)}, f32[1,512]{1,0:T(1,128)S(1)}) custom-call(s32[2]{0:T(128)S(1)} %pad_add_fusion.place, bf16[16,16,512]{2,1,0:T(8,128)(2,1)S(1)} %all-to-all-done.rows_ref, ...), custom_call_target="tpu_custom_call" | custom-call | tf_op jit(solution)/shard_map/pallas_call | solution.py:249
  33.7 0.1 collective-permute-start.10
  33.8 1.9 %shard_map.68 = (bf16[16,4,32,256]{3,2,1,0:T(8,128)(2,1)S(1)}, bf16[128,640]{1,0:T(8,128)(2,1)}) custom-call(s32[2]{0:T(128)S(1)} %pad_add_fusion.place, bf16[16,16,512]{2,1,0:T(8,128)(2,1)S(1)} %all-to-all-done.rows_ref, f32[1,512]{1,0:T(1,128)S(1)} %get-tuple-element.26.gain_ref, bf16[4,512,512]{2,1,0:T(8,128)(2,1)S(1)} %get-tuple-element.27.w_all, ...), custom_call_target="tpu_custom_call" | custom-call | flops 335544320 | bytes 4194304 | tf_op jit(solution)/shard_map/pallas_call | solution.py:263
  35.7 0.8 %collective-permute-done.10 = bf16[16,4,32,256]{3,2,1,0:T(8,128)(2,1)S(1)} collective-permute-done((bf16[16,4,32,256]{3,2,1,0:T(8,128)(2,1)S(1)}, bf16[16,4,32,256]{3,2,1,0:T(8,128)(2,1)S(1)}, u32[]{:S(2)}, u32[]{:S(2)}) %collective-permute-start.10) | collective-permute-done | bytes 1048608 | tf_op jit(solution)/shard_map/ppermute | solution.py:283
  36.5 0.4 add_convert_fusion
  36.9 0.1 fusion.6
  36.9 1.7 %collective-permute-start.11 = (bf16[4,4,32,256]{3,2,1,0:T(8,128)(2,1)S(1)}, bf16[4,4,32,256]{3,2,1,0:T(8,128)(2,1)S(1)}, u32[]{:S(2)}, u32[]{:S(2)}) collective-permute-start(bf16[4,4,32,256]{3,2,1,0:T(8,128)(2,1)S(1)} %get-tuple-element.41), channel_id=1, source_target_pairs={{0,1},{1,0},{2,3},{3,2},{4,5},{5,4},{6,7},{7,6},{8,9},{9,8},{10,11... | collective-permute-start | bytes 786440 | tf_op jit(solution)/shard_map/ppermute | solution.py:172
  38.6 0.7 %collective-permute-start.13 = (bf16[4,4,32,256]{3,2,1,0:T(8,128)(2,1)S(1)}, bf16[4,4,32,256]{3,2,1,0:T(8,128)(2,1)S(1)}, u32[]{:S(2)}, u32[]{:S(2)}) collective-permute-start(bf16[4,4,32,256]{3,2,1,0:T(8,128)(2,1)S(1)} %get-tuple-element.42), channel_id=1, source_target_pairs={{0,2},{1,3},{2,0},{3,1},{4,6},{5,7},{6,4},{7,5},{8,10},{9,11},{10,... | collective-permute-start | bytes 786440 | tf_op jit(solution)/shard_map/ppermute | solution.py:172
  39.4 1.1 %collective-permute-start.12 = (bf16[4,4,32,256]{3,2,1,0:T(8,128)(2,1)S(1)}, bf16[4,4,32,256]{3,2,1,0:T(8,128)(2,1)S(1)}, u32[]{:S(2)}, u32[]{:S(2)}) collective-permute-start(bf16[4,4,32,256]{3,2,1,0:T(8,128)(2,1)S(1)} %get-tuple-element.43), channel_id=1, source_target_pairs={{0,3},{1,2},{2,1},{3,0},{4,7},{5,6},{6,5},{7,4},{8,11},{9,10},{10,... | collective-permute-start | bytes 786440 | tf_op jit(solution)/shard_map/ppermute | solution.py:172
  40.5 5.5 %all-to-all-start.1 = ((bf16[16,8,640]{2,1,0:T(8,128)(2,1)}), bf16[16,8,640]{2,1,0:T(8,128)(2,1)S(1)}, u32[]{:S(2)}, u32[]{:S(2)}) async-start(bf16[16,8,640]{2,1,0:T(8,128)(2,1)} %bitcast.8), calls=%async_computation.1 | async-start | bytes 327680 | tf_op jit(solution)/shard_map/all_to_all | solution.py:280
  46.0 0.2 collective-permute-done.11
  46.2 6.6 %collective-permute-done.13 = bf16[4,4,32,256]{3,2,1,0:T(8,128)(2,1)S(1)} collective-permute-done((bf16[4,4,32,256]{3,2,1,0:T(8,128)(2,1)S(1)}, bf16[4,4,32,256]{3,2,1,0:T(8,128)(2,1)S(1)}, u32[]{:S(2)}, u32[]{:S(2)}) %collective-permute-start.13) | collective-permute-done | bytes 262176 | tf_op jit(solution)/shard_map/ppermute | solution.py:172
  52.8 1.0 %collective-permute-done.12 = bf16[4,4,32,256]{3,2,1,0:T(8,128)(2,1)S(1)} collective-permute-done((bf16[4,4,32,256]{3,2,1,0:T(8,128)(2,1)S(1)}, bf16[4,4,32,256]{3,2,1,0:T(8,128)(2,1)S(1)}, u32[]{:S(2)}, u32[]{:S(2)}) %collective-permute-start.12) | collective-permute-done | bytes 262176 | tf_op jit(solution)/shard_map/ppermute | solution.py:172
  53.8 0.2 fusion.5
  54.0 2.8 %collective-permute-start.16 = (bf16[4,32,256]{2,1,0:T(8,128)(2,1)S(1)}, bf16[4,32,256]{2,1,0:T(8,128)(2,1)S(1)}, u32[]{:S(2)}, u32[]{:S(2)}) collective-permute-start(bf16[4,32,256]{2,1,0:T(8,128)(2,1)S(1)} %get-tuple-element.44), channel_id=1, source_target_pairs={{0,12},{1,13},{2,14},{3,15},{4,8},{5,9},{6,10},{7,11},{8,4},{9,5},... | collective-permute-start | bytes 196616 | tf_op jit(solution)/shard_map/ppermute | solution.py:172
  56.8 0.0 collective-permute-start.15
  56.8 1.6 %collective-permute-start.14 = (bf16[4,32,256]{2,1,0:T(8,128)(2,1)S(1)}, bf16[4,32,256]{2,1,0:T(8,128)(2,1)S(1)}, u32[]{:S(2)}, u32[]{:S(2)}) collective-permute-start(bf16[4,32,256]{2,1,0:T(8,128)(2,1)S(1)} %get-tuple-element.46), channel_id=1, source_target_pairs={{0,8},{1,9},{2,10},{3,11},{4,12},{5,13},{6,14},{7,15},{8,0},{9,1},... | collective-permute-start | bytes 196616 | tf_op jit(solution)/shard_map/ppermute | solution.py:172
  58.5 0.0 all-to-all-done.1
  58.5 1.8 %collective-permute-done.16 = bf16[4,32,256]{2,1,0:T(8,128)(2,1)S(1)} collective-permute-done((bf16[4,32,256]{2,1,0:T(8,128)(2,1)S(1)}, bf16[4,32,256]{2,1,0:T(8,128)(2,1)S(1)}, u32[]{:S(2)}, u32[]{:S(2)}) %collective-permute-start.16) | collective-permute-done | bytes 65568 | tf_op jit(solution)/shard_map/ppermute | solution.py:172
  60.3 0.1 collective-permute-start.17
  60.4 0.7 %slice_bitcast_fusion.1 = bf16[16,8,512]{2,1,0:T(8,128)(2,1)} fusion(bf16[128,640]{1,0:T(8,128)(2,1)S(1)} %bitcast.30), kind=kLoop, calls=%fused_computation.10 | loop fusion | bytes 262144 | tf_op jit(solution)/shard_map/reshape | solution.py:286
  61.1 0.5 collective-permute-done.17
  61.6 0.6 add_multiply_fusion
  62.1 0.0 collective-permute-done.15
  62.1 0.0 collective-permute-done.14
  62.2 0.7 %fusion.4 = f32[4,256,32]{1,2,0:T(8,128)} fusion(f32[4,4,32,256]{3,2,1,0:T(8,128)S(1)} %get-tuple-element.40, bf16[4,32,256]{2,1,0:T(8,128)(2,1)S(1)} %collective-permute-done.16, bf16[4,32,256]{2,1,0:T(8,128)(2,1)S(1)} %collective-permute-done.15, bf16[4,32,256]{2,1,0:T(8,128)(2,1)S(1)} %collective-permute-done.14), kind=kLoop, calls=%fused_computation.9 | loop fusion | flops 229376 | bytes 458752 | tf_op jit(solution)/shard_map/mul | solution.py:298
  (4 shorter events, 0.1 us)
Async XLA Ops:
  0.6 11.0 %collective-permute-start.2 = (bf16[1,4,32,256]{3,2,1,0:T(8,128)(2,1)}, bf16[1,4,32,256]{3,2,1,0:T(8,128)(2,1)S(1)}, u32[]{:S(2)}, u32[]{:S(2)}) collective-permute-start(bf16[1,4,32,256]{3,2,1,0:T(8,128)(2,1)} %bitcast.31), channel_id=1, source_target_pairs={{0,12},{1,13},{2,14},{3,15},{4,8},{5,9},{6,10},{7,11},{8,4},{9,5},... | collective-permute-start | bytes 196616 | tf_op jit(solution)/shard_map/ppermute | solution.py:172
  5.7 5.9 %collective-permute-start.1 = (bf16[1,4,32,256]{3,2,1,0:T(8,128)(2,1)}, bf16[1,4,32,256]{3,2,1,0:T(8,128)(2,1)S(1)}, u32[]{:S(2)}, u32[]{:S(2)}) collective-permute-start(bf16[1,4,32,256]{3,2,1,0:T(8,128)(2,1)} %bitcast.32), channel_id=1, source_target_pairs={{0,4},{1,5},{2,6},{3,7},{4,0},{5,1},{6,2},{7,3},{8,12},{9,13},{10,... | collective-permute-start | bytes 196616 | tf_op jit(solution)/shard_map/ppermute | solution.py:172
  5.7 5.8 %collective-permute-start = (bf16[1,4,32,256]{3,2,1,0:T(8,128)(2,1)}, bf16[1,4,32,256]{3,2,1,0:T(8,128)(2,1)S(1)}, u32[]{:S(2)}, u32[]{:S(2)}) collective-permute-start(bf16[1,4,32,256]{3,2,1,0:T(8,128)(2,1)} %bitcast.33), channel_id=1, source_target_pairs={{0,8},{1,9},{2,10},{3,11},{4,12},{5,13},{6,14},{7,15},{8,0},{9,1},... | collective-permute-start | bytes 196616 | tf_op jit(solution)/shard_map/ppermute | solution.py:172
  12.5 10.2 %collective-permute-start.5 = (bf16[4,4,32,256]{3,2,1,0:T(8,128)(2,1)S(1)}, bf16[4,4,32,256]{3,2,1,0:T(8,128)(2,1)S(1)}, u32[]{:S(2)}, u32[]{:S(2)}) collective-permute-start(bf16[4,4,32,256]{3,2,1,0:T(8,128)(2,1)S(1)} %pad_maximum_fusion.1.refs_0_), channel_id=1, source_target_pairs={{0,3},{1,2},{2,1},{3,0},{4,7},{5,6},{6,5},{7,4},{8,11},{9,10},{10,... | collective-permute-start | bytes 786440 | tf_op jit(solution)/shard_map/ppermute | solution.py:172
  15.0 12.9 %collective-permute-start.4 = (bf16[4,4,32,256]{3,2,1,0:T(8,128)(2,1)S(1)}, bf16[4,4,32,256]{3,2,1,0:T(8,128)(2,1)S(1)}, u32[]{:S(2)}, u32[]{:S(2)}) collective-permute-start(bf16[4,4,32,256]{3,2,1,0:T(8,128)(2,1)S(1)} %pad_maximum_fusion.1.refs_0_), channel_id=1, source_target_pairs={{0,2},{1,3},{2,0},{3,1},{4,6},{5,7},{6,4},{7,5},{8,10},{9,11},{10,... | collective-permute-start | bytes 786440 | tf_op jit(solution)/shard_map/ppermute | solution.py:172
  15.5 12.7 %collective-permute-start.3 = (bf16[4,4,32,256]{3,2,1,0:T(8,128)(2,1)S(1)}, bf16[4,4,32,256]{3,2,1,0:T(8,128)(2,1)S(1)}, u32[]{:S(2)}, u32[]{:S(2)}) collective-permute-start(bf16[4,4,32,256]{3,2,1,0:T(8,128)(2,1)S(1)} %pad_maximum_fusion.1.refs_0_), channel_id=1, source_target_pairs={{0,1},{1,0},{2,3},{3,2},{4,5},{5,4},{6,7},{7,6},{8,9},{9,8},{10,11... | collective-permute-start | bytes 786440 | tf_op jit(solution)/shard_map/ppermute | solution.py:172
  16.0 13.9 %all-to-all-start = ((bf16[16,16,512]{2,1,0:T(8,128)(2,1)}), bf16[16,16,512]{2,1,0:T(8,128)(2,1)S(1)}, u32[]{:S(2)}, u32[]{:S(2)}) async-start(bf16[16,16,512]{2,1,0:T(8,128)(2,1)} %pad_maximum_fusion), calls=%async_computation | async-start | bytes 524288 | tf_op jit(solution)/shard_map/all_to_all | solution.py:233
  21.5 7.0 %collective-permute-start.6 = (bf16[4,4,32,256]{3,2,1,0:T(8,128)(2,1)S(1)}, bf16[4,4,32,256]{3,2,1,0:T(8,128)(2,1)S(1)}, u32[]{:S(2)}, u32[]{:S(2)}) collective-permute-start(bf16[4,4,32,256]{3,2,1,0:T(8,128)(2,1)S(1)} %pad_maximum_fusion.1.refs_0_), channel_id=1, source_target_pairs={{0,16},{16,0},{1,17},{17,1},{2,18},{18,2},{3,19},{19,3},{4,20},{20... | collective-permute-start | bytes 786440 | tf_op jit(solution)/shard_map/ppermute | solution.py:240
  22.7 7.3 %collective-permute-start.9 = (bf16[4,4,32,256]{3,2,1,0:T(8,128)(2,1)S(1)}, bf16[4,4,32,256]{3,2,1,0:T(8,128)(2,1)S(1)}, u32[]{:S(2)}, u32[]{:S(2)}) collective-permute-start(bf16[4,4,32,256]{3,2,1,0:T(8,128)(2,1)S(1)} %collective-permute-done.5.refs_3_), channel_id=1, source_target_pairs={{0,16},{16,0},{1,17},{17,1},{2,18},{18,2},{3,19},{19,3},{4,20},{20... | collective-permute-start | bytes 786440 | tf_op jit(solution)/shard_map/ppermute | solution.py:240
  27.9 2.0 %collective-permute-start.8 = (bf16[4,4,32,256]{3,2,1,0:T(8,128)(2,1)S(1)}, bf16[4,4,32,256]{3,2,1,0:T(8,128)(2,1)S(1)}, u32[]{:S(2)}, u32[]{:S(2)}) collective-permute-start(bf16[4,4,32,256]{3,2,1,0:T(8,128)(2,1)S(1)} %collective-permute-done.4.refs_2_), channel_id=1, source_target_pairs={{0,16},{16,0},{1,17},{17,1},{2,18},{18,2},{3,19},{19,3},{4,20},{20... | collective-permute-start | bytes 786440 | tf_op jit(solution)/shard_map/ppermute | solution.py:240
  28.2 1.8 %collective-permute-start.7 = (bf16[4,4,32,256]{3,2,1,0:T(8,128)(2,1)S(1)}, bf16[4,4,32,256]{3,2,1,0:T(8,128)(2,1)S(1)}, u32[]{:S(2)}, u32[]{:S(2)}) collective-permute-start(bf16[4,4,32,256]{3,2,1,0:T(8,128)(2,1)S(1)} %collective-permute-done.3.refs_1_), channel_id=1, source_target_pairs={{0,16},{16,0},{1,17},{17,1},{2,18},{18,2},{3,19},{19,3},{4,20},{20... | collective-permute-start | bytes 786440 | tf_op jit(solution)/shard_map/ppermute | solution.py:240
  33.7 2.7 %collective-permute-start.10 = (bf16[16,4,32,256]{3,2,1,0:T(8,128)(2,1)S(1)}, bf16[16,4,32,256]{3,2,1,0:T(8,128)(2,1)S(1)}, u32[]{:S(2)}, u32[]{:S(2)}) collective-permute-start(bf16[16,4,32,256]{3,2,1,0:T(8,128)(2,1)S(1)} %get-tuple-element.31), channel_id=1, source_target_pairs={{0,16},{16,0},{1,17},{17,1},{2,18},{18,2},{3,19},{19,3},{4,20},{20... | collective-permute-start | bytes 3145736 | tf_op jit(solution)/shard_map/ppermute | solution.py:283
  36.9 9.2 %collective-permute-start.11 = (bf16[4,4,32,256]{3,2,1,0:T(8,128)(2,1)S(1)}, bf16[4,4,32,256]{3,2,1,0:T(8,128)(2,1)S(1)}, u32[]{:S(2)}, u32[]{:S(2)}) collective-permute-start(bf16[4,4,32,256]{3,2,1,0:T(8,128)(2,1)S(1)} %get-tuple-element.41), channel_id=1, source_target_pairs={{0,1},{1,0},{2,3},{3,2},{4,5},{5,4},{6,7},{7,6},{8,9},{9,8},{10,11... | collective-permute-start | bytes 786440 | tf_op jit(solution)/shard_map/ppermute | solution.py:172
  38.6 14.2 %collective-permute-start.13 = (bf16[4,4,32,256]{3,2,1,0:T(8,128)(2,1)S(1)}, bf16[4,4,32,256]{3,2,1,0:T(8,128)(2,1)S(1)}, u32[]{:S(2)}, u32[]{:S(2)}) collective-permute-start(bf16[4,4,32,256]{3,2,1,0:T(8,128)(2,1)S(1)} %get-tuple-element.42), channel_id=1, source_target_pairs={{0,2},{1,3},{2,0},{3,1},{4,6},{5,7},{6,4},{7,5},{8,10},{9,11},{10,... | collective-permute-start | bytes 786440 | tf_op jit(solution)/shard_map/ppermute | solution.py:172
  39.4 14.4 %collective-permute-start.12 = (bf16[4,4,32,256]{3,2,1,0:T(8,128)(2,1)S(1)}, bf16[4,4,32,256]{3,2,1,0:T(8,128)(2,1)S(1)}, u32[]{:S(2)}, u32[]{:S(2)}) collective-permute-start(bf16[4,4,32,256]{3,2,1,0:T(8,128)(2,1)S(1)} %get-tuple-element.43), channel_id=1, source_target_pairs={{0,3},{1,2},{2,1},{3,0},{4,7},{5,6},{6,5},{7,4},{8,11},{9,10},{10,... | collective-permute-start | bytes 786440 | tf_op jit(solution)/shard_map/ppermute | solution.py:172
  40.5 18.0 %all-to-all-start.1 = ((bf16[16,8,640]{2,1,0:T(8,128)(2,1)}), bf16[16,8,640]{2,1,0:T(8,128)(2,1)S(1)}, u32[]{:S(2)}, u32[]{:S(2)}) async-start(bf16[16,8,640]{2,1,0:T(8,128)(2,1)} %bitcast.8), calls=%async_computation.1 | async-start | bytes 327680 | tf_op jit(solution)/shard_map/all_to_all | solution.py:280
  54.0 6.2 %collective-permute-start.16 = (bf16[4,32,256]{2,1,0:T(8,128)(2,1)S(1)}, bf16[4,32,256]{2,1,0:T(8,128)(2,1)S(1)}, u32[]{:S(2)}, u32[]{:S(2)}) collective-permute-start(bf16[4,32,256]{2,1,0:T(8,128)(2,1)S(1)} %get-tuple-element.44), channel_id=1, source_target_pairs={{0,12},{1,13},{2,14},{3,15},{4,8},{5,9},{6,10},{7,11},{8,4},{9,5},... | collective-permute-start | bytes 196616 | tf_op jit(solution)/shard_map/ppermute | solution.py:172
  56.8 5.3 %collective-permute-start.15 = (bf16[4,32,256]{2,1,0:T(8,128)(2,1)S(1)}, bf16[4,32,256]{2,1,0:T(8,128)(2,1)S(1)}, u32[]{:S(2)}, u32[]{:S(2)}) collective-permute-start(bf16[4,32,256]{2,1,0:T(8,128)(2,1)S(1)} %get-tuple-element.45), channel_id=1, source_target_pairs={{0,4},{1,5},{2,6},{3,7},{4,0},{5,1},{6,2},{7,3},{8,12},{9,13},{10,... | collective-permute-start | bytes 196616 | tf_op jit(solution)/shard_map/ppermute | solution.py:172
  56.8 5.3 %collective-permute-start.14 = (bf16[4,32,256]{2,1,0:T(8,128)(2,1)S(1)}, bf16[4,32,256]{2,1,0:T(8,128)(2,1)S(1)}, u32[]{:S(2)}, u32[]{:S(2)}) collective-permute-start(bf16[4,32,256]{2,1,0:T(8,128)(2,1)S(1)} %get-tuple-element.46), channel_id=1, source_target_pairs={{0,8},{1,9},{2,10},{3,11},{4,12},{5,13},{6,14},{7,15},{8,0},{9,1},... | collective-permute-start | bytes 196616 | tf_op jit(solution)/shard_map/ppermute | solution.py:172
  60.3 1.2 %collective-permute-start.17 = (f32[512]{0:T(512)S(1)}, f32[512]{0:T(512)S(1)}, u32[]{:S(2)}, u32[]{:S(2)}) collective-permute-start(f32[512]{0:T(512)S(1)} %reduce_sum.9), channel_id=1, source_target_pairs={{0,16},{16,0},{1,17},{17,1},{2,18},{18,2},{3,19},{19,3},{4,20},{20... | collective-permute-start | bytes 6152 | tf_op jit(solution)/shard_map/ppermute | solution.py:289

commit v7 on v6

--- a/solution.py
+++ b/solution.py
@@ -91,28 +91,33 @@
     span = 2 * size
     lane = lax.broadcasted_iota(jnp.int32, (length, span), 1)
     first = lane < size
-    pieces = [[], [], [], []]
-    for at in range(0, width, span):
-        query, keyed, valued = [member[:, at : at + span] for member in projected]
-        grad_out = grad_att[:, at : at + span]
-        zero = jnp.zeros_like(query)
-        query2 = jnp.concatenate([jnp.where(first, query, zero), jnp.where(first, zero, query)], 0)
-        grad2 = jnp.concatenate(
-            [jnp.where(first, grad_out, zero), jnp.where(first, zero, grad_out)], 0
-        )
-        scores = dot(query2, keyed, ((1,), (1,))) * scaling
-        shifted = jnp.exp(scores - jnp.max(scores, -1, keepdims=True))
-        prob = shifted / jnp.sum(shifted, -1, keepdims=True)
-        prob_low = prob.astype(BF)
-        dprobs = dot(grad2, valued, ((1,), (1,)))
-        row_dot = jnp.sum(prob * dprobs, -1, keepdims=True)
-        score_grad = (prob * (dprobs - row_dot) * scaling).astype(BF)
-        out2 = dot(prob_low, valued, ((1,), (0,)))
-        gq2 = dot(score_grad, keyed, ((1,), (0,)))
-        pieces[0].append(jnp.where(first, gq2[:length], gq2[length:]).astype(BF))
-        pieces[1].append(dot(score_grad, query2, ((0,), (0,))).astype(BF))
-        pieces[2].append(dot(prob_low, grad2, ((0,), (0,))).astype(BF))
-        pieces[3].append(jnp.where(first, out2[:length], out2[length:]).astype(BF))
+    spans = [slice(at, at + span) for at in range(0, width, span)]
+    query, keyed, valued = [[member[:, at] for at in spans] for member in projected]
+    grad_out = [grad_att[:, at] for at in spans]
+    zero = jnp.zeros((length, span), BF)
+
+    def apart(member):
+        return jnp.concatenate([jnp.where(first, member, zero), jnp.where(first, zero, member)], 0)
+
+    def together(member):
+        return jnp.where(first, member[:length], member[length:]).astype(BF)
+
+    query2, grad2 = [apart(m) for m in query], [apart(m) for m in grad_out]
+    scores = [dot(k, q, ((1,), (1,))) * scaling for k, q in zip(keyed, query2)]
+    dprobs = [dot(v, g, ((1,), (1,))) for v, g in zip(valued, grad2)]
+    shifted = [jnp.exp(s - jnp.max(s, 0, keepdims=True)) for s in scores]
+    prob = [s * (1.0 / jnp.sum(s, 0, keepdims=True)) for s in shifted]
+    prob_low = [p.astype(BF) for p in prob]
+    row_dot = [jnp.sum(p * d, 0, keepdims=True) for p, d in zip(prob, dprobs)]
+    score_grad = [
+        (p * (d - r) * scaling).astype(BF) for p, d, r in zip(prob, dprobs, row_dot)
+    ]
+    pieces = [
+        [together(dot(s, k, ((0,), (0,)))) for s, k in zip(score_grad, keyed)],
+        [dot(s, q, ((1,), (0,))).astype(BF) for s, q in zip(score_grad, query2)],
+        [dot(p, g, ((1,), (0,))).astype(BF) for p, g in zip(prob_low, grad2)],
+        [together(dot(p, v, ((0,), (0,)))) for p, v in zip(prob_low, valued)],
+    ]
     grads = [jnp.concatenate(piece, 1) for piece in pieces[:3]]
     attended = jnp.concatenate(pieces[3], 1)
     for step in range(1, groups):
@@ -189,6 +194,24 @@
     return jnp.take(blocks, track ^ jnp.array(order), axis=0)
 
 
+def stack_blocks(parts):
+    def kernel(*refs):
+        at = 0
+        for ref in refs[:-1]:
+            refs[-1][at : at + ref.shape[0]] = ref[...]
+            at += ref.shape[0]
+
+    vmem = pl.BlockSpec(memory_space=pltpu.VMEM)
+    shape = (sum(part.shape[0] for part in parts),) + parts[0].shape[1:]
+    return pl.pallas_call(
+        kernel,
+        out_shape=jax.ShapeDtypeStruct(shape, BF),
+        in_specs=[vmem] * len(parts),
+        out_specs=vmem,
+        compiler_params=pltpu.CompilerParams(vmem_limit_bytes=16 * 2**20),
+    )(*parts)
+
+
 def gather_blocks(block, axis, other):
     count = lax.axis_size(axis)
     held, order, bit = block[None], [0], count // 2
@@ -198,8 +221,9 @@
         bit //= 2
     far = [bits for bits in (8, 4, 12) if bits < 2 * bit]
     moved = [swap(held, axis, bits) for bits in far]
+    held, other = lax.optimization_barrier((stack_blocks([held]), other))
     moved[0], other = lax.optimization_barrier((moved[0], other))
-    held = jnp.concatenate([held] + moved)
+    held = stack_blocks([held] + moved)
     order = order + [offset ^ bits for bits in far for offset in order]
     parts = [swap(held, axis, bits) if bits else held for bits in range(4)]
     return parts, [[offset ^ bits for offset in order] for bits in range(4)], other

time: 63.3 us -> 61.2 us (0.967)
  Pallas kernels: 5.62 us -> 4.41 us
  waiting for transfers between devices: 21.8 us -> 20.9 us
  other arithmetic: 4.57 us -> 3.69 us
  local copies, waits for them, and re-layouts: 1.45 us -> 2.32 us
    pallas_call x1, Pallas kernels: 3.74 us -> 2.51 us  [shards(): pl.pallas_call(functools.partial(attend_kernel, groups, offsets), out_sha...]
    concatenate x1 -> x0, other arithmetic: 0.88 us -> none  [gather_blocks(): held = jnp.concatenate([held] + moved)]
    ppermute x12, waiting for transfers between devices: 19 us -> 18.1 us  [swap(): lax.ppermute(array, axis, [(i, i ^ bits) for i in range(lax.axis_size(axi...]
    unnamed x0 -> x2, local copies, waits for them, and re-layouts: none -> 0.87 us
  transfers between devices with their start and end apart: 20 -> 20, of which waited for: 11 -> 12; matrix products, arithmetic and copies ran while one was open for 6% -> 7% of each run, Pallas kernels for 3% -> 3%
where the time goes in v7:
time: 61.2 us; the launch traced here: 60.8 us
  starting transfers between devices  28.7 us (47%)
  waiting for transfers between devices  20.9 us (34%)
  Pallas kernels  4.41 us (7%)
  other arithmetic  3.69 us (6%)
  local copies, waits for them, and re-layouts  2.32 us (4%)
  between operations  0.74 us (1%)
    ppermute x12, waiting for transfers between devices, swap(): lax.ppermute(array, axis, [(i, i ^ bits) for i in range(lax.axis_size(axi...  18.1 us
    ppermute x12, starting transfers between devices, swap(): lax.ppermute(array, axis, [(i, i ^ bits) for i in range(lax.axis_size(axi...  17.3 us
    all_to_all x1, starting transfers between devices, shards(): back = lax.all_to_all(cells, 'trk', split_axis=0, concat_axis=0, tiled=True)  5.49 us
    all_to_all x1, starting transfers between devices, shards(): row = lax.all_to_all(both, 'trk', split_axis=0, concat_axis=0, tiled=True)  5.42 us
    pallas_call x1, Pallas kernels, shards(): pl.pallas_call(functools.partial(attend_kernel, groups, offsets), out_sha...  2.51 us
    pallas_call x1, Pallas kernels, shards(): pl.pallas_call(functools.partial(cells_kernel, groups), out_shape=(wg_sha...  1.88 us
    concatenate x1, other arithmetic, shards(): both = jnp.concatenate([fields, upstream], 1)  1.7 us
    all_to_all x1, waiting for transfers between devices, shards(): row = lax.all_to_all(both, 'trk', split_axis=0, concat_axis=0, tiled=True)  1.52 us
  transfers between devices with their start and end apart: 20, of which 12 were waited for; matrix products, arithmetic and copies ran while one was open for 7% of the time, Pallas kernels for 3%

profile of v7, /device:TPU:0, one launch (start us, length us, event | category | flops | bytes accessed | tf_op | source)
XLA Modules:
  0.0 60.8 jit_solution(15520597596323035616)
XLA Ops:
  0.6 5.1 %collective-permute-start.2 = (bf16[1,4,32,256]{3,2,1,0:T(8,128)(2,1)}, bf16[1,4,32,256]{3,2,1,0:T(8,128)(2,1)S(1)}, u32[]{:S(2)}, u32[]{:S(2)}) collective-permute-start(bf16[1,4,32,256]{3,2,1,0:T(8,128)(2,1)} %bitcast.29), channel_id=1, source_target_pairs={{0,12},{1,13},{2,14},{3,15},{4,8},{5,9},{6,10},{7,11},{8,4},{9,5},... | collective-permute-start | bytes 196616 | tf_op jit(solution)/shard_map/ppermute | solution.py:177
  5.7 0.0 collective-permute-start.1
  5.7 0.6 %collective-permute-start = (bf16[1,4,32,256]{3,2,1,0:T(8,128)(2,1)}, bf16[1,4,32,256]{3,2,1,0:T(8,128)(2,1)S(1)}, u32[]{:S(2)}, u32[]{:S(2)}) collective-permute-start(bf16[1,4,32,256]{3,2,1,0:T(8,128)(2,1)} %bitcast.31), channel_id=1, source_target_pairs={{0,8},{1,9},{2,10},{3,11},{4,12},{5,13},{6,14},{7,15},{8,0},{9,1},... | collective-permute-start | bytes 196616 | tf_op jit(solution)/shard_map/ppermute | solution.py:177
  6.4 0.0 copy-start
  6.4 0.9 %copy-done = bf16[4,256,32]{1,2,0:T(8,128)(2,1)S(1)} copy-done((bf16[4,256,32]{1,2,0:T(8,128)(2,1)S(1)}, bf16[4,256,32]{1,2,0:T(8,128)(2,1)}, u32[]{:S(2)}) %copy-start) | copy-done | bytes 65560
  7.3 1.7 %pad_maximum_fusion = bf16[16,16,512]{2,1,0:T(8,128)(2,1)} fusion(bf16[16,8,512]{2,1,0:T(8,128)(2,1)} %param.5, bf16[16,8,512]{2,1,0:T(8,128)(2,1)} %param.4), kind=kLoop, calls=%fused_computation.2 | loop fusion | flops 524288 | bytes 524288 | tf_op jit(solution)/shard_map/concatenate | solution.py:252
  9.0 0.1 pad_add_fusion.place
  9.0 0.7 %broadcast_in_dim.6.gain_ref = f32[8,512]{1,0:T(8,128)S(1)} broadcast(f32[512]{0:T(512)} %param.6), dimensions={1} | broadcast | bytes 18432 | tf_op jit(solution)/shard_map/broadcast_in_dim | solution.py:253
  9.7 1.9 %collective-permute-done.refs_1_ = bf16[1,4,32,256]{3,2,1,0:T(8,128)(2,1)S(1)} collective-permute-done((bf16[1,4,32,256]{3,2,1,0:T(8,128)(2,1)}, bf16[1,4,32,256]{3,2,1,0:T(8,128)(2,1)S(1)}, u32[]{:S(2)}, u32[]{:S(2)}) %collective-permute-start) | collective-permute-done | bytes 65568 | tf_op jit(solution)/shard_map/ppermute | solution.py:177
  11.6 0.0 collective-permute-done.2.refs_3_
  11.6 0.0 collective-permute-done.1.refs_2_
  11.6 2.5 %collective-permute-start.5 = (bf16[4,4,32,256]{3,2,1,0:T(8,128)(2,1)S(1)}, bf16[4,4,32,256]{3,2,1,0:T(8,128)(2,1)S(1)}, u32[]{:S(2)}, u32[]{:S(2)}) collective-permute-start(bf16[4,4,32,256]{3,2,1,0:T(8,128)(2,1)S(1)} %shard_map.68.refs_0_), channel_id=1, source_target_pairs={{0,3},{1,2},{2,1},{3,0},{4,7},{5,6},{6,5},{7,4},{8,11},{9,10},{10,... | collective-permute-start | bytes 786440 | tf_op jit(solution)/shard_map/ppermute | solution.py:177
  14.1 0.5 collective-permute-start.4
  14.6 0.5 collective-permute-start.3
  15.2 5.4 %all-to-all-start = ((bf16[16,16,512]{2,1,0:T(8,128)(2,1)}), bf16[16,16,512]{2,1,0:T(8,128)(2,1)S(1)}, u32[]{:S(2)}, u32[]{:S(2)}) async-start(bf16[16,16,512]{2,1,0:T(8,128)(2,1)} %pad_maximum_fusion), calls=%async_computation | async-start | bytes 524288 | tf_op jit(solution)/shard_map/all_to_all | solution.py:257
  20.6 0.1 collective-permute-start.6
  20.7 1.2 %collective-permute-done.5.refs_3_ = bf16[4,4,32,256]{3,2,1,0:T(8,128)(2,1)S(1)} collective-permute-done((bf16[4,4,32,256]{3,2,1,0:T(8,128)(2,1)S(1)}, bf16[4,4,32,256]{3,2,1,0:T(8,128)(2,1)S(1)}, u32[]{:S(2)}, u32[]{:S(2)}) %collective-permute-start.5) | collective-permute-done | bytes 262176 | tf_op jit(solution)/shard_map/ppermute | solution.py:177
  21.8 0.0 collective-permute-start.9
  21.9 5.2 %collective-permute-done.4.refs_2_ = bf16[4,4,32,256]{3,2,1,0:T(8,128)(2,1)S(1)} collective-permute-done((bf16[4,4,32,256]{3,2,1,0:T(8,128)(2,1)S(1)}, bf16[4,4,32,256]{3,2,1,0:T(8,128)(2,1)S(1)}, u32[]{:S(2)}, u32[]{:S(2)}) %collective-permute-start.4) | collective-permute-done | bytes 262176 | tf_op jit(solution)/shard_map/ppermute | solution.py:177
  27.1 0.0 collective-permute-start.8
  27.1 0.2 collective-permute-done.3.refs_1_
  27.3 0.3 collective-permute-start.7
  27.6 0.0 collective-permute-done.6.refs_4_
  27.6 1.5 %all-to-all-done.rows_ref = bf16[16,16,512]{2,1,0:T(8,128)(2,1)S(1)} async-done(((bf16[16,16,512]{2,1,0:T(8,128)(2,1)}), bf16[16,16,512]{2,1,0:T(8,128)(2,1)S(1)}, u32[]{:S(2)}, u32[]{:S(2)}) %all-to-all-start) | async-done | bytes 262176 | tf_op jit(solution)/shard_map/all_to_all | solution.py:257
  29.1 0.0 collective-permute-done.9.refs_7_
  29.1 0.0 collective-permute-done.8.refs_6_
  29.1 0.0 collective-permute-done.7.refs_5_
  29.1 2.5 %shard_map.69 = (bf16[16,4,32,256]{3,2,1,0:T(8,128)(2,1)S(1)}, bf16[3,128,512]{2,1,0:T(8,128)(2,1)S(1)}, bf16[128,512]{1,0:T(8,128)(2,1)S(1)}, bf16[4,512,512]{2,1,0:T(8,128)(2,1)S(1)}, f32[1,512]{1,0:T(1,128)S(1)}) custom-call(s32[2]{0:T(128)S(1)} %pad_add_fusion.place, bf16[16,16,512]{2,1,0:T(8,128)(2,1)S(1)} %all-to-all-done.rows_ref, ...), custom_call_target="tpu_custom_call" | custom-call | tf_op jit(solution)/shard_map/pallas_call | solution.py:273
  31.6 0.1 collective-permute-start.10
  31.7 1.9 %shard_map.70 = (bf16[16,4,32,256]{3,2,1,0:T(8,128)(2,1)S(1)}, bf16[128,640]{1,0:T(8,128)(2,1)}) custom-call(s32[2]{0:T(128)S(1)} %pad_add_fusion.place, bf16[16,16,512]{2,1,0:T(8,128)(2,1)S(1)} %all-to-all-done.rows_ref, f32[1,512]{1,0:T(1,128)S(1)} %get-tuple-element.30.gain_ref, bf16[4,512,512]{2,1,0:T(8,128)(2,1)S(1)} %get-tuple-element.31.w_all, ...), custom_call_target="tpu_custom_call" | custom-call | flops 335544320 | bytes 4194304 | tf_op jit(solution)/shard_map/pallas_call | solution.py:287
  33.6 0.8 %collective-permute-done.10 = bf16[16,4,32,256]{3,2,1,0:T(8,128)(2,1)S(1)} collective-permute-done((bf16[16,4,32,256]{3,2,1,0:T(8,128)(2,1)S(1)}, bf16[16,4,32,256]{3,2,1,0:T(8,128)(2,1)S(1)}, u32[]{:S(2)}, u32[]{:S(2)}) %collective-permute-start.10) | collective-permute-done | bytes 1048608 | tf_op jit(solution)/shard_map/ppermute | solution.py:307
  34.4 0.4 add_convert_fusion
  34.8 0.1 fusion.6
  34.8 1.7 %collective-permute-start.11 = (bf16[4,4,32,256]{3,2,1,0:T(8,128)(2,1)S(1)}, bf16[4,4,32,256]{3,2,1,0:T(8,128)(2,1)S(1)}, u32[]{:S(2)}, u32[]{:S(2)}) collective-permute-start(bf16[4,4,32,256]{3,2,1,0:T(8,128)(2,1)S(1)} %get-tuple-element.45), channel_id=1, source_target_pairs={{0,1},{1,0},{2,3},{3,2},{4,5},{5,4},{6,7},{7,6},{8,9},{9,8},{10,11... | collective-permute-start | bytes 786440 | tf_op jit(solution)/shard_map/ppermute | solution.py:177
  36.5 0.8 %collective-permute-start.13 = (bf16[4,4,32,256]{3,2,1,0:T(8,128)(2,1)S(1)}, bf16[4,4,32,256]{3,2,1,0:T(8,128)(2,1)S(1)}, u32[]{:S(2)}, u32[]{:S(2)}) collective-permute-start(bf16[4,4,32,256]{3,2,1,0:T(8,128)(2,1)S(1)} %get-tuple-element.46), channel_id=1, source_target_pairs={{0,2},{1,3},{2,0},{3,1},{4,6},{5,7},{6,4},{7,5},{8,10},{9,11},{10,... | collective-permute-start | bytes 786440 | tf_op jit(solution)/shard_map/ppermute | solution.py:177
  37.3 1.1 %collective-permute-start.12 = (bf16[4,4,32,256]{3,2,1,0:T(8,128)(2,1)S(1)}, bf16[4,4,32,256]{3,2,1,0:T(8,128)(2,1)S(1)}, u32[]{:S(2)}, u32[]{:S(2)}) collective-permute-start(bf16[4,4,32,256]{3,2,1,0:T(8,128)(2,1)S(1)} %get-tuple-element.47), channel_id=1, source_target_pairs={{0,3},{1,2},{2,1},{3,0},{4,7},{5,6},{6,5},{7,4},{8,11},{9,10},{10,... | collective-permute-start | bytes 786440 | tf_op jit(solution)/shard_map/ppermute | solution.py:177
  38.4 5.5 %all-to-all-start.1 = ((bf16[16,8,640]{2,1,0:T(8,128)(2,1)}), bf16[16,8,640]{2,1,0:T(8,128)(2,1)S(1)}, u32[]{:S(2)}, u32[]{:S(2)}) async-start(bf16[16,8,640]{2,1,0:T(8,128)(2,1)} %bitcast.8), calls=%async_computation.1 | async-start | bytes 327680 | tf_op jit(solution)/shard_map/all_to_all | solution.py:304
  43.9 0.2 collective-permute-done.11
  44.1 6.6 %collective-permute-done.13 = bf16[4,4,32,256]{3,2,1,0:T(8,128)(2,1)S(1)} collective-permute-done((bf16[4,4,32,256]{3,2,1,0:T(8,128)(2,1)S(1)}, bf16[4,4,32,256]{3,2,1,0:T(8,128)(2,1)S(1)}, u32[]{:S(2)}, u32[]{:S(2)}) %collective-permute-start.13) | collective-permute-done | bytes 262176 | tf_op jit(solution)/shard_map/ppermute | solution.py:177
  50.7 1.0 %collective-permute-done.12 = bf16[4,4,32,256]{3,2,1,0:T(8,128)(2,1)S(1)} collective-permute-done((bf16[4,4,32,256]{3,2,1,0:T(8,128)(2,1)S(1)}, bf16[4,4,32,256]{3,2,1,0:T(8,128)(2,1)S(1)}, u32[]{:S(2)}, u32[]{:S(2)}) %collective-permute-start.12) | collective-permute-done | bytes 262176 | tf_op jit(solution)/shard_map/ppermute | solution.py:177
  51.7 0.2 fusion.5
  51.9 2.8 %collective-permute-start.16 = (bf16[4,32,256]{2,1,0:T(8,128)(2,1)S(1)}, bf16[4,32,256]{2,1,0:T(8,128)(2,1)S(1)}, u32[]{:S(2)}, u32[]{:S(2)}) collective-permute-start(bf16[4,32,256]{2,1,0:T(8,128)(2,1)S(1)} %get-tuple-element.48), channel_id=1, source_target_pairs={{0,12},{1,13},{2,14},{3,15},{4,8},{5,9},{6,10},{7,11},{8,4},{9,5},... | collective-permute-start | bytes 196616 | tf_op jit(solution)/shard_map/ppermute | solution.py:177
  54.7 0.0 collective-permute-start.15
  54.7 1.6 %collective-permute-start.14 = (bf16[4,32,256]{2,1,0:T(8,128)(2,1)S(1)}, bf16[4,32,256]{2,1,0:T(8,128)(2,1)S(1)}, u32[]{:S(2)}, u32[]{:S(2)}) collective-permute-start(bf16[4,32,256]{2,1,0:T(8,128)(2,1)S(1)} %get-tuple-element.50), channel_id=1, source_target_pairs={{0,8},{1,9},{2,10},{3,11},{4,12},{5,13},{6,14},{7,15},{8,0},{9,1},... | collective-permute-start | bytes 196616 | tf_op jit(solution)/shard_map/ppermute | solution.py:177
  56.4 0.0 all-to-all-done.1
  56.4 1.8 %collective-permute-done.16 = bf16[4,32,256]{2,1,0:T(8,128)(2,1)S(1)} collective-permute-done((bf16[4,32,256]{2,1,0:T(8,128)(2,1)S(1)}, bf16[4,32,256]{2,1,0:T(8,128)(2,1)S(1)}, u32[]{:S(2)}, u32[]{:S(2)}) %collective-permute-start.16) | collective-permute-done | bytes 65568 | tf_op jit(solution)/shard_map/ppermute | solution.py:177
  58.2 0.1 collective-permute-start.17
  58.3 0.7 %slice_bitcast_fusion.1 = bf16[16,8,512]{2,1,0:T(8,128)(2,1)} fusion(bf16[128,640]{1,0:T(8,128)(2,1)S(1)} %bitcast.34), kind=kLoop, calls=%fused_computation.9 | loop fusion | bytes 262144 | tf_op jit(solution)/shard_map/reshape | solution.py:310
  59.0 0.5 collective-permute-done.17
  59.4 0.6 add_multiply_fusion
  60.0 0.0 collective-permute-done.15
  60.0 0.1 collective-permute-done.14
  60.1 0.7 %fusion.4 = f32[4,256,32]{1,2,0:T(8,128)} fusion(f32[4,4,32,256]{3,2,1,0:T(8,128)S(1)} %get-tuple-element.44, bf16[4,32,256]{2,1,0:T(8,128)(2,1)S(1)} %collective-permute-done.16, bf16[4,32,256]{2,1,0:T(8,128)(2,1)S(1)} %collective-permute-done.15, bf16[4,32,256]{2,1,0:T(8,128)(2,1)S(1)} %collective-permute-done.14), kind=kLoop, calls=%fused_computation.8 | loop fusion | flops 229376 | bytes 458752 | tf_op jit(solution)/shard_map/mul | solution.py:322
  (6 shorter events, 0.1 us)
Async XLA Ops:
  0.6 11.0 %collective-permute-start.2 = (bf16[1,4,32,256]{3,2,1,0:T(8,128)(2,1)}, bf16[1,4,32,256]{3,2,1,0:T(8,128)(2,1)S(1)}, u32[]{:S(2)}, u32[]{:S(2)}) collective-permute-start(bf16[1,4,32,256]{3,2,1,0:T(8,128)(2,1)} %bitcast.29), channel_id=1, source_target_pairs={{0,12},{1,13},{2,14},{3,15},{4,8},{5,9},{6,10},{7,11},{8,4},{9,5},... | collective-permute-start | bytes 196616 | tf_op jit(solution)/shard_map/ppermute | solution.py:177
  5.7 5.9 %collective-permute-start.1 = (bf16[1,4,32,256]{3,2,1,0:T(8,128)(2,1)}, bf16[1,4,32,256]{3,2,1,0:T(8,128)(2,1)S(1)}, u32[]{:S(2)}, u32[]{:S(2)}) collective-permute-start(bf16[1,4,32,256]{3,2,1,0:T(8,128)(2,1)} %bitcast.30), channel_id=1, source_target_pairs={{0,4},{1,5},{2,6},{3,7},{4,0},{5,1},{6,2},{7,3},{8,12},{9,13},{10,... | collective-permute-start | bytes 196616 | tf_op jit(solution)/shard_map/ppermute | solution.py:177
  5.7 5.8 %collective-permute-start = (bf16[1,4,32,256]{3,2,1,0:T(8,128)(2,1)}, bf16[1,4,32,256]{3,2,1,0:T(8,128)(2,1)S(1)}, u32[]{:S(2)}, u32[]{:S(2)}) collective-permute-start(bf16[1,4,32,256]{3,2,1,0:T(8,128)(2,1)} %bitcast.31), channel_id=1, source_target_pairs={{0,8},{1,9},{2,10},{3,11},{4,12},{5,13},{6,14},{7,15},{8,0},{9,1},... | collective-permute-start | bytes 196616 | tf_op jit(solution)/shard_map/ppermute | solution.py:177
  6.4 0.9 %copy-start = (bf16[4,256,32]{1,2,0:T(8,128)(2,1)S(1)}, bf16[4,256,32]{1,2,0:T(8,128)(2,1)}, u32[]{:S(2)}) copy-start(bf16[4,256,32]{1,2,0:T(8,128)(2,1)} %param.7) | copy-start | bytes 196612
  11.6 10.2 %collective-permute-start.5 = (bf16[4,4,32,256]{3,2,1,0:T(8,128)(2,1)S(1)}, bf16[4,4,32,256]{3,2,1,0:T(8,128)(2,1)S(1)}, u32[]{:S(2)}, u32[]{:S(2)}) collective-permute-start(bf16[4,4,32,256]{3,2,1,0:T(8,128)(2,1)S(1)} %shard_map.68.refs_0_), channel_id=1, source_target_pairs={{0,3},{1,2},{2,1},{3,0},{4,7},{5,6},{6,5},{7,4},{8,11},{9,10},{10,... | collective-permute-start | bytes 786440 | tf_op jit(solution)/shard_map/ppermute | solution.py:177
  14.1 12.9 %collective-permute-start.4 = (bf16[4,4,32,256]{3,2,1,0:T(8,128)(2,1)S(1)}, bf16[4,4,32,256]{3,2,1,0:T(8,128)(2,1)S(1)}, u32[]{:S(2)}, u32[]{:S(2)}) collective-permute-start(bf16[4,4,32,256]{3,2,1,0:T(8,128)(2,1)S(1)} %shard_map.68.refs_0_), channel_id=1, source_target_pairs={{0,2},{1,3},{2,0},{3,1},{4,6},{5,7},{6,4},{7,5},{8,10},{9,11},{10,... | collective-permute-start | bytes 786440 | tf_op jit(solution)/shard_map/ppermute | solution.py:177
  14.6 12.7 %collective-permute-start.3 = (bf16[4,4,32,256]{3,2,1,0:T(8,128)(2,1)S(1)}, bf16[4,4,32,256]{3,2,1,0:T(8,128)(2,1)S(1)}, u32[]{:S(2)}, u32[]{:S(2)}) collective-permute-start(bf16[4,4,32,256]{3,2,1,0:T(8,128)(2,1)S(1)} %shard_map.68.refs_0_), channel_id=1, source_target_pairs={{0,1},{1,0},{2,3},{3,2},{4,5},{5,4},{6,7},{7,6},{8,9},{9,8},{10,11... | collective-permute-start | bytes 786440 | tf_op jit(solution)/shard_map/ppermute | solution.py:177
  15.2 13.9 %all-to-all-start = ((bf16[16,16,512]{2,1,0:T(8,128)(2,1)}), bf16[16,16,512]{2,1,0:T(8,128)(2,1)S(1)}, u32[]{:S(2)}, u32[]{:S(2)}) async-start(bf16[16,16,512]{2,1,0:T(8,128)(2,1)} %pad_maximum_fusion), calls=%async_computation | async-start | bytes 524288 | tf_op jit(solution)/shard_map/all_to_all | solution.py:257
  20.6 7.0 %collective-permute-start.6 = (bf16[4,4,32,256]{3,2,1,0:T(8,128)(2,1)S(1)}, bf16[4,4,32,256]{3,2,1,0:T(8,128)(2,1)S(1)}, u32[]{:S(2)}, u32[]{:S(2)}) collective-permute-start(bf16[4,4,32,256]{3,2,1,0:T(8,128)(2,1)S(1)} %shard_map.68.refs_0_), channel_id=1, source_target_pairs={{0,16},{16,0},{1,17},{17,1},{2,18},{18,2},{3,19},{19,3},{4,20},{20... | collective-permute-start | bytes 786440 | tf_op jit(solution)/shard_map/ppermute | solution.py:264
  21.8 7.3 %collective-permute-start.9 = (bf16[4,4,32,256]{3,2,1,0:T(8,128)(2,1)S(1)}, bf16[4,4,32,256]{3,2,1,0:T(8,128)(2,1)S(1)}, u32[]{:S(2)}, u32[]{:S(2)}) collective-permute-start(bf16[4,4,32,256]{3,2,1,0:T(8,128)(2,1)S(1)} %collective-permute-done.5.refs_3_), channel_id=1, source_target_pairs={{0,16},{16,0},{1,17},{17,1},{2,18},{18,2},{3,19},{19,3},{4,20},{20... | collective-permute-start | bytes 786440 | tf_op jit(solution)/shard_map/ppermute | solution.py:264
  27.1 2.0 %collective-permute-start.8 = (bf16[4,4,32,256]{3,2,1,0:T(8,128)(2,1)S(1)}, bf16[4,4,32,256]{3,2,1,0:T(8,128)(2,1)S(1)}, u32[]{:S(2)}, u32[]{:S(2)}) collective-permute-start(bf16[4,4,32,256]{3,2,1,0:T(8,128)(2,1)S(1)} %collective-permute-done.4.refs_2_), channel_id=1, source_target_pairs={{0,16},{16,0},{1,17},{17,1},{2,18},{18,2},{3,19},{19,3},{4,20},{20... | collective-permute-start | bytes 786440 | tf_op jit(solution)/shard_map/ppermute | solution.py:264
  27.3 1.8 %collective-permute-start.7 = (bf16[4,4,32,256]{3,2,1,0:T(8,128)(2,1)S(1)}, bf16[4,4,32,256]{3,2,1,0:T(8,128)(2,1)S(1)}, u32[]{:S(2)}, u32[]{:S(2)}) collective-permute-start(bf16[4,4,32,256]{3,2,1,0:T(8,128)(2,1)S(1)} %collective-permute-done.3.refs_1_), channel_id=1, source_target_pairs={{0,16},{16,0},{1,17},{17,1},{2,18},{18,2},{3,19},{19,3},{4,20},{20... | collective-permute-start | bytes 786440 | tf_op jit(solution)/shard_map/ppermute | solution.py:264
  31.6 2.7 %collective-permute-start.10 = (bf16[16,4,32,256]{3,2,1,0:T(8,128)(2,1)S(1)}, bf16[16,4,32,256]{3,2,1,0:T(8,128)(2,1)S(1)}, u32[]{:S(2)}, u32[]{:S(2)}) collective-permute-start(bf16[16,4,32,256]{3,2,1,0:T(8,128)(2,1)S(1)} %get-tuple-element.35), channel_id=1, source_target_pairs={{0,16},{16,0},{1,17},{17,1},{2,18},{18,2},{3,19},{19,3},{4,20},{20... | collective-permute-start | bytes 3145736 | tf_op jit(solution)/shard_map/ppermute | solution.py:307
  34.8 9.2 %collective-permute-start.11 = (bf16[4,4,32,256]{3,2,1,0:T(8,128)(2,1)S(1)}, bf16[4,4,32,256]{3,2,1,0:T(8,128)(2,1)S(1)}, u32[]{:S(2)}, u32[]{:S(2)}) collective-permute-start(bf16[4,4,32,256]{3,2,1,0:T(8,128)(2,1)S(1)} %get-tuple-element.45), channel_id=1, source_target_pairs={{0,1},{1,0},{2,3},{3,2},{4,5},{5,4},{6,7},{7,6},{8,9},{9,8},{10,11... | collective-permute-start | bytes 786440 | tf_op jit(solution)/shard_map/ppermute | solution.py:177
  36.5 14.2 %collective-permute-start.13 = (bf16[4,4,32,256]{3,2,1,0:T(8,128)(2,1)S(1)}, bf16[4,4,32,256]{3,2,1,0:T(8,128)(2,1)S(1)}, u32[]{:S(2)}, u32[]{:S(2)}) collective-permute-start(bf16[4,4,32,256]{3,2,1,0:T(8,128)(2,1)S(1)} %get-tuple-element.46), channel_id=1, source_target_pairs={{0,2},{1,3},{2,0},{3,1},{4,6},{5,7},{6,4},{7,5},{8,10},{9,11},{10,... | collective-permute-start | bytes 786440 | tf_op jit(solution)/shard_map/ppermute | solution.py:177
  37.3 14.4 %collective-permute-start.12 = (bf16[4,4,32,256]{3,2,1,0:T(8,128)(2,1)S(1)}, bf16[4,4,32,256]{3,2,1,0:T(8,128)(2,1)S(1)}, u32[]{:S(2)}, u32[]{:S(2)}) collective-permute-start(bf16[4,4,32,256]{3,2,1,0:T(8,128)(2,1)S(1)} %get-tuple-element.47), channel_id=1, source_target_pairs={{0,3},{1,2},{2,1},{3,0},{4,7},{5,6},{6,5},{7,4},{8,11},{9,10},{10,... | collective-permute-start | bytes 786440 | tf_op jit(solution)/shard_map/ppermute | solution.py:177
  38.4 18.0 %all-to-all-start.1 = ((bf16[16,8,640]{2,1,0:T(8,128)(2,1)}), bf16[16,8,640]{2,1,0:T(8,128)(2,1)S(1)}, u32[]{:S(2)}, u32[]{:S(2)}) async-start(bf16[16,8,640]{2,1,0:T(8,128)(2,1)} %bitcast.8), calls=%async_computation.1 | async-start | bytes 327680 | tf_op jit(solution)/shard_map/all_to_all | solution.py:304
  51.9 6.2 %collective-permute-start.16 = (bf16[4,32,256]{2,1,0:T(8,128)(2,1)S(1)}, bf16[4,32,256]{2,1,0:T(8,128)(2,1)S(1)}, u32[]{:S(2)}, u32[]{:S(2)}) collective-permute-start(bf16[4,32,256]{2,1,0:T(8,128)(2,1)S(1)} %get-tuple-element.48), channel_id=1, source_target_pairs={{0,12},{1,13},{2,14},{3,15},{4,8},{5,9},{6,10},{7,11},{8,4},{9,5},... | collective-permute-start | bytes 196616 | tf_op jit(solution)/shard_map/ppermute | solution.py:177
  54.7 5.3 %collective-permute-start.15 = (bf16[4,32,256]{2,1,0:T(8,128)(2,1)S(1)}, bf16[4,32,256]{2,1,0:T(8,128)(2,1)S(1)}, u32[]{:S(2)}, u32[]{:S(2)}) collective-permute-start(bf16[4,32,256]{2,1,0:T(8,128)(2,1)S(1)} %get-tuple-element.49), channel_id=1, source_target_pairs={{0,4},{1,5},{2,6},{3,7},{4,0},{5,1},{6,2},{7,3},{8,12},{9,13},{10,... | collective-permute-start | bytes 196616 | tf_op jit(solution)/shard_map/ppermute | solution.py:177
  54.7 5.3 %collective-permute-start.14 = (bf16[4,32,256]{2,1,0:T(8,128)(2,1)S(1)}, bf16[4,32,256]{2,1,0:T(8,128)(2,1)S(1)}, u32[]{:S(2)}, u32[]{:S(2)}) collective-permute-start(bf16[4,32,256]{2,1,0:T(8,128)(2,1)S(1)} %get-tuple-element.50), channel_id=1, source_target_pairs={{0,8},{1,9},{2,10},{3,11},{4,12},{5,13},{6,14},{7,15},{8,0},{9,1},... | collective-permute-start | bytes 196616 | tf_op jit(solution)/shard_map/ppermute | solution.py:177
  58.2 1.2 %collective-permute-start.17 = (f32[512]{0:T(512)S(1)}, f32[512]{0:T(512)S(1)}, u32[]{:S(2)}, u32[]{:S(2)}) collective-permute-start(f32[512]{0:T(512)S(1)} %reduce_sum.9), channel_id=1, source_target_pairs={{0,16},{16,0},{1,17},{17,1},{2,18},{18,2},{3,19},{19,3},{4,20},{20... | collective-permute-start | bytes 6152 | tf_op jit(solution)/shard_map/ppermute | solution.py:313

commit v8 on v7

--- a/solution.py
+++ b/solution.py
@@ -17,11 +17,7 @@
 
 
 def send_slot(offset, count):
-    slot, bit = offset & 3, 4
-    while bit < count:
-        slot = slot * 2 + (offset // bit) % 2
-        bit *= 2
-    return slot
+    return (offset & 3) * (count // 4) + offset // 4
 
 
 def join_weights(groups, offsets, group, track, w_refs, w_all):
@@ -232,15 +228,21 @@
 def scatter_sum(blocks, axis):
     count = lax.axis_size(axis)
     blocks = blocks.reshape((4, count // 4) + blocks.shape[1:])
-    moved = [swap(blocks[bits], axis, bits) for bits in (1, 3, 2)]
-    total = blocks[0].astype(F32) + sum(block.astype(F32) for block in moved)
-    bit = 4
-    while total.shape[0] > 4:
-        half = total.shape[0] // 2
-        total = total[:half] + swap(total[half:].astype(BF), axis, bit).astype(F32)
-        bit *= 2
-    low = total.astype(BF)
-    return [total[0]] + [swap(low[at], axis, bits * bit) for at, bits in ((1, 2), (2, 1), (3, 3))]
+    half = blocks.shape[1] // 2
+
+    def plane_sum(blocks):
+        moved = [swap(blocks[bits], axis, bits) for bits in (2, 3, 1)]
+        return blocks[0].astype(F32) + sum(block.astype(F32) for block in moved)
+
+    far, close = plane_sum(blocks[:, half:]), plane_sum(blocks[:, :half])
+    bit = count // 2
+    while bit > 8:
+        total = close + swap(far.astype(BF), axis, bit).astype(F32)
+        half //= 2
+        far, close = total[half:], total[:half]
+        bit //= 2
+    moved = [swap(far[at].astype(BF), axis, 8 + 4 * at) for at in range(2)]
+    return [close[0], swap(close[1].astype(BF), axis, 4)] + moved
 
 
 def shards(fields, upstream, ln_gain, weights):

time: 61.2 us -> 60.4 us (0.987)
  waiting for transfers between devices: 20.9 us -> 16.7 us
  starting transfers between devices: 28.7 us -> 32.2 us
    ppermute x12 -> x15, waiting for transfers between devices: 18.1 us -> 13.4 us  [swap(): lax.ppermute(array, axis, [(i, i ^ bits) for i in range(lax.axis_size(axi...]
    ppermute x12 -> x15, starting transfers between devices: 17.3 us -> 21.2 us  [swap(): lax.ppermute(array, axis, [(i, i ^ bits) for i in range(lax.axis_size(axi...]
  transfers between devices with their start and end apart: 20 -> 23, of which waited for: 12 -> 11; matrix products, arithmetic and copies ran while one was open for 7% -> 7% of each run, Pallas kernels for 3% -> 3%
where the time goes in v8:
time: 60.4 us; the launch traced here: 60 us
  starting transfers between devices  32.2 us (53%)
  waiting for transfers between devices  16.7 us (28%)
  Pallas kernels  4.34 us (7%)
  other arithmetic  3.69 us (6%)
  local copies, waits for them, and re-layouts  2.33 us (4%)
  between operations  0.77 us (1%)
    ppermute x15, starting transfers between devices, swap(): lax.ppermute(array, axis, [(i, i ^ bits) for i in range(lax.axis_size(axi...  21.2 us
    ppermute x15, waiting for transfers between devices, swap(): lax.ppermute(array, axis, [(i, i ^ bits) for i in range(lax.axis_size(axi...  13.4 us
    all_to_all x1, starting transfers between devices, shards(): row = lax.all_to_all(both, 'trk', split_axis=0, concat_axis=0, tiled=True)  5.42 us
    all_to_all x1, starting transfers between devices, shards(): back = lax.all_to_all(cells, 'trk', split_axis=0, concat_axis=0, tiled=True)  5.13 us
    pallas_call x1, Pallas kernels, shards(): pl.pallas_call(functools.partial(attend_kernel, groups, offsets), out_sha...  2.52 us
    pallas_call x1, Pallas kernels, shards(): pl.pallas_call(functools.partial(cells_kernel, groups), out_shape=(wg_sha...  1.79 us
    concatenate x1, other arithmetic, shards(): both = jnp.concatenate([fields, upstream], 1)  1.71 us
    all_to_all x1, waiting for transfers between devices, shards(): row = lax.all_to_all(both, 'trk', split_axis=0, concat_axis=0, tiled=True)  1.52 us
  transfers between devices with their start and end apart: 23, of which 11 were waited for; matrix products, arithmetic and copies ran while one was open for 7% of the time, Pallas kernels for 3%

profile of v8, /device:TPU:0, one launch (start us, length us, event | category | flops | bytes accessed | tf_op | source)
XLA Modules:
  0.0 60.0 jit_solution(14171619809307796284)
XLA Ops:
  0.6 5.1 %collective-permute-start.2 = (bf16[1,4,32,256]{3,2,1,0:T(8,128)(2,1)}, bf16[1,4,32,256]{3,2,1,0:T(8,128)(2,1)S(1)}, u32[]{:S(2)}, u32[]{:S(2)}) collective-permute-start(bf16[1,4,32,256]{3,2,1,0:T(8,128)(2,1)} %bitcast.52), channel_id=1, source_target_pairs={{0,12},{1,13},{2,14},{3,15},{4,8},{5,9},{6,10},{7,11},{8,4},{9,5},... | collective-permute-start | bytes 196616 | tf_op jit(solution)/shard_map/ppermute | solution.py:173
  5.7 0.0 collective-permute-start.1
  5.7 0.6 %collective-permute-start = (bf16[1,4,32,256]{3,2,1,0:T(8,128)(2,1)}, bf16[1,4,32,256]{3,2,1,0:T(8,128)(2,1)S(1)}, u32[]{:S(2)}, u32[]{:S(2)}) collective-permute-start(bf16[1,4,32,256]{3,2,1,0:T(8,128)(2,1)} %bitcast.54), channel_id=1, source_target_pairs={{0,8},{1,9},{2,10},{3,11},{4,12},{5,13},{6,14},{7,15},{8,0},{9,1},... | collective-permute-start | bytes 196616 | tf_op jit(solution)/shard_map/ppermute | solution.py:173
  6.4 0.0 copy-start
  6.4 0.9 %copy-done = bf16[4,256,32]{1,2,0:T(8,128)(2,1)S(1)} copy-done((bf16[4,256,32]{1,2,0:T(8,128)(2,1)S(1)}, bf16[4,256,32]{1,2,0:T(8,128)(2,1)}, u32[]{:S(2)}) %copy-start) | copy-done | bytes 65560
  7.3 1.7 %pad_maximum_fusion = bf16[16,16,512]{2,1,0:T(8,128)(2,1)} fusion(bf16[16,8,512]{2,1,0:T(8,128)(2,1)} %param.5, bf16[16,8,512]{2,1,0:T(8,128)(2,1)} %param.4), kind=kLoop, calls=%fused_computation.1 | loop fusion | flops 524288 | bytes 524288 | tf_op jit(solution)/shard_map/concatenate | solution.py:254
  9.0 0.1 pad_add_fusion.place
  9.1 0.7 %broadcast_in_dim.6.gain_ref = f32[8,512]{1,0:T(8,128)S(1)} broadcast(f32[512]{0:T(512)} %param.6), dimensions={1} | broadcast | bytes 18432 | tf_op jit(solution)/shard_map/broadcast_in_dim | solution.py:255
  9.7 1.9 %collective-permute-done.refs_1_ = bf16[1,4,32,256]{3,2,1,0:T(8,128)(2,1)S(1)} collective-permute-done((bf16[1,4,32,256]{3,2,1,0:T(8,128)(2,1)}, bf16[1,4,32,256]{3,2,1,0:T(8,128)(2,1)S(1)}, u32[]{:S(2)}, u32[]{:S(2)}) %collective-permute-start) | collective-permute-done | bytes 65568 | tf_op jit(solution)/shard_map/ppermute | solution.py:173
  11.6 0.0 collective-permute-done.2.refs_3_
  11.6 0.0 collective-permute-done.1.refs_2_
  11.6 2.5 %collective-permute-start.5 = (bf16[4,4,32,256]{3,2,1,0:T(8,128)(2,1)S(1)}, bf16[4,4,32,256]{3,2,1,0:T(8,128)(2,1)S(1)}, u32[]{:S(2)}, u32[]{:S(2)}) collective-permute-start(bf16[4,4,32,256]{3,2,1,0:T(8,128)(2,1)S(1)} %shard_map.68.refs_0_), channel_id=1, source_target_pairs={{0,3},{1,2},{2,1},{3,0},{4,7},{5,6},{6,5},{7,4},{8,11},{9,10},{10,... | collective-permute-start | bytes 786440 | tf_op jit(solution)/shard_map/ppermute | solution.py:173
  14.1 0.5 collective-permute-start.4
  14.6 0.5 collective-permute-start.3
  15.2 5.4 %all-to-all-start = ((bf16[16,16,512]{2,1,0:T(8,128)(2,1)}), bf16[16,16,512]{2,1,0:T(8,128)(2,1)S(1)}, u32[]{:S(2)}, u32[]{:S(2)}) async-start(bf16[16,16,512]{2,1,0:T(8,128)(2,1)} %pad_maximum_fusion), calls=%async_computation | async-start | bytes 524288 | tf_op jit(solution)/shard_map/all_to_all | solution.py:259
  20.6 0.1 collective-permute-start.6
  20.7 1.2 %collective-permute-done.5.refs_3_ = bf16[4,4,32,256]{3,2,1,0:T(8,128)(2,1)S(1)} collective-permute-done((bf16[4,4,32,256]{3,2,1,0:T(8,128)(2,1)S(1)}, bf16[4,4,32,256]{3,2,1,0:T(8,128)(2,1)S(1)}, u32[]{:S(2)}, u32[]{:S(2)}) %collective-permute-start.5) | collective-permute-done | bytes 262176 | tf_op jit(solution)/shard_map/ppermute | solution.py:173
  21.8 0.0 collective-permute-start.9
  21.9 5.2 %collective-permute-done.4.refs_2_ = bf16[4,4,32,256]{3,2,1,0:T(8,128)(2,1)S(1)} collective-permute-done((bf16[4,4,32,256]{3,2,1,0:T(8,128)(2,1)S(1)}, bf16[4,4,32,256]{3,2,1,0:T(8,128)(2,1)S(1)}, u32[]{:S(2)}, u32[]{:S(2)}) %collective-permute-start.4) | collective-permute-done | bytes 262176 | tf_op jit(solution)/shard_map/ppermute | solution.py:173
  27.1 0.0 collective-permute-start.8
  27.1 0.2 collective-permute-done.3.refs_1_
  27.3 0.3 collective-permute-start.7
  27.6 0.0 collective-permute-done.6.refs_4_
  27.6 1.5 %all-to-all-done.rows_ref = bf16[16,16,512]{2,1,0:T(8,128)(2,1)S(1)} async-done(((bf16[16,16,512]{2,1,0:T(8,128)(2,1)}), bf16[16,16,512]{2,1,0:T(8,128)(2,1)S(1)}, u32[]{:S(2)}, u32[]{:S(2)}) %all-to-all-start) | async-done | bytes 262176 | tf_op jit(solution)/shard_map/all_to_all | solution.py:259
  29.1 0.0 collective-permute-done.9.refs_7_
  29.1 0.0 collective-permute-done.8.refs_6_
  29.1 0.0 collective-permute-done.7.refs_5_
  29.1 2.5 %shard_map.69 = (bf16[16,4,32,256]{3,2,1,0:T(8,128)(2,1)S(1)}, bf16[3,128,512]{2,1,0:T(8,128)(2,1)S(1)}, bf16[128,512]{1,0:T(8,128)(2,1)S(1)}, bf16[4,512,512]{2,1,0:T(8,128)(2,1)S(1)}, f32[1,512]{1,0:T(1,128)S(1)}) custom-call(s32[2]{0:T(128)S(1)} %pad_add_fusion.place, bf16[16,16,512]{2,1,0:T(8,128)(2,1)S(1)} %all-to-all-done.rows_ref, ...), custom_call_target="tpu_custom_call" | custom-call | tf_op jit(solution)/shard_map/pallas_call | solution.py:275
  31.6 0.1 collective-permute-start.10
  31.7 1.8 %shard_map.70 = (bf16[16,4,32,256]{3,2,1,0:T(8,128)(2,1)S(1)}, bf16[128,640]{1,0:T(8,128)(2,1)}) custom-call(s32[2]{0:T(128)S(1)} %pad_add_fusion.place, bf16[16,16,512]{2,1,0:T(8,128)(2,1)S(1)} %all-to-all-done.rows_ref, f32[1,512]{1,0:T(1,128)S(1)} %get-tuple-element.30.gain_ref, bf16[4,512,512]{2,1,0:T(8,128)(2,1)S(1)} %get-tuple-element.31.w_all, ...), custom_call_target="tpu_custom_call" | custom-call | flops 335544320 | bytes 4194304 | tf_op jit(solution)/shard_map/pallas_call | solution.py:289
  33.5 0.9 %collective-permute-done.10 = bf16[16,4,32,256]{3,2,1,0:T(8,128)(2,1)S(1)} collective-permute-done((bf16[16,4,32,256]{3,2,1,0:T(8,128)(2,1)S(1)}, bf16[16,4,32,256]{3,2,1,0:T(8,128)(2,1)S(1)}, u32[]{:S(2)}, u32[]{:S(2)}) %collective-permute-start.10) | collective-permute-done | bytes 1048608 | tf_op jit(solution)/shard_map/ppermute | solution.py:309
  34.4 0.4 add_convert_fusion
  34.8 0.1 slice_bitcast_fusion.3
  34.9 1.8 %collective-permute-start.15 = (bf16[2,4,32,256]{3,2,1,0:T(8,128)(2,1)S(1)}, bf16[2,4,32,256]{3,2,1,0:T(8,128)(2,1)S(1)}, u32[]{:S(2)}, u32[]{:S(2)}) collective-permute-start(bf16[2,4,32,256]{3,2,1,0:T(8,128)(2,1)S(1)} %get-tuple-element.45), channel_id=1, source_target_pairs={{0,2},{1,3},{2,0},{3,1},{4,6},{5,7},{6,4},{7,5},{8,10},{9,11},{10,... | collective-permute-start | bytes 393224 | tf_op jit(solution)/shard_map/ppermute | solution.py:173
  36.7 0.6 collective-permute-start.17
  37.3 1.1 %collective-permute-start.16 = (bf16[2,4,32,256]{3,2,1,0:T(8,128)(2,1)S(1)}, bf16[2,4,32,256]{3,2,1,0:T(8,128)(2,1)S(1)}, u32[]{:S(2)}, u32[]{:S(2)}) collective-permute-start(bf16[2,4,32,256]{3,2,1,0:T(8,128)(2,1)S(1)} %get-tuple-element.47), channel_id=1, source_target_pairs={{0,3},{1,2},{2,1},{3,0},{4,7},{5,6},{6,5},{7,4},{8,11},{9,10},{10,... | collective-permute-start | bytes 393224 | tf_op jit(solution)/shard_map/ppermute | solution.py:173
  38.4 1.6 %collective-permute-start.13 = (bf16[2,4,32,256]{3,2,1,0:T(8,128)(2,1)S(1)}, bf16[2,4,32,256]{3,2,1,0:T(8,128)(2,1)S(1)}, u32[]{:S(2)}, u32[]{:S(2)}) collective-permute-start(bf16[2,4,32,256]{3,2,1,0:T(8,128)(2,1)S(1)} %get-tuple-element.48), channel_id=1, source_target_pairs={{0,1},{1,0},{2,3},{3,2},{4,5},{5,4},{6,7},{7,6},{8,9},{9,8},{10,11... | collective-permute-start | bytes 393224 | tf_op jit(solution)/shard_map/ppermute | solution.py:173
  40.0 1.6 %collective-permute-start.12 = (bf16[2,4,32,256]{3,2,1,0:T(8,128)(2,1)S(1)}, bf16[2,4,32,256]{3,2,1,0:T(8,128)(2,1)S(1)}, u32[]{:S(2)}, u32[]{:S(2)}) collective-permute-start(bf16[2,4,32,256]{3,2,1,0:T(8,128)(2,1)S(1)} %get-tuple-element.49), channel_id=1, source_target_pairs={{0,3},{1,2},{2,1},{3,0},{4,7},{5,6},{6,5},{7,4},{8,11},{9,10},{10,... | collective-permute-start | bytes 393224 | tf_op jit(solution)/shard_map/ppermute | solution.py:173
  41.7 0.0 collective-permute-done.15
  41.7 0.6 collective-permute-start.11
  42.2 5.1 %all-to-all-start.1 = ((bf16[16,8,640]{2,1,0:T(8,128)(2,1)}), bf16[16,8,640]{2,1,0:T(8,128)(2,1)S(1)}, u32[]{:S(2)}, u32[]{:S(2)}) async-start(bf16[16,8,640]{2,1,0:T(8,128)(2,1)} %bitcast.17), calls=%async_computation.1 | async-start | bytes 327680 | tf_op jit(solution)/shard_map/all_to_all | solution.py:306
  47.4 0.0 collective-permute-done.17
  47.4 0.0 collective-permute-done.16
  47.4 1.3 %collective-permute-done.13 = bf16[2,4,32,256]{3,2,1,0:T(8,128)(2,1)S(1)} collective-permute-done((bf16[2,4,32,256]{3,2,1,0:T(8,128)(2,1)S(1)}, bf16[2,4,32,256]{3,2,1,0:T(8,128)(2,1)S(1)}, u32[]{:S(2)}, u32[]{:S(2)}) %collective-permute-start.13) | collective-permute-done | bytes 131104 | tf_op jit(solution)/shard_map/ppermute | solution.py:173
  48.7 1.9 %collective-permute-done.12 = bf16[2,4,32,256]{3,2,1,0:T(8,128)(2,1)S(1)} collective-permute-done((bf16[2,4,32,256]{3,2,1,0:T(8,128)(2,1)S(1)}, bf16[2,4,32,256]{3,2,1,0:T(8,128)(2,1)S(1)}, u32[]{:S(2)}, u32[]{:S(2)}) %collective-permute-start.12) | collective-permute-done | bytes 131104 | tf_op jit(solution)/shard_map/ppermute | solution.py:173
  50.6 0.0 collective-permute-done.11
  50.6 0.2 fusion
  50.8 2.6 %collective-permute-start.19 = (bf16[4,32,256]{2,1,0:T(8,128)(2,1)S(1)}, bf16[4,32,256]{2,1,0:T(8,128)(2,1)S(1)}, u32[]{:S(2)}, u32[]{:S(2)}) collective-permute-start(bf16[4,32,256]{2,1,0:T(8,128)(2,1)S(1)} %get-tuple-element.51), channel_id=1, source_target_pairs={{0,12},{1,13},{2,14},{3,15},{4,8},{5,9},{6,10},{7,11},{8,4},{9,5},... | collective-permute-start | bytes 196616 | tf_op jit(solution)/shard_map/ppermute | solution.py:173
  53.4 0.1 collective-permute-start.14
  53.5 1.8 %collective-permute-start.18 = (bf16[4,32,256]{2,1,0:T(8,128)(2,1)S(1)}, bf16[4,32,256]{2,1,0:T(8,128)(2,1)S(1)}, u32[]{:S(2)}, u32[]{:S(2)}) collective-permute-start(bf16[4,32,256]{2,1,0:T(8,128)(2,1)S(1)} %get-tuple-element.52), channel_id=1, source_target_pairs={{0,8},{1,9},{2,10},{3,11},{4,12},{5,13},{6,14},{7,15},{8,0},{9,1},... | collective-permute-start | bytes 196616 | tf_op jit(solution)/shard_map/ppermute | solution.py:173
  55.3 0.4 all-to-all-done.1
  55.7 1.8 %collective-permute-done.19 = bf16[4,32,256]{2,1,0:T(8,128)(2,1)S(1)} collective-permute-done((bf16[4,32,256]{2,1,0:T(8,128)(2,1)S(1)}, bf16[4,32,256]{2,1,0:T(8,128)(2,1)S(1)}, u32[]{:S(2)}, u32[]{:S(2)}) %collective-permute-start.19) | collective-permute-done | bytes 65568 | tf_op jit(solution)/shard_map/ppermute | solution.py:173
  57.5 0.1 collective-permute-start.20
  57.6 0.7 %slice_bitcast_fusion.9 = bf16[16,8,512]{2,1,0:T(8,128)(2,1)} fusion(bf16[128,640]{1,0:T(8,128)(2,1)S(1)} %bitcast.59), kind=kLoop, calls=%fused_computation.20 | loop fusion | bytes 262144 | tf_op jit(solution)/shard_map/reshape | solution.py:312
  58.3 0.5 collective-permute-done.20
  58.7 0.6 add_multiply_fusion
  59.3 0.0 collective-permute-done.14
  59.3 0.0 collective-permute-done.18
  59.3 0.7 %fusion.5 = f32[4,256,32]{1,2,0:T(8,128)} fusion(f32[2,4,32,256]{3,2,1,0:T(8,128)S(1)} %get-tuple-element.44, bf16[4,32,256]{2,1,0:T(8,128)(2,1)S(1)} %collective-permute-done.19, bf16[4,32,256]{2,1,0:T(8,128)(2,1)S(1)} %collective-permute-done.18, bf16[4,32,256]{2,1,0:T(8,128)(2,1)S(1)} %collective-permute-done.14), kind=kLoop, calls=%fused_computation.10 | loop fusion | flops 229376 | bytes 458752 | tf_op jit(solution)/shard_map/mul | solution.py:324
  (7 shorter events, 0.1 us)
Async XLA Ops:
  0.6 11.0 %collective-permute-start.2 = (bf16[1,4,32,256]{3,2,1,0:T(8,128)(2,1)}, bf16[1,4,32,256]{3,2,1,0:T(8,128)(2,1)S(1)}, u32[]{:S(2)}, u32[]{:S(2)}) collective-permute-start(bf16[1,4,32,256]{3,2,1,0:T(8,128)(2,1)} %bitcast.52), channel_id=1, source_target_pairs={{0,12},{1,13},{2,14},{3,15},{4,8},{5,9},{6,10},{7,11},{8,4},{9,5},... | collective-permute-start | bytes 196616 | tf_op jit(solution)/shard_map/ppermute | solution.py:173
  5.7 5.9 %collective-permute-start.1 = (bf16[1,4,32,256]{3,2,1,0:T(8,128)(2,1)}, bf16[1,4,32,256]{3,2,1,0:T(8,128)(2,1)S(1)}, u32[]{:S(2)}, u32[]{:S(2)}) collective-permute-start(bf16[1,4,32,256]{3,2,1,0:T(8,128)(2,1)} %bitcast.53), channel_id=1, source_target_pairs={{0,4},{1,5},{2,6},{3,7},{4,0},{5,1},{6,2},{7,3},{8,12},{9,13},{10,... | collective-permute-start | bytes 196616 | tf_op jit(solution)/shard_map/ppermute | solution.py:173
  5.7 5.8 %collective-permute-start = (bf16[1,4,32,256]{3,2,1,0:T(8,128)(2,1)}, bf16[1,4,32,256]{3,2,1,0:T(8,128)(2,1)S(1)}, u32[]{:S(2)}, u32[]{:S(2)}) collective-permute-start(bf16[1,4,32,256]{3,2,1,0:T(8,128)(2,1)} %bitcast.54), channel_id=1, source_target_pairs={{0,8},{1,9},{2,10},{3,11},{4,12},{5,13},{6,14},{7,15},{8,0},{9,1},... | collective-permute-start | bytes 196616 | tf_op jit(solution)/shard_map/ppermute | solution.py:173
  6.4 0.9 %copy-start = (bf16[4,256,32]{1,2,0:T(8,128)(2,1)S(1)}, bf16[4,256,32]{1,2,0:T(8,128)(2,1)}, u32[]{:S(2)}) copy-start(bf16[4,256,32]{1,2,0:T(8,128)(2,1)} %param.7) | copy-start | bytes 196612
  11.6 10.2 %collective-permute-start.5 = (bf16[4,4,32,256]{3,2,1,0:T(8,128)(2,1)S(1)}, bf16[4,4,32,256]{3,2,1,0:T(8,128)(2,1)S(1)}, u32[]{:S(2)}, u32[]{:S(2)}) collective-permute-start(bf16[4,4,32,256]{3,2,1,0:T(8,128)(2,1)S(1)} %shard_map.68.refs_0_), channel_id=1, source_target_pairs={{0,3},{1,2},{2,1},{3,0},{4,7},{5,6},{6,5},{7,4},{8,11},{9,10},{10,... | collective-permute-start | bytes 786440 | tf_op jit(solution)/shard_map/ppermute | solution.py:173
  14.1 12.9 %collective-permute-start.4 = (bf16[4,4,32,256]{3,2,1,0:T(8,128)(2,1)S(1)}, bf16[4,4,32,256]{3,2,1,0:T(8,128)(2,1)S(1)}, u32[]{:S(2)}, u32[]{:S(2)}) collective-permute-start(bf16[4,4,32,256]{3,2,1,0:T(8,128)(2,1)S(1)} %shard_map.68.refs_0_), channel_id=1, source_target_pairs={{0,2},{1,3},{2,0},{3,1},{4,6},{5,7},{6,4},{7,5},{8,10},{9,11},{10,... | collective-permute-start | bytes 786440 | tf_op jit(solution)/shard_map/ppermute | solution.py:173
  14.6 12.7 %collective-permute-start.3 = (bf16[4,4,32,256]{3,2,1,0:T(8,128)(2,1)S(1)}, bf16[4,4,32,256]{3,2,1,0:T(8,128)(2,1)S(1)}, u32[]{:S(2)}, u32[]{:S(2)}) collective-permute-start(bf16[4,4,32,256]{3,2,1,0:T(8,128)(2,1)S(1)} %shard_map.68.refs_0_), channel_id=1, source_target_pairs={{0,1},{1,0},{2,3},{3,2},{4,5},{5,4},{6,7},{7,6},{8,9},{9,8},{10,11... | collective-permute-start | bytes 786440 | tf_op jit(solution)/shard_map/ppermute | solution.py:173
  15.2 13.9 %all-to-all-start = ((bf16[16,16,512]{2,1,0:T(8,128)(2,1)}), bf16[16,16,512]{2,1,0:T(8,128)(2,1)S(1)}, u32[]{:S(2)}, u32[]{:S(2)}) async-start(bf16[16,16,512]{2,1,0:T(8,128)(2,1)} %pad_maximum_fusion), calls=%async_computation | async-start | bytes 524288 | tf_op jit(solution)/shard_map/all_to_all | solution.py:259
  20.6 7.0 %collective-permute-start.6 = (bf16[4,4,32,256]{3,2,1,0:T(8,128)(2,1)S(1)}, bf16[4,4,32,256]{3,2,1,0:T(8,128)(2,1)S(1)}, u32[]{:S(2)}, u32[]{:S(2)}) collective-permute-start(bf16[4,4,32,256]{3,2,1,0:T(8,128)(2,1)S(1)} %shard_map.68.refs_0_), channel_id=1, source_target_pairs={{0,16},{16,0},{1,17},{17,1},{2,18},{18,2},{3,19},{19,3},{4,20},{20... | collective-permute-start | bytes 786440 | tf_op jit(solution)/shard_map/ppermute | solution.py:266
  21.8 7.3 %collective-permute-start.9 = (bf16[4,4,32,256]{3,2,1,0:T(8,128)(2,1)S(1)}, bf16[4,4,32,256]{3,2,1,0:T(8,128)(2,1)S(1)}, u32[]{:S(2)}, u32[]{:S(2)}) collective-permute-start(bf16[4,4,32,256]{3,2,1,0:T(8,128)(2,1)S(1)} %collective-permute-done.5.refs_3_), channel_id=1, source_target_pairs={{0,16},{16,0},{1,17},{17,1},{2,18},{18,2},{3,19},{19,3},{4,20},{20... | collective-permute-start | bytes 786440 | tf_op jit(solution)/shard_map/ppermute | solution.py:266
  27.1 2.0 %collective-permute-start.8 = (bf16[4,4,32,256]{3,2,1,0:T(8,128)(2,1)S(1)}, bf16[4,4,32,256]{3,2,1,0:T(8,128)(2,1)S(1)}, u32[]{:S(2)}, u32[]{:S(2)}) collective-permute-start(bf16[4,4,32,256]{3,2,1,0:T(8,128)(2,1)S(1)} %collective-permute-done.4.refs_2_), channel_id=1, source_target_pairs={{0,16},{16,0},{1,17},{17,1},{2,18},{18,2},{3,19},{19,3},{4,20},{20... | collective-permute-start | bytes 786440 | tf_op jit(solution)/shard_map/ppermute | solution.py:266
  27.3 1.8 %collective-permute-start.7 = (bf16[4,4,32,256]{3,2,1,0:T(8,128)(2,1)S(1)}, bf16[4,4,32,256]{3,2,1,0:T(8,128)(2,1)S(1)}, u32[]{:S(2)}, u32[]{:S(2)}) collective-permute-start(bf16[4,4,32,256]{3,2,1,0:T(8,128)(2,1)S(1)} %collective-permute-done.3.refs_1_), channel_id=1, source_target_pairs={{0,16},{16,0},{1,17},{17,1},{2,18},{18,2},{3,19},{19,3},{4,20},{20... | collective-permute-start | bytes 786440 | tf_op jit(solution)/shard_map/ppermute | solution.py:266
  31.6 2.7 %collective-permute-start.10 = (bf16[16,4,32,256]{3,2,1,0:T(8,128)(2,1)S(1)}, bf16[16,4,32,256]{3,2,1,0:T(8,128)(2,1)S(1)}, u32[]{:S(2)}, u32[]{:S(2)}) collective-permute-start(bf16[16,4,32,256]{3,2,1,0:T(8,128)(2,1)S(1)} %get-tuple-element.35), channel_id=1, source_target_pairs={{0,16},{16,0},{1,17},{17,1},{2,18},{18,2},{3,19},{19,3},{4,20},{20... | collective-permute-start | bytes 3145736 | tf_op jit(solution)/shard_map/ppermute | solution.py:309
  34.9 6.8 %collective-permute-start.15 = (bf16[2,4,32,256]{3,2,1,0:T(8,128)(2,1)S(1)}, bf16[2,4,32,256]{3,2,1,0:T(8,128)(2,1)S(1)}, u32[]{:S(2)}, u32[]{:S(2)}) collective-permute-start(bf16[2,4,32,256]{3,2,1,0:T(8,128)(2,1)S(1)} %get-tuple-element.45), channel_id=1, source_target_pairs={{0,2},{1,3},{2,0},{3,1},{4,6},{5,7},{6,4},{7,5},{8,10},{9,11},{10,... | collective-permute-start | bytes 393224 | tf_op jit(solution)/shard_map/ppermute | solution.py:173
  36.7 10.7 %collective-permute-start.17 = (bf16[2,4,32,256]{3,2,1,0:T(8,128)(2,1)S(1)}, bf16[2,4,32,256]{3,2,1,0:T(8,128)(2,1)S(1)}, u32[]{:S(2)}, u32[]{:S(2)}) collective-permute-start(bf16[2,4,32,256]{3,2,1,0:T(8,128)(2,1)S(1)} %get-tuple-element.46), channel_id=1, source_target_pairs={{0,1},{1,0},{2,3},{3,2},{4,5},{5,4},{6,7},{7,6},{8,9},{9,8},{10,11... | collective-permute-start | bytes 393224 | tf_op jit(solution)/shard_map/ppermute | solution.py:173
  37.3 10.1 %collective-permute-start.16 = (bf16[2,4,32,256]{3,2,1,0:T(8,128)(2,1)S(1)}, bf16[2,4,32,256]{3,2,1,0:T(8,128)(2,1)S(1)}, u32[]{:S(2)}, u32[]{:S(2)}) collective-permute-start(bf16[2,4,32,256]{3,2,1,0:T(8,128)(2,1)S(1)} %get-tuple-element.47), channel_id=1, source_target_pairs={{0,3},{1,2},{2,1},{3,0},{4,7},{5,6},{6,5},{7,4},{8,11},{9,10},{10,... | collective-permute-start | bytes 393224 | tf_op jit(solution)/shard_map/ppermute | solution.py:173
  38.4 10.3 %collective-permute-start.13 = (bf16[2,4,32,256]{3,2,1,0:T(8,128)(2,1)S(1)}, bf16[2,4,32,256]{3,2,1,0:T(8,128)(2,1)S(1)}, u32[]{:S(2)}, u32[]{:S(2)}) collective-permute-start(bf16[2,4,32,256]{3,2,1,0:T(8,128)(2,1)S(1)} %get-tuple-element.48), channel_id=1, source_target_pairs={{0,1},{1,0},{2,3},{3,2},{4,5},{5,4},{6,7},{7,6},{8,9},{9,8},{10,11... | collective-permute-start | bytes 393224 | tf_op jit(solution)/shard_map/ppermute | solution.py:173
  40.0 10.6 %collective-permute-start.12 = (bf16[2,4,32,256]{3,2,1,0:T(8,128)(2,1)S(1)}, bf16[2,4,32,256]{3,2,1,0:T(8,128)(2,1)S(1)}, u32[]{:S(2)}, u32[]{:S(2)}) collective-permute-start(bf16[2,4,32,256]{3,2,1,0:T(8,128)(2,1)S(1)} %get-tuple-element.49), channel_id=1, source_target_pairs={{0,3},{1,2},{2,1},{3,0},{4,7},{5,6},{6,5},{7,4},{8,11},{9,10},{10,... | collective-permute-start | bytes 393224 | tf_op jit(solution)/shard_map/ppermute | solution.py:173
  41.7 8.9 %collective-permute-start.11 = (bf16[2,4,32,256]{3,2,1,0:T(8,128)(2,1)S(1)}, bf16[2,4,32,256]{3,2,1,0:T(8,128)(2,1)S(1)}, u32[]{:S(2)}, u32[]{:S(2)}) collective-permute-start(bf16[2,4,32,256]{3,2,1,0:T(8,128)(2,1)S(1)} %get-tuple-element.50), channel_id=1, source_target_pairs={{0,2},{1,3},{2,0},{3,1},{4,6},{5,7},{6,4},{7,5},{8,10},{9,11},{10,... | collective-permute-start | bytes 393224 | tf_op jit(solution)/shard_map/ppermute | solution.py:173
  42.2 13.4 %all-to-all-start.1 = ((bf16[16,8,640]{2,1,0:T(8,128)(2,1)}), bf16[16,8,640]{2,1,0:T(8,128)(2,1)S(1)}, u32[]{:S(2)}, u32[]{:S(2)}) async-start(bf16[16,8,640]{2,1,0:T(8,128)(2,1)} %bitcast.17), calls=%async_computation.1 | async-start | bytes 327680 | tf_op jit(solution)/shard_map/all_to_all | solution.py:306
  50.8 6.6 %collective-permute-start.19 = (bf16[4,32,256]{2,1,0:T(8,128)(2,1)S(1)}, bf16[4,32,256]{2,1,0:T(8,128)(2,1)S(1)}, u32[]{:S(2)}, u32[]{:S(2)}) collective-permute-start(bf16[4,32,256]{2,1,0:T(8,128)(2,1)S(1)} %get-tuple-element.51), channel_id=1, source_target_pairs={{0,12},{1,13},{2,14},{3,15},{4,8},{5,9},{6,10},{7,11},{8,4},{9,5},... | collective-permute-start | bytes 196616 | tf_op jit(solution)/shard_map/ppermute | solution.py:173
  53.4 5.9 %collective-permute-start.14 = (bf16[4,32,256]{2,1,0:T(8,128)(2,1)S(1)}, bf16[4,32,256]{2,1,0:T(8,128)(2,1)S(1)}, u32[]{:S(2)}, u32[]{:S(2)}) collective-permute-start(bf16[4,32,256]{2,1,0:T(8,128)(2,1)S(1)} %fusion.6), channel_id=1, source_target_pairs={{0,4},{1,5},{2,6},{3,7},{4,0},{5,1},{6,2},{7,3},{8,12},{9,13},{10,... | collective-permute-start | bytes 196616 | tf_op jit(solution)/shard_map/ppermute | solution.py:173
  53.5 5.8 %collective-permute-start.18 = (bf16[4,32,256]{2,1,0:T(8,128)(2,1)S(1)}, bf16[4,32,256]{2,1,0:T(8,128)(2,1)S(1)}, u32[]{:S(2)}, u32[]{:S(2)}) collective-permute-start(bf16[4,32,256]{2,1,0:T(8,128)(2,1)S(1)} %get-tuple-element.52), channel_id=1, source_target_pairs={{0,8},{1,9},{2,10},{3,11},{4,12},{5,13},{6,14},{7,15},{8,0},{9,1},... | collective-permute-start | bytes 196616 | tf_op jit(solution)/shard_map/ppermute | solution.py:173
  57.5 1.2 %collective-permute-start.20 = (f32[512]{0:T(512)S(1)}, f32[512]{0:T(512)S(1)}, u32[]{:S(2)}, u32[]{:S(2)}) collective-permute-start(f32[512]{0:T(512)S(1)} %reduce_sum.9), channel_id=1, source_target_pairs={{0,16},{16,0},{1,17},{17,1},{2,18},{18,2},{3,19},{19,3},{4,20},{20... | collective-permute-start | bytes 6152 | tf_op jit(solution)/shard_map/ppermute | solution.py:315

commit v9 on v8

--- a/solution.py
+++ b/solution.py
@@ -163,6 +163,12 @@
         pick(normed, group, groups, norm_s),
         pick(att_ref[...], group, groups, att_s),
     )
+
+
+def finish_kernel(count, factor, *refs):
+    terms, gains, (total_ref, gain_ref) = refs[:count], refs[count:-2], refs[-2:]
+    total_ref[...] = sum(term[...].astype(F32) for term in terms) * factor
+    gain_ref[...] = sum(gain[...] for gain in gains) * factor
 
 
 def ring(size, step):
@@ -312,16 +318,24 @@
     grad_fields = back[:, :width].reshape(count, trk_dev, width)
     gain_sum = jnp.sum(back[:, width:].astype(F32).reshape(count, 2, width), (0, 1))
     if groups == 2:
-        gain_sum = gain_sum + lax.ppermute(gain_sum, "grp", ring(2, 1))
+        gains = [gain_sum, lax.ppermute(gain_sum, "grp", ring(2, 1))]
     else:
-        gain_sum = jnp.sum(lax.all_gather(gain_sum, "grp"), 0)
+        gains = [jnp.sum(lax.all_gather(gain_sum, "grp"), 0)]
     factor = float(cell_count) ** (-0.5)
-    gain_sum = gain_sum * factor
-    terms[1], terms[2], grad_fields, gain_sum = lax.optimization_barrier(
-        (terms[1], terms[2], grad_fields, gain_sum)
+    terms[1], terms[2], grad_fields, gains[0] = lax.optimization_barrier(
+        (terms[1], terms[2], grad_fields, gains[0])
     )
-    total = sum(term.astype(F32) for term in terms)
-    return (grad_fields, total.transpose(0, 2, 1) * factor, gain_sum)
+    total, gain_sum = pl.pallas_call(
+        functools.partial(finish_kernel, len(terms), factor),
+        out_shape=(
+            jax.ShapeDtypeStruct(terms[0].shape, F32),
+            jax.ShapeDtypeStruct((1, width), F32),
+        ),
+        in_specs=[vmem] * (len(terms) + len(gains)),
+        out_specs=(vmem, vmem),
+        compiler_params=pltpu.CompilerParams(vmem_limit_bytes=16 * 2**20),
+    )(*[term.astype(F32) if narrow else term for term in terms], *[gain[None] for gain in gains])
+    return (grad_fields, total.transpose(0, 2, 1), gain_sum[0])
 
 
 def solution(mesh):

time: 60.4 us -> 60 us (level)
  other arithmetic: 3.69 us -> 2.4 us
  Pallas kernels: 4.34 us -> 5.03 us
    mul x2 -> x0, other arithmetic: 1.27 us -> none  [the longest x1 0.69 us: shards(): return (grad_fields, total.transpose(0, 2, 1) * factor, gain_sum)]
    pallas_call x0 -> x1, Pallas kernels: none -> 0.69 us  [shards(): pl.pallas_call(functools.partial(finish_kernel, len(terms), factor), out_...]
    ppermute x15, waiting for transfers between devices: 13.4 us -> 14.1 us  [swap(): lax.ppermute(array, axis, [(i, i ^ bits) for i in range(lax.axis_size(axi...]
  transfers between devices with their start and end apart: 23 -> 23, of which waited for: 11 -> 11; matrix products, arithmetic and copies ran while one was open for 7% -> 6% of each run, Pallas kernels for 3% -> 3%
where the time goes in v9:
time: 60 us; the launch traced here: 59.6 us
  starting transfers between devices  32.2 us (54%)
  waiting for transfers between devices  16.8 us (28%)
  Pallas kernels  5.03 us (8%)
  other arithmetic  2.4 us (4%)
  local copies, waits for them, and re-layouts  2.34 us (4%)
  between operations  0.78 us (1%)
    ppermute x15, starting transfers between devices, swap(): lax.ppermute(array, axis, [(i, i ^ bits) for i in range(lax.axis_size(axi...  21.2 us
    ppermute x15, waiting for transfers between devices, swap(): lax.ppermute(array, axis, [(i, i ^ bits) for i in range(lax.axis_size(axi...  14.1 us
    all_to_all x1, starting transfers between devices, shards(): row = lax.all_to_all(both, 'trk', split_axis=0, concat_axis=0, tiled=True)  5.42 us
    all_to_all x1, starting transfers between devices, shards(): back = lax.all_to_all(cells, 'trk', split_axis=0, concat_axis=0, tiled=True)  5.13 us
    pallas_call x1, Pallas kernels, shards(): pl.pallas_call(functools.partial(attend_kernel, groups, offsets), out_sha...  2.52 us
    pallas_call x1, Pallas kernels, shards(): pl.pallas_call(functools.partial(cells_kernel, groups), out_shape=(wg_sha...  1.79 us
    concatenate x1, other arithmetic, shards(): both = jnp.concatenate([fields, upstream], 1)  1.69 us
    all_to_all x1, waiting for transfers between devices, shards(): row = lax.all_to_all(both, 'trk', split_axis=0, concat_axis=0, tiled=True)  1.52 us
  transfers between devices with their start and end apart: 23, of which 11 were waited for; matrix products, arithmetic and copies ran while one was open for 6% of the time, Pallas kernels for 3%

profile of v9, /device:TPU:0, one launch (start us, length us, event | category | flops | bytes accessed | tf_op | source)
XLA Modules:
  0.0 59.6 jit_solution(6776093119433772681)
XLA Ops:
  0.6 5.1 %collective-permute-start.2 = (bf16[1,4,32,256]{3,2,1,0:T(8,128)(2,1)}, bf16[1,4,32,256]{3,2,1,0:T(8,128)(2,1)S(1)}, u32[]{:S(2)}, u32[]{:S(2)}) collective-permute-start(bf16[1,4,32,256]{3,2,1,0:T(8,128)(2,1)} %bitcast.44), channel_id=1, source_target_pairs={{0,12},{1,13},{2,14},{3,15},{4,8},{5,9},{6,10},{7,11},{8,4},{9,5},... | collective-permute-start | bytes 196616 | tf_op jit(solution)/shard_map/ppermute | solution.py:179
  5.7 0.0 collective-permute-start.1
  5.7 0.6 %collective-permute-start = (bf16[1,4,32,256]{3,2,1,0:T(8,128)(2,1)}, bf16[1,4,32,256]{3,2,1,0:T(8,128)(2,1)S(1)}, u32[]{:S(2)}, u32[]{:S(2)}) collective-permute-start(bf16[1,4,32,256]{3,2,1,0:T(8,128)(2,1)} %bitcast.46), channel_id=1, source_target_pairs={{0,8},{1,9},{2,10},{3,11},{4,12},{5,13},{6,14},{7,15},{8,0},{9,1},... | collective-permute-start | bytes 196616 | tf_op jit(solution)/shard_map/ppermute | solution.py:179
  6.4 0.0 copy-start
  6.4 0.9 %copy-done = bf16[4,256,32]{1,2,0:T(8,128)(2,1)S(1)} copy-done((bf16[4,256,32]{1,2,0:T(8,128)(2,1)S(1)}, bf16[4,256,32]{1,2,0:T(8,128)(2,1)}, u32[]{:S(2)}) %copy-start) | copy-done | bytes 65560
  7.3 1.7 %pad_maximum_fusion = bf16[16,16,512]{2,1,0:T(8,128)(2,1)} fusion(bf16[16,8,512]{2,1,0:T(8,128)(2,1)} %param.5, bf16[16,8,512]{2,1,0:T(8,128)(2,1)} %param.4), kind=kLoop, calls=%fused_computation.1 | loop fusion | flops 524288 | bytes 524288 | tf_op jit(solution)/shard_map/concatenate | solution.py:260
  9.0 0.1 pad_add_fusion.place
  9.0 0.7 %broadcast_in_dim.12.gain_ref = f32[8,512]{1,0:T(8,128)S(1)} broadcast(f32[512]{0:T(512)} %param.6), dimensions={1} | broadcast | bytes 18432 | tf_op jit(solution)/shard_map/broadcast_in_dim | solution.py:261
  9.7 1.9 %collective-permute-done.refs_1_ = bf16[1,4,32,256]{3,2,1,0:T(8,128)(2,1)S(1)} collective-permute-done((bf16[1,4,32,256]{3,2,1,0:T(8,128)(2,1)}, bf16[1,4,32,256]{3,2,1,0:T(8,128)(2,1)S(1)}, u32[]{:S(2)}, u32[]{:S(2)}) %collective-permute-start) | collective-permute-done | bytes 65568 | tf_op jit(solution)/shard_map/ppermute | solution.py:179
  11.6 0.0 collective-permute-done.2.refs_3_
  11.6 0.0 collective-permute-done.1.refs_2_
  11.6 2.5 %collective-permute-start.5 = (bf16[4,4,32,256]{3,2,1,0:T(8,128)(2,1)S(1)}, bf16[4,4,32,256]{3,2,1,0:T(8,128)(2,1)S(1)}, u32[]{:S(2)}, u32[]{:S(2)}) collective-permute-start(bf16[4,4,32,256]{3,2,1,0:T(8,128)(2,1)S(1)} %shard_map.68.refs_0_), channel_id=1, source_target_pairs={{0,3},{1,2},{2,1},{3,0},{4,7},{5,6},{6,5},{7,4},{8,11},{9,10},{10,... | collective-permute-start | bytes 786440 | tf_op jit(solution)/shard_map/ppermute | solution.py:179
  14.1 0.5 collective-permute-start.4
  14.6 0.5 collective-permute-start.3
  15.2 5.4 %all-to-all-start = ((bf16[16,16,512]{2,1,0:T(8,128)(2,1)}), bf16[16,16,512]{2,1,0:T(8,128)(2,1)S(1)}, u32[]{:S(2)}, u32[]{:S(2)}) async-start(bf16[16,16,512]{2,1,0:T(8,128)(2,1)} %pad_maximum_fusion), calls=%async_computation | async-start | bytes 524288 | tf_op jit(solution)/shard_map/all_to_all | solution.py:265
  20.6 0.1 collective-permute-start.6
  20.7 1.2 %collective-permute-done.5.refs_3_ = bf16[4,4,32,256]{3,2,1,0:T(8,128)(2,1)S(1)} collective-permute-done((bf16[4,4,32,256]{3,2,1,0:T(8,128)(2,1)S(1)}, bf16[4,4,32,256]{3,2,1,0:T(8,128)(2,1)S(1)}, u32[]{:S(2)}, u32[]{:S(2)}) %collective-permute-start.5) | collective-permute-done | bytes 262176 | tf_op jit(solution)/shard_map/ppermute | solution.py:179
  21.8 0.0 collective-permute-start.9
  21.9 5.2 %collective-permute-done.4.refs_2_ = bf16[4,4,32,256]{3,2,1,0:T(8,128)(2,1)S(1)} collective-permute-done((bf16[4,4,32,256]{3,2,1,0:T(8,128)(2,1)S(1)}, bf16[4,4,32,256]{3,2,1,0:T(8,128)(2,1)S(1)}, u32[]{:S(2)}, u32[]{:S(2)}) %collective-permute-start.4) | collective-permute-done | bytes 262176 | tf_op jit(solution)/shard_map/ppermute | solution.py:179
  27.1 0.0 collective-permute-start.8
  27.1 0.2 collective-permute-done.3.refs_1_
  27.3 0.3 collective-permute-start.7
  27.6 0.0 collective-permute-done.6.refs_4_
  27.6 1.5 %all-to-all-done.rows_ref = bf16[16,16,512]{2,1,0:T(8,128)(2,1)S(1)} async-done(((bf16[16,16,512]{2,1,0:T(8,128)(2,1)}), bf16[16,16,512]{2,1,0:T(8,128)(2,1)S(1)}, u32[]{:S(2)}, u32[]{:S(2)}) %all-to-all-start) | async-done | bytes 262176 | tf_op jit(solution)/shard_map/all_to_all | solution.py:265
  29.1 0.0 collective-permute-done.9.refs_7_
  29.1 0.0 collective-permute-done.8.refs_6_
  29.1 0.0 collective-permute-done.7.refs_5_
  29.1 2.5 %shard_map.69 = (bf16[16,4,32,256]{3,2,1,0:T(8,128)(2,1)S(1)}, bf16[3,128,512]{2,1,0:T(8,128)(2,1)S(1)}, bf16[128,512]{1,0:T(8,128)(2,1)S(1)}, bf16[4,512,512]{2,1,0:T(8,128)(2,1)S(1)}, f32[1,512]{1,0:T(1,128)S(1)}) custom-call(s32[2]{0:T(128)S(1)} %pad_add_fusion.place, bf16[16,16,512]{2,1,0:T(8,128)(2,1)S(1)} %all-to-all-done.rows_ref, ...), custom_call_target="tpu_custom_call" | custom-call | tf_op jit(solution)/shard_map/pallas_call | solution.py:281
  31.6 0.1 collective-permute-start.10
  31.7 1.8 %shard_map.70 = (bf16[16,4,32,256]{3,2,1,0:T(8,128)(2,1)S(1)}, bf16[128,640]{1,0:T(8,128)(2,1)}) custom-call(s32[2]{0:T(128)S(1)} %pad_add_fusion.place, bf16[16,16,512]{2,1,0:T(8,128)(2,1)S(1)} %all-to-all-done.rows_ref, f32[1,512]{1,0:T(1,128)S(1)} %get-tuple-element.32.gain_ref, bf16[4,512,512]{2,1,0:T(8,128)(2,1)S(1)} %get-tuple-element.33.w_all, ...), custom_call_target="tpu_custom_call" | custom-call | flops 335544320 | bytes 4194304 | tf_op jit(solution)/shard_map/pallas_call | solution.py:295
  33.5 0.9 %collective-permute-done.10 = bf16[16,4,32,256]{3,2,1,0:T(8,128)(2,1)S(1)} collective-permute-done((bf16[16,4,32,256]{3,2,1,0:T(8,128)(2,1)S(1)}, bf16[16,4,32,256]{3,2,1,0:T(8,128)(2,1)S(1)}, u32[]{:S(2)}, u32[]{:S(2)}) %collective-permute-start.10) | collective-permute-done | bytes 1048608 | tf_op jit(solution)/shard_map/ppermute | solution.py:315
  34.4 0.4 add_convert_fusion
  34.8 0.1 slice_bitcast_fusion.3
  34.9 1.8 %collective-permute-start.15 = (bf16[2,4,32,256]{3,2,1,0:T(8,128)(2,1)S(1)}, bf16[2,4,32,256]{3,2,1,0:T(8,128)(2,1)S(1)}, u32[]{:S(2)}, u32[]{:S(2)}) collective-permute-start(bf16[2,4,32,256]{3,2,1,0:T(8,128)(2,1)S(1)} %get-tuple-element.49), channel_id=1, source_target_pairs={{0,2},{1,3},{2,0},{3,1},{4,6},{5,7},{6,4},{7,5},{8,10},{9,11},{10,... | collective-permute-start | bytes 393224 | tf_op jit(solution)/shard_map/ppermute | solution.py:179
  36.7 0.6 collective-permute-start.17
  37.3 1.1 %collective-permute-start.16 = (bf16[2,4,32,256]{3,2,1,0:T(8,128)(2,1)S(1)}, bf16[2,4,32,256]{3,2,1,0:T(8,128)(2,1)S(1)}, u32[]{:S(2)}, u32[]{:S(2)}) collective-permute-start(bf16[2,4,32,256]{3,2,1,0:T(8,128)(2,1)S(1)} %get-tuple-element.51), channel_id=1, source_target_pairs={{0,3},{1,2},{2,1},{3,0},{4,7},{5,6},{6,5},{7,4},{8,11},{9,10},{10,... | collective-permute-start | bytes 393224 | tf_op jit(solution)/shard_map/ppermute | solution.py:179
  38.4 1.6 %collective-permute-start.13 = (bf16[2,4,32,256]{3,2,1,0:T(8,128)(2,1)S(1)}, bf16[2,4,32,256]{3,2,1,0:T(8,128)(2,1)S(1)}, u32[]{:S(2)}, u32[]{:S(2)}) collective-permute-start(bf16[2,4,32,256]{3,2,1,0:T(8,128)(2,1)S(1)} %get-tuple-element.52), channel_id=1, source_target_pairs={{0,1},{1,0},{2,3},{3,2},{4,5},{5,4},{6,7},{7,6},{8,9},{9,8},{10,11... | collective-permute-start | bytes 393224 | tf_op jit(solution)/shard_map/ppermute | solution.py:179
  40.0 1.6 %collective-permute-start.12 = (bf16[2,4,32,256]{3,2,1,0:T(8,128)(2,1)S(1)}, bf16[2,4,32,256]{3,2,1,0:T(8,128)(2,1)S(1)}, u32[]{:S(2)}, u32[]{:S(2)}) collective-permute-start(bf16[2,4,32,256]{3,2,1,0:T(8,128)(2,1)S(1)} %get-tuple-element.53), channel_id=1, source_target_pairs={{0,3},{1,2},{2,1},{3,0},{4,7},{5,6},{6,5},{7,4},{8,11},{9,10},{10,... | collective-permute-start | bytes 393224 | tf_op jit(solution)/shard_map/ppermute | solution.py:179
  41.7 0.0 collective-permute-done.15
  41.7 0.6 collective-permute-start.11
  42.2 5.1 %all-to-all-start.1 = ((bf16[16,8,640]{2,1,0:T(8,128)(2,1)}), bf16[16,8,640]{2,1,0:T(8,128)(2,1)S(1)}, u32[]{:S(2)}, u32[]{:S(2)}) async-start(bf16[16,8,640]{2,1,0:T(8,128)(2,1)} %bitcast.17), calls=%async_computation.1 | async-start | bytes 327680 | tf_op jit(solution)/shard_map/all_to_all | solution.py:312
  47.4 0.0 collective-permute-done.17
  47.4 0.0 collective-permute-done.16
  47.4 1.3 %collective-permute-done.13 = bf16[2,4,32,256]{3,2,1,0:T(8,128)(2,1)S(1)} collective-permute-done((bf16[2,4,32,256]{3,2,1,0:T(8,128)(2,1)S(1)}, bf16[2,4,32,256]{3,2,1,0:T(8,128)(2,1)S(1)}, u32[]{:S(2)}, u32[]{:S(2)}) %collective-permute-start.13) | collective-permute-done | bytes 131104 | tf_op jit(solution)/shard_map/ppermute | solution.py:179
  48.7 1.9 %collective-permute-done.12 = bf16[2,4,32,256]{3,2,1,0:T(8,128)(2,1)S(1)} collective-permute-done((bf16[2,4,32,256]{3,2,1,0:T(8,128)(2,1)S(1)}, bf16[2,4,32,256]{3,2,1,0:T(8,128)(2,1)S(1)}, u32[]{:S(2)}, u32[]{:S(2)}) %collective-permute-start.12) | collective-permute-done | bytes 131104 | tf_op jit(solution)/shard_map/ppermute | solution.py:179
  50.6 0.0 collective-permute-done.11
  50.6 0.2 fusion
  50.8 2.6 %collective-permute-start.19 = (bf16[4,32,256]{2,1,0:T(8,128)(2,1)S(1)}, bf16[4,32,256]{2,1,0:T(8,128)(2,1)S(1)}, u32[]{:S(2)}, u32[]{:S(2)}) collective-permute-start(bf16[4,32,256]{2,1,0:T(8,128)(2,1)S(1)} %get-tuple-element.55), channel_id=1, source_target_pairs={{0,12},{1,13},{2,14},{3,15},{4,8},{5,9},{6,10},{7,11},{8,4},{9,5},... | collective-permute-start | bytes 196616 | tf_op jit(solution)/shard_map/ppermute | solution.py:179
  53.4 0.1 collective-permute-start.14
  53.5 1.8 %collective-permute-start.18 = (bf16[4,32,256]{2,1,0:T(8,128)(2,1)S(1)}, bf16[4,32,256]{2,1,0:T(8,128)(2,1)S(1)}, u32[]{:S(2)}, u32[]{:S(2)}) collective-permute-start(bf16[4,32,256]{2,1,0:T(8,128)(2,1)S(1)} %get-tuple-element.56), channel_id=1, source_target_pairs={{0,8},{1,9},{2,10},{3,11},{4,12},{5,13},{6,14},{7,15},{8,0},{9,1},... | collective-permute-start | bytes 196616 | tf_op jit(solution)/shard_map/ppermute | solution.py:179
  55.3 0.3 all-to-all-done.1
  55.7 1.8 %collective-permute-done.19.refs_3_ = bf16[4,32,256]{2,1,0:T(8,128)(2,1)S(1)} collective-permute-done((bf16[4,32,256]{2,1,0:T(8,128)(2,1)S(1)}, bf16[4,32,256]{2,1,0:T(8,128)(2,1)S(1)}, u32[]{:S(2)}, u32[]{:S(2)}) %collective-permute-start.19) | collective-permute-done | bytes 65568 | tf_op jit(solution)/shard_map/ppermute | solution.py:179
  57.5 0.1 collective-permute-start.20
  57.6 0.7 %slice_bitcast_fusion.9 = bf16[16,8,512]{2,1,0:T(8,128)(2,1)} fusion(bf16[128,640]{1,0:T(8,128)(2,1)S(1)} %bitcast.53), kind=kLoop, calls=%fused_computation.15 | loop fusion | bytes 262144 | tf_op jit(solution)/shard_map/reshape | solution.py:318
  58.3 0.0 collective-permute-done.14.refs_1_
  58.3 0.6 collective-permute-done.18.refs_2_
  58.9 0.0 collective-permute-done.20
  58.9 0.7 %shard_map.71 = (f32[4,32,256]{2,1,0:T(8,128)}, f32[1,512]{1,0:T(1,128)}) custom-call(f32[4,32,256]{2,1,0:T(8,128)S(1)} %slice_bitcast_fusion.refs_0_, bf16[4,32,256]{2,1,0:T(8,128)(2,1)S(1)} %collective-permute-done.14.refs_1_, bf16[4,32,256]{2,1,0:T(8,128)(2,1)S(1)} %collective-permute-done.18.refs_2_, ...), custom_call_target="tpu_custom_call" | custom-call | tf_op jit(solution)/shard_map/pallas_call | solution.py:328
  (8 shorter events, 0.1 us)
Async XLA Ops:
  0.6 11.0 %collective-permute-start.2 = (bf16[1,4,32,256]{3,2,1,0:T(8,128)(2,1)}, bf16[1,4,32,256]{3,2,1,0:T(8,128)(2,1)S(1)}, u32[]{:S(2)}, u32[]{:S(2)}) collective-permute-start(bf16[1,4,32,256]{3,2,1,0:T(8,128)(2,1)} %bitcast.44), channel_id=1, source_target_pairs={{0,12},{1,13},{2,14},{3,15},{4,8},{5,9},{6,10},{7,11},{8,4},{9,5},... | collective-permute-start | bytes 196616 | tf_op jit(solution)/shard_map/ppermute | solution.py:179
  5.7 5.9 %collective-permute-start.1 = (bf16[1,4,32,256]{3,2,1,0:T(8,128)(2,1)}, bf16[1,4,32,256]{3,2,1,0:T(8,128)(2,1)S(1)}, u32[]{:S(2)}, u32[]{:S(2)}) collective-permute-start(bf16[1,4,32,256]{3,2,1,0:T(8,128)(2,1)} %bitcast.45), channel_id=1, source_target_pairs={{0,4},{1,5},{2,6},{3,7},{4,0},{5,1},{6,2},{7,3},{8,12},{9,13},{10,... | collective-permute-start | bytes 196616 | tf_op jit(solution)/shard_map/ppermute | solution.py:179
  5.7 5.8 %collective-permute-start = (bf16[1,4,32,256]{3,2,1,0:T(8,128)(2,1)}, bf16[1,4,32,256]{3,2,1,0:T(8,128)(2,1)S(1)}, u32[]{:S(2)}, u32[]{:S(2)}) collective-permute-start(bf16[1,4,32,256]{3,2,1,0:T(8,128)(2,1)} %bitcast.46), channel_id=1, source_target_pairs={{0,8},{1,9},{2,10},{3,11},{4,12},{5,13},{6,14},{7,15},{8,0},{9,1},... | collective-permute-start | bytes 196616 | tf_op jit(solution)/shard_map/ppermute | solution.py:179
  6.4 0.9 %copy-start = (bf16[4,256,32]{1,2,0:T(8,128)(2,1)S(1)}, bf16[4,256,32]{1,2,0:T(8,128)(2,1)}, u32[]{:S(2)}) copy-start(bf16[4,256,32]{1,2,0:T(8,128)(2,1)} %param.7) | copy-start | bytes 196612
  11.6 10.2 %collective-permute-start.5 = (bf16[4,4,32,256]{3,2,1,0:T(8,128)(2,1)S(1)}, bf16[4,4,32,256]{3,2,1,0:T(8,128)(2,1)S(1)}, u32[]{:S(2)}, u32[]{:S(2)}) collective-permute-start(bf16[4,4,32,256]{3,2,1,0:T(8,128)(2,1)S(1)} %shard_map.68.refs_0_), channel_id=1, source_target_pairs={{0,3},{1,2},{2,1},{3,0},{4,7},{5,6},{6,5},{7,4},{8,11},{9,10},{10,... | collective-permute-start | bytes 786440 | tf_op jit(solution)/shard_map/ppermute | solution.py:179
  14.1 12.9 %collective-permute-start.4 = (bf16[4,4,32,256]{3,2,1,0:T(8,128)(2,1)S(1)}, bf16[4,4,32,256]{3,2,1,0:T(8,128)(2,1)S(1)}, u32[]{:S(2)}, u32[]{:S(2)}) collective-permute-start(bf16[4,4,32,256]{3,2,1,0:T(8,128)(2,1)S(1)} %shard_map.68.refs_0_), channel_id=1, source_target_pairs={{0,2},{1,3},{2,0},{3,1},{4,6},{5,7},{6,4},{7,5},{8,10},{9,11},{10,... | collective-permute-start | bytes 786440 | tf_op jit(solution)/shard_map/ppermute | solution.py:179
  14.6 12.7 %collective-permute-start.3 = (bf16[4,4,32,256]{3,2,1,0:T(8,128)(2,1)S(1)}, bf16[4,4,32,256]{3,2,1,0:T(8,128)(2,1)S(1)}, u32[]{:S(2)}, u32[]{:S(2)}) collective-permute-start(bf16[4,4,32,256]{3,2,1,0:T(8,128)(2,1)S(1)} %shard_map.68.refs_0_), channel_id=1, source_target_pairs={{0,1},{1,0},{2,3},{3,2},{4,5},{5,4},{6,7},{7,6},{8,9},{9,8},{10,11... | collective-permute-start | bytes 786440 | tf_op jit(solution)/shard_map/ppermute | solution.py:179
  15.2 13.9 %all-to-all-start = ((bf16[16,16,512]{2,1,0:T(8,128)(2,1)}), bf16[16,16,512]{2,1,0:T(8,128)(2,1)S(1)}, u32[]{:S(2)}, u32[]{:S(2)}) async-start(bf16[16,16,512]{2,1,0:T(8,128)(2,1)} %pad_maximum_fusion), calls=%async_computation | async-start | bytes 524288 | tf_op jit(solution)/shard_map/all_to_all | solution.py:265
  20.6 7.0 %collective-permute-start.6 = (bf16[4,4,32,256]{3,2,1,0:T(8,128)(2,1)S(1)}, bf16[4,4,32,256]{3,2,1,0:T(8,128)(2,1)S(1)}, u32[]{:S(2)}, u32[]{:S(2)}) collective-permute-start(bf16[4,4,32,256]{3,2,1,0:T(8,128)(2,1)S(1)} %shard_map.68.refs_0_), channel_id=1, source_target_pairs={{0,16},{16,0},{1,17},{17,1},{2,18},{18,2},{3,19},{19,3},{4,20},{20... | collective-permute-start | bytes 786440 | tf_op jit(solution)/shard_map/ppermute | solution.py:272
  21.8 7.3 %collective-permute-start.9 = (bf16[4,4,32,256]{3,2,1,0:T(8,128)(2,1)S(1)}, bf16[4,4,32,256]{3,2,1,0:T(8,128)(2,1)S(1)}, u32[]{:S(2)}, u32[]{:S(2)}) collective-permute-start(bf16[4,4,32,256]{3,2,1,0:T(8,128)(2,1)S(1)} %collective-permute-done.5.refs_3_), channel_id=1, source_target_pairs={{0,16},{16,0},{1,17},{17,1},{2,18},{18,2},{3,19},{19,3},{4,20},{20... | collective-permute-start | bytes 786440 | tf_op jit(solution)/shard_map/ppermute | solution.py:272
  27.1 2.0 %collective-permute-start.8 = (bf16[4,4,32,256]{3,2,1,0:T(8,128)(2,1)S(1)}, bf16[4,4,32,256]{3,2,1,0:T(8,128)(2,1)S(1)}, u32[]{:S(2)}, u32[]{:S(2)}) collective-permute-start(bf16[4,4,32,256]{3,2,1,0:T(8,128)(2,1)S(1)} %collective-permute-done.4.refs_2_), channel_id=1, source_target_pairs={{0,16},{16,0},{1,17},{17,1},{2,18},{18,2},{3,19},{19,3},{4,20},{20... | collective-permute-start | bytes 786440 | tf_op jit(solution)/shard_map/ppermute | solution.py:272
  27.3 1.8 %collective-permute-start.7 = (bf16[4,4,32,256]{3,2,1,0:T(8,128)(2,1)S(1)}, bf16[4,4,32,256]{3,2,1,0:T(8,128)(2,1)S(1)}, u32[]{:S(2)}, u32[]{:S(2)}) collective-permute-start(bf16[4,4,32,256]{3,2,1,0:T(8,128)(2,1)S(1)} %collective-permute-done.3.refs_1_), channel_id=1, source_target_pairs={{0,16},{16,0},{1,17},{17,1},{2,18},{18,2},{3,19},{19,3},{4,20},{20... | collective-permute-start | bytes 786440 | tf_op jit(solution)/shard_map/ppermute | solution.py:272
  31.6 2.7 %collective-permute-start.10 = (bf16[16,4,32,256]{3,2,1,0:T(8,128)(2,1)S(1)}, bf16[16,4,32,256]{3,2,1,0:T(8,128)(2,1)S(1)}, u32[]{:S(2)}, u32[]{:S(2)}) collective-permute-start(bf16[16,4,32,256]{3,2,1,0:T(8,128)(2,1)S(1)} %get-tuple-element.37), channel_id=1, source_target_pairs={{0,16},{16,0},{1,17},{17,1},{2,18},{18,2},{3,19},{19,3},{4,20},{20... | collective-permute-start | bytes 3145736 | tf_op jit(solution)/shard_map/ppermute | solution.py:315
  34.9 6.8 %collective-permute-start.15 = (bf16[2,4,32,256]{3,2,1,0:T(8,128)(2,1)S(1)}, bf16[2,4,32,256]{3,2,1,0:T(8,128)(2,1)S(1)}, u32[]{:S(2)}, u32[]{:S(2)}) collective-permute-start(bf16[2,4,32,256]{3,2,1,0:T(8,128)(2,1)S(1)} %get-tuple-element.49), channel_id=1, source_target_pairs={{0,2},{1,3},{2,0},{3,1},{4,6},{5,7},{6,4},{7,5},{8,10},{9,11},{10,... | collective-permute-start | bytes 393224 | tf_op jit(solution)/shard_map/ppermute | solution.py:179
  36.7 10.7 %collective-permute-start.17 = (bf16[2,4,32,256]{3,2,1,0:T(8,128)(2,1)S(1)}, bf16[2,4,32,256]{3,2,1,0:T(8,128)(2,1)S(1)}, u32[]{:S(2)}, u32[]{:S(2)}) collective-permute-start(bf16[2,4,32,256]{3,2,1,0:T(8,128)(2,1)S(1)} %get-tuple-element.50), channel_id=1, source_target_pairs={{0,1},{1,0},{2,3},{3,2},{4,5},{5,4},{6,7},{7,6},{8,9},{9,8},{10,11... | collective-permute-start | bytes 393224 | tf_op jit(solution)/shard_map/ppermute | solution.py:179
  37.3 10.1 %collective-permute-start.16 = (bf16[2,4,32,256]{3,2,1,0:T(8,128)(2,1)S(1)}, bf16[2,4,32,256]{3,2,1,0:T(8,128)(2,1)S(1)}, u32[]{:S(2)}, u32[]{:S(2)}) collective-permute-start(bf16[2,4,32,256]{3,2,1,0:T(8,128)(2,1)S(1)} %get-tuple-element.51), channel_id=1, source_target_pairs={{0,3},{1,2},{2,1},{3,0},{4,7},{5,6},{6,5},{7,4},{8,11},{9,10},{10,... | collective-permute-start | bytes 393224 | tf_op jit(solution)/shard_map/ppermute | solution.py:179
  38.4 10.3 %collective-permute-start.13 = (bf16[2,4,32,256]{3,2,1,0:T(8,128)(2,1)S(1)}, bf16[2,4,32,256]{3,2,1,0:T(8,128)(2,1)S(1)}, u32[]{:S(2)}, u32[]{:S(2)}) collective-permute-start(bf16[2,4,32,256]{3,2,1,0:T(8,128)(2,1)S(1)} %get-tuple-element.52), channel_id=1, source_target_pairs={{0,1},{1,0},{2,3},{3,2},{4,5},{5,4},{6,7},{7,6},{8,9},{9,8},{10,11... | collective-permute-start | bytes 393224 | tf_op jit(solution)/shard_map/ppermute | solution.py:179
  40.0 10.6 %collective-permute-start.12 = (bf16[2,4,32,256]{3,2,1,0:T(8,128)(2,1)S(1)}, bf16[2,4,32,256]{3,2,1,0:T(8,128)(2,1)S(1)}, u32[]{:S(2)}, u32[]{:S(2)}) collective-permute-start(bf16[2,4,32,256]{3,2,1,0:T(8,128)(2,1)S(1)} %get-tuple-element.53), channel_id=1, source_target_pairs={{0,3},{1,2},{2,1},{3,0},{4,7},{5,6},{6,5},{7,4},{8,11},{9,10},{10,... | collective-permute-start | bytes 393224 | tf_op jit(solution)/shard_map/ppermute | solution.py:179
  41.7 8.9 %collective-permute-start.11 = (bf16[2,4,32,256]{3,2,1,0:T(8,128)(2,1)S(1)}, bf16[2,4,32,256]{3,2,1,0:T(8,128)(2,1)S(1)}, u32[]{:S(2)}, u32[]{:S(2)}) collective-permute-start(bf16[2,4,32,256]{3,2,1,0:T(8,128)(2,1)S(1)} %get-tuple-element.54), channel_id=1, source_target_pairs={{0,2},{1,3},{2,0},{3,1},{4,6},{5,7},{6,4},{7,5},{8,10},{9,11},{10,... | collective-permute-start | bytes 393224 | tf_op jit(solution)/shard_map/ppermute | solution.py:179
  42.2 13.4 %all-to-all-start.1 = ((bf16[16,8,640]{2,1,0:T(8,128)(2,1)}), bf16[16,8,640]{2,1,0:T(8,128)(2,1)S(1)}, u32[]{:S(2)}, u32[]{:S(2)}) async-start(bf16[16,8,640]{2,1,0:T(8,128)(2,1)} %bitcast.17), calls=%async_computation.1 | async-start | bytes 327680 | tf_op jit(solution)/shard_map/all_to_all | solution.py:312
  50.8 6.6 %collective-permute-start.19 = (bf16[4,32,256]{2,1,0:T(8,128)(2,1)S(1)}, bf16[4,32,256]{2,1,0:T(8,128)(2,1)S(1)}, u32[]{:S(2)}, u32[]{:S(2)}) collective-permute-start(bf16[4,32,256]{2,1,0:T(8,128)(2,1)S(1)} %get-tuple-element.55), channel_id=1, source_target_pairs={{0,12},{1,13},{2,14},{3,15},{4,8},{5,9},{6,10},{7,11},{8,4},{9,5},... | collective-permute-start | bytes 196616 | tf_op jit(solution)/shard_map/ppermute | solution.py:179
  53.4 4.8 %collective-permute-start.14 = (bf16[4,32,256]{2,1,0:T(8,128)(2,1)S(1)}, bf16[4,32,256]{2,1,0:T(8,128)(2,1)S(1)}, u32[]{:S(2)}, u32[]{:S(2)}) collective-permute-start(bf16[4,32,256]{2,1,0:T(8,128)(2,1)S(1)} %fusion.1), channel_id=1, source_target_pairs={{0,4},{1,5},{2,6},{3,7},{4,0},{5,1},{6,2},{7,3},{8,12},{9,13},{10,... | collective-permute-start | bytes 196616 | tf_op jit(solution)/shard_map/ppermute | solution.py:179
  53.5 5.3 %collective-permute-start.18 = (bf16[4,32,256]{2,1,0:T(8,128)(2,1)S(1)}, bf16[4,32,256]{2,1,0:T(8,128)(2,1)S(1)}, u32[]{:S(2)}, u32[]{:S(2)}) collective-permute-start(bf16[4,32,256]{2,1,0:T(8,128)(2,1)S(1)} %get-tuple-element.56), channel_id=1, source_target_pairs={{0,8},{1,9},{2,10},{3,11},{4,12},{5,13},{6,14},{7,15},{8,0},{9,1},... | collective-permute-start | bytes 196616 | tf_op jit(solution)/shard_map/ppermute | solution.py:179
  57.5 1.3 %collective-permute-start.20 = (f32[512]{0:T(512)S(1)}, f32[512]{0:T(512)S(1)}, u32[]{:S(2)}, u32[]{:S(2)}) collective-permute-start(f32[512]{0:T(512)S(1)} %reduce_sum.9), channel_id=1, source_target_pairs={{0,16},{16,0},{1,17},{17,1},{2,18},{18,2},{3,19},{19,3},{4,20},{20... | collective-permute-start | bytes 6152 | tf_op jit(solution)/shard_map/ppermute | solution.py:321

commit v10 on v9

--- a/solution.py
+++ b/solution.py
@@ -227,8 +227,12 @@
     moved[0], other = lax.optimization_barrier((moved[0], other))
     held = stack_blocks([held] + moved)
     order = order + [offset ^ bits for bits in far for offset in order]
-    parts = [swap(held, axis, bits) if bits else held for bits in range(4)]
-    return parts, [[offset ^ bits for offset in order] for bits in range(4)], other
+    first, second = swap(held, axis, 1), swap(held, axis, 2)
+    half = len(order) // 2
+    parts = [held, first, second, swap(first[:half], axis, 2), swap(second[half:], axis, 1)]
+    where = [order, [o ^ 1 for o in order], [o ^ 2 for o in order]]
+    where += [[o ^ 3 for o in order[:half]], [o ^ 3 for o in order[half:]]]
+    return parts, where, other
 
 
 def scatter_sum(blocks, axis):
@@ -236,11 +240,11 @@
     blocks = blocks.reshape((4, count // 4) + blocks.shape[1:])
     half = blocks.shape[1] // 2
 
-    def plane_sum(blocks):
-        moved = [swap(blocks[bits], axis, bits) for bits in (2, 3, 1)]
+    def plane_sum(blocks, order):
+        moved = [swap(blocks[bits], axis, bits) for bits in order]
         return blocks[0].astype(F32) + sum(block.astype(F32) for block in moved)
 
-    far, close = plane_sum(blocks[:, half:]), plane_sum(blocks[:, :half])
+    far, close = plane_sum(blocks[:, half:], (1, 3, 2)), plane_sum(blocks[:, :half], (3, 1, 2))
     bit = count // 2
     while bit > 8:
         total = close + swap(far.astype(BF), axis, bit).astype(F32)

time: 60 us -> 59.7 us (level)
  waiting for transfers between devices: 16.8 us -> 15.7 us
  starting transfers between devices: 32.2 us -> 33 us
    ppermute x15 -> x16, starting transfers between devices: 21.2 us -> 23.2 us  [swap(): lax.ppermute(array, axis, [(i, i ^ bits) for i in range(lax.axis_size(axi...]
    all_to_all x1, starting transfers between devices: 5.42 us -> 3.55 us  [shards(): row = lax.all_to_all(both, 'trk', split_axis=0, concat_axis=0, tiled=True)]
    ppermute x15 -> x16, waiting for transfers between devices: 14.1 us -> 12.5 us  [swap(): lax.ppermute(array, axis, [(i, i ^ bits) for i in range(lax.axis_size(axi...]
    all_to_all x1, waiting for transfers between devices: 1.52 us -> 0.01 us  [shards(): row = lax.all_to_all(both, 'trk', split_axis=0, concat_axis=0, tiled=True)]
    ppermute x4 -> x5, waiting for transfers between devices: 0.01 us -> 1.32 us  [shards(): lax.ppermute(held, 'grp', ring(groups, k))]
    all_to_all x1, waiting for transfers between devices: 0.32 us -> 1.15 us  [shards(): back = lax.all_to_all(cells, 'trk', split_axis=0, concat_axis=0, tiled=True)]
  transfers between devices with their start and end apart: 23 -> 25, of which waited for: 11 -> 12; matrix products, arithmetic and copies ran while one was open for 6% -> 6% of each run, Pallas kernels for 3% -> 3%
where the time goes in v10:
time: 59.7 us; the launch traced here: 59.3 us
  starting transfers between devices  33 us (55%)
  waiting for transfers between devices  15.7 us (26%)
  Pallas kernels  5.01 us (8%)
  other arithmetic  2.41 us (4%)
  local copies, waits for them, and re-layouts  2.36 us (4%)
  between operations  0.79 us (1%)
    ppermute x16, starting transfers between devices, swap(): lax.ppermute(array, axis, [(i, i ^ bits) for i in range(lax.axis_size(axi...  23.2 us
    ppermute x16, waiting for transfers between devices, swap(): lax.ppermute(array, axis, [(i, i ^ bits) for i in range(lax.axis_size(axi...  12.5 us
    all_to_all x1, starting transfers between devices, shards(): back = lax.all_to_all(cells, 'trk', split_axis=0, concat_axis=0, tiled=True)  5.3 us
    all_to_all x1, starting transfers between devices, shards(): row = lax.all_to_all(both, 'trk', split_axis=0, concat_axis=0, tiled=True)  3.55 us
    pallas_call x1, Pallas kernels, shards(): pl.pallas_call(functools.partial(attend_kernel, groups, offsets), out_sha...  2.5 us
    pallas_call x1, Pallas kernels, shards(): pl.pallas_call(functools.partial(cells_kernel, groups), out_shape=(wg_sha...  1.78 us
    concatenate x1, other arithmetic, shards(): both = jnp.concatenate([fields, upstream], 1)  1.7 us
    ppermute x5, waiting for transfers between devices, shards(): lax.ppermute(held, 'grp', ring(groups, k))  1.32 us
  transfers between devices with their start and end apart: 25, of which 12 were waited for; matrix products, arithmetic and copies ran while one was open for 6% of the time, Pallas kernels for 3%

profile of v10, /device:TPU:0, one launch (start us, length us, event | category | flops | bytes accessed | tf_op | source)
XLA Modules:
  0.0 59.3 jit_solution(13700431923453916976)
XLA Ops:
  0.6 5.1 %collective-permute-start.2 = (bf16[1,4,32,256]{3,2,1,0:T(8,128)(2,1)}, bf16[1,4,32,256]{3,2,1,0:T(8,128)(2,1)S(1)}, u32[]{:S(2)}, u32[]{:S(2)}) collective-permute-start(bf16[1,4,32,256]{3,2,1,0:T(8,128)(2,1)} %bitcast.44), channel_id=1, source_target_pairs={{0,12},{1,13},{2,14},{3,15},{4,8},{5,9},{6,10},{7,11},{8,4},{9,5},... | collective-permute-start | bytes 196616 | tf_op jit(solution)/shard_map/ppermute | solution.py:179
  5.7 0.0 collective-permute-start.1
  5.7 0.6 %collective-permute-start = (bf16[1,4,32,256]{3,2,1,0:T(8,128)(2,1)}, bf16[1,4,32,256]{3,2,1,0:T(8,128)(2,1)S(1)}, u32[]{:S(2)}, u32[]{:S(2)}) collective-permute-start(bf16[1,4,32,256]{3,2,1,0:T(8,128)(2,1)} %bitcast.46), channel_id=1, source_target_pairs={{0,8},{1,9},{2,10},{3,11},{4,12},{5,13},{6,14},{7,15},{8,0},{9,1},... | collective-permute-start | bytes 196616 | tf_op jit(solution)/shard_map/ppermute | solution.py:179
  6.4 0.0 copy-start
  6.4 0.9 %copy-done = bf16[4,256,32]{1,2,0:T(8,128)(2,1)S(1)} copy-done((bf16[4,256,32]{1,2,0:T(8,128)(2,1)S(1)}, bf16[4,256,32]{1,2,0:T(8,128)(2,1)}, u32[]{:S(2)}) %copy-start) | copy-done | bytes 65560
  7.3 1.7 %pad_maximum_fusion = bf16[16,16,512]{2,1,0:T(8,128)(2,1)} fusion(bf16[16,8,512]{2,1,0:T(8,128)(2,1)} %param.5, bf16[16,8,512]{2,1,0:T(8,128)(2,1)} %param.4), kind=kLoop, calls=%fused_computation.1 | loop fusion | flops 524288 | bytes 524288 | tf_op jit(solution)/shard_map/concatenate | solution.py:264
  9.0 0.1 pad_add_fusion.place
  9.0 0.7 %broadcast_in_dim.12.gain_ref = f32[8,512]{1,0:T(8,128)S(1)} broadcast(f32[512]{0:T(512)} %param.6), dimensions={1} | broadcast | bytes 18432 | tf_op jit(solution)/shard_map/broadcast_in_dim | solution.py:265
  9.7 1.9 %collective-permute-done.refs_1_ = bf16[1,4,32,256]{3,2,1,0:T(8,128)(2,1)S(1)} collective-permute-done((bf16[1,4,32,256]{3,2,1,0:T(8,128)(2,1)}, bf16[1,4,32,256]{3,2,1,0:T(8,128)(2,1)S(1)}, u32[]{:S(2)}, u32[]{:S(2)}) %collective-permute-start) | collective-permute-done | bytes 65568 | tf_op jit(solution)/shard_map/ppermute | solution.py:179
  11.6 0.0 collective-permute-done.2.refs_3_
  11.6 0.0 collective-permute-done.1.refs_2_
  11.6 1.6 %collective-permute-start.4 = (bf16[4,4,32,256]{3,2,1,0:T(8,128)(2,1)S(1)}, bf16[4,4,32,256]{3,2,1,0:T(8,128)(2,1)S(1)}, u32[]{:S(2)}, u32[]{:S(2)}) collective-permute-start(bf16[4,4,32,256]{3,2,1,0:T(8,128)(2,1)S(1)} %shard_map.68.refs_0_), channel_id=1, source_target_pairs={{0,2},{1,3},{2,0},{3,1},{4,6},{5,7},{6,4},{7,5},{8,10},{9,11},{10,... | collective-permute-start | bytes 786440 | tf_op jit(solution)/shard_map/ppermute | solution.py:179
  13.2 1.5 %collective-permute-start.3 = (bf16[4,4,32,256]{3,2,1,0:T(8,128)(2,1)S(1)}, bf16[4,4,32,256]{3,2,1,0:T(8,128)(2,1)S(1)}, u32[]{:S(2)}, u32[]{:S(2)}) collective-permute-start(bf16[4,4,32,256]{3,2,1,0:T(8,128)(2,1)S(1)} %shard_map.68.refs_0_), channel_id=1, source_target_pairs={{0,1},{1,0},{2,3},{3,2},{4,5},{5,4},{6,7},{7,6},{8,9},{9,8},{10,11... | collective-permute-start | bytes 786440 | tf_op jit(solution)/shard_map/ppermute | solution.py:179
  14.7 3.5 %all-to-all-start = ((bf16[16,16,512]{2,1,0:T(8,128)(2,1)}), bf16[16,16,512]{2,1,0:T(8,128)(2,1)S(1)}, u32[]{:S(2)}, u32[]{:S(2)}) async-start(bf16[16,16,512]{2,1,0:T(8,128)(2,1)} %pad_maximum_fusion), calls=%async_computation | async-start | bytes 524288 | tf_op jit(solution)/shard_map/all_to_all | solution.py:269
  18.3 0.1 collective-permute-start.7
  18.3 0.1 collective-permute-done.4.refs_2_
  18.4 1.8 %collective-permute-start.6 = (bf16[2,4,32,256]{3,2,1,0:T(8,128)(2,1)S(1)}, bf16[2,4,32,256]{3,2,1,0:T(8,128)(2,1)S(1)}, u32[]{:S(2)}, u32[]{:S(2)}) collective-permute-start(bf16[2,4,32,256]{3,2,1,0:T(8,128)(2,1)S(1)} %slice.78), channel_id=1, source_target_pairs={{0,1},{1,0},{2,3},{3,2},{4,5},{5,4},{6,7},{7,6},{8,9},{9,8},{10,11... | collective-permute-start | bytes 393224 | tf_op jit(solution)/shard_map/ppermute | solution.py:179
  20.3 0.2 collective-permute-start.9
  20.5 0.0 collective-permute-done.3.refs_1_
  20.5 0.4 collective-permute-start.8
  20.9 1.8 %collective-permute-start.5 = (bf16[2,4,32,256]{3,2,1,0:T(8,128)(2,1)S(1)}, bf16[2,4,32,256]{3,2,1,0:T(8,128)(2,1)S(1)}, u32[]{:S(2)}, u32[]{:S(2)}) collective-permute-start(bf16[2,4,32,256]{3,2,1,0:T(8,128)(2,1)S(1)} %slice.77), channel_id=1, source_target_pairs={{0,2},{1,3},{2,0},{3,1},{4,6},{5,7},{6,4},{7,5},{8,10},{9,11},{10,... | collective-permute-start | bytes 393224 | tf_op jit(solution)/shard_map/ppermute | solution.py:179
  22.7 3.9 %collective-permute-done.6.refs_4_ = bf16[2,4,32,256]{3,2,1,0:T(8,128)(2,1)S(1)} collective-permute-done((bf16[2,4,32,256]{3,2,1,0:T(8,128)(2,1)S(1)}, bf16[2,4,32,256]{3,2,1,0:T(8,128)(2,1)S(1)}, u32[]{:S(2)}, u32[]{:S(2)}) %collective-permute-start.6) | collective-permute-done | bytes 131104 | tf_op jit(solution)/shard_map/ppermute | solution.py:179
  26.5 0.0 collective-permute-start.11
  26.5 1.2 %collective-permute-done.5.refs_3_ = bf16[2,4,32,256]{3,2,1,0:T(8,128)(2,1)S(1)} collective-permute-done((bf16[2,4,32,256]{3,2,1,0:T(8,128)(2,1)S(1)}, bf16[2,4,32,256]{3,2,1,0:T(8,128)(2,1)S(1)}, u32[]{:S(2)}, u32[]{:S(2)}) %collective-permute-start.5) | collective-permute-done | bytes 131104 | tf_op jit(solution)/shard_map/ppermute | solution.py:179
  27.7 0.0 collective-permute-start.10
  27.7 0.0 collective-permute-done.7.refs_5_
  27.7 0.0 all-to-all-done.rows_ref
  27.7 0.0 collective-permute-done.9.refs_7_
  27.7 0.0 collective-permute-done.8.refs_6_
  27.7 0.1 collective-permute-done.11.refs_9_
  27.9 1.2 %collective-permute-done.10.refs_8_ = bf16[2,4,32,256]{3,2,1,0:T(8,128)(2,1)S(1)} collective-permute-done((bf16[2,4,32,256]{3,2,1,0:T(8,128)(2,1)S(1)}, bf16[2,4,32,256]{3,2,1,0:T(8,128)(2,1)S(1)}, u32[]{:S(2)}, u32[]{:S(2)}) %collective-permute-start.10) | collective-permute-done | bytes 131104 | tf_op jit(solution)/shard_map/ppermute | solution.py:276
  29.1 2.5 %shard_map.69 = (bf16[16,4,32,256]{3,2,1,0:T(8,128)(2,1)S(1)}, bf16[3,128,512]{2,1,0:T(8,128)(2,1)S(1)}, bf16[128,512]{1,0:T(8,128)(2,1)S(1)}, bf16[4,512,512]{2,1,0:T(8,128)(2,1)S(1)}, f32[1,512]{1,0:T(1,128)S(1)}) custom-call(s32[2]{0:T(128)S(1)} %pad_add_fusion.place, bf16[16,16,512]{2,1,0:T(8,128)(2,1)S(1)} %all-to-all-done.rows_ref, ...), custom_call_target="tpu_custom_call" | custom-call | tf_op jit(solution)/shard_map/pallas_call | solution.py:285
  31.6 0.2 collective-permute-start.12
  31.8 1.8 %shard_map.70 = (bf16[16,4,32,256]{3,2,1,0:T(8,128)(2,1)S(1)}, bf16[128,640]{1,0:T(8,128)(2,1)}) custom-call(s32[2]{0:T(128)S(1)} %pad_add_fusion.place, bf16[16,16,512]{2,1,0:T(8,128)(2,1)S(1)} %all-to-all-done.rows_ref, f32[1,512]{1,0:T(1,128)S(1)} %get-tuple-element.32.gain_ref, bf16[4,512,512]{2,1,0:T(8,128)(2,1)S(1)} %get-tuple-element.33.w_all, ...), custom_call_target="tpu_custom_call" | custom-call | flops 335544320 | bytes 4194304 | tf_op jit(solution)/shard_map/pallas_call | solution.py:299
  33.6 0.7 %collective-permute-done.12 = bf16[16,4,32,256]{3,2,1,0:T(8,128)(2,1)S(1)} collective-permute-done((bf16[16,4,32,256]{3,2,1,0:T(8,128)(2,1)S(1)}, bf16[16,4,32,256]{3,2,1,0:T(8,128)(2,1)S(1)}, u32[]{:S(2)}, u32[]{:S(2)}) %collective-permute-start.12) | collective-permute-done | bytes 1048608 | tf_op jit(solution)/shard_map/ppermute | solution.py:319
  34.3 0.4 add_convert_fusion
  34.7 0.1 slice_bitcast_fusion.3
  34.8 1.3 %collective-permute-start.17 = (bf16[2,4,32,256]{3,2,1,0:T(8,128)(2,1)S(1)}, bf16[2,4,32,256]{3,2,1,0:T(8,128)(2,1)S(1)}, u32[]{:S(2)}, u32[]{:S(2)}) collective-permute-start(bf16[2,4,32,256]{3,2,1,0:T(8,128)(2,1)S(1)} %get-tuple-element.49), channel_id=1, source_target_pairs={{0,1},{1,0},{2,3},{3,2},{4,5},{5,4},{6,7},{7,6},{8,9},{9,8},{10,11... | collective-permute-start | bytes 393224 | tf_op jit(solution)/shard_map/ppermute | solution.py:179
  36.1 0.5 collective-permute-start.19
  36.5 1.8 %collective-permute-start.18 = (bf16[2,4,32,256]{3,2,1,0:T(8,128)(2,1)S(1)}, bf16[2,4,32,256]{3,2,1,0:T(8,128)(2,1)S(1)}, u32[]{:S(2)}, u32[]{:S(2)}) collective-permute-start(bf16[2,4,32,256]{3,2,1,0:T(8,128)(2,1)S(1)} %get-tuple-element.51), channel_id=1, source_target_pairs={{0,3},{1,2},{2,1},{3,0},{4,7},{5,6},{6,5},{7,4},{8,11},{9,10},{10,... | collective-permute-start | bytes 393224 | tf_op jit(solution)/shard_map/ppermute | solution.py:179
  38.3 1.0 %collective-permute-start.15 = (bf16[2,4,32,256]{3,2,1,0:T(8,128)(2,1)S(1)}, bf16[2,4,32,256]{3,2,1,0:T(8,128)(2,1)S(1)}, u32[]{:S(2)}, u32[]{:S(2)}) collective-permute-start(bf16[2,4,32,256]{3,2,1,0:T(8,128)(2,1)S(1)} %get-tuple-element.52), channel_id=1, source_target_pairs={{0,2},{1,3},{2,0},{3,1},{4,6},{5,7},{6,4},{7,5},{8,10},{9,11},{10,... | collective-permute-start | bytes 393224 | tf_op jit(solution)/shard_map/ppermute | solution.py:179
  39.4 0.7 %collective-permute-start.14 = (bf16[2,4,32,256]{3,2,1,0:T(8,128)(2,1)S(1)}, bf16[2,4,32,256]{3,2,1,0:T(8,128)(2,1)S(1)}, u32[]{:S(2)}, u32[]{:S(2)}) collective-permute-start(bf16[2,4,32,256]{3,2,1,0:T(8,128)(2,1)S(1)} %get-tuple-element.53), channel_id=1, source_target_pairs={{0,1},{1,0},{2,3},{3,2},{4,5},{5,4},{6,7},{7,6},{8,9},{9,8},{10,11... | collective-permute-start | bytes 393224 | tf_op jit(solution)/shard_map/ppermute | solution.py:179
  40.0 1.0 %collective-permute-done.17 = bf16[2,4,32,256]{3,2,1,0:T(8,128)(2,1)S(1)} collective-permute-done((bf16[2,4,32,256]{3,2,1,0:T(8,128)(2,1)S(1)}, bf16[2,4,32,256]{3,2,1,0:T(8,128)(2,1)S(1)}, u32[]{:S(2)}, u32[]{:S(2)}) %collective-permute-start.17) | collective-permute-done | bytes 131104 | tf_op jit(solution)/shard_map/ppermute | solution.py:179
  41.0 1.0 %collective-permute-start.13 = (bf16[2,4,32,256]{3,2,1,0:T(8,128)(2,1)S(1)}, bf16[2,4,32,256]{3,2,1,0:T(8,128)(2,1)S(1)}, u32[]{:S(2)}, u32[]{:S(2)}) collective-permute-start(bf16[2,4,32,256]{3,2,1,0:T(8,128)(2,1)S(1)} %get-tuple-element.54), channel_id=1, source_target_pairs={{0,3},{1,2},{2,1},{3,0},{4,7},{5,6},{6,5},{7,4},{8,11},{9,10},{10,... | collective-permute-start | bytes 393224 | tf_op jit(solution)/shard_map/ppermute | solution.py:179
  42.0 5.3 %all-to-all-start.1 = ((bf16[16,8,640]{2,1,0:T(8,128)(2,1)}), bf16[16,8,640]{2,1,0:T(8,128)(2,1)S(1)}, u32[]{:S(2)}, u32[]{:S(2)}) async-start(bf16[16,8,640]{2,1,0:T(8,128)(2,1)} %bitcast.17), calls=%async_computation.1 | async-start | bytes 327680 | tf_op jit(solution)/shard_map/all_to_all | solution.py:316
  47.3 0.0 collective-permute-done.19
  47.3 0.0 collective-permute-done.18
  47.4 3.0 %collective-permute-done.15 = bf16[2,4,32,256]{3,2,1,0:T(8,128)(2,1)S(1)} collective-permute-done((bf16[2,4,32,256]{3,2,1,0:T(8,128)(2,1)S(1)}, bf16[2,4,32,256]{3,2,1,0:T(8,128)(2,1)S(1)}, u32[]{:S(2)}, u32[]{:S(2)}) %collective-permute-start.15) | collective-permute-done | bytes 131104 | tf_op jit(solution)/shard_map/ppermute | solution.py:179
  50.3 0.0 collective-permute-done.14
  50.3 0.0 collective-permute-done.13
  50.3 0.2 fusion
  50.5 2.3 %collective-permute-start.21 = (bf16[4,32,256]{2,1,0:T(8,128)(2,1)S(1)}, bf16[4,32,256]{2,1,0:T(8,128)(2,1)S(1)}, u32[]{:S(2)}, u32[]{:S(2)}) collective-permute-start(bf16[4,32,256]{2,1,0:T(8,128)(2,1)S(1)} %get-tuple-element.55), channel_id=1, source_target_pairs={{0,12},{1,13},{2,14},{3,15},{4,8},{5,9},{6,10},{7,11},{8,4},{9,5},... | collective-permute-start | bytes 196616 | tf_op jit(solution)/shard_map/ppermute | solution.py:179
  52.9 0.1 collective-permute-start.16
  53.0 2.1 %collective-permute-start.20 = (bf16[4,32,256]{2,1,0:T(8,128)(2,1)S(1)}, bf16[4,32,256]{2,1,0:T(8,128)(2,1)S(1)}, u32[]{:S(2)}, u32[]{:S(2)}) collective-permute-start(bf16[4,32,256]{2,1,0:T(8,128)(2,1)S(1)} %get-tuple-element.56), channel_id=1, source_target_pairs={{0,8},{1,9},{2,10},{3,11},{4,12},{5,13},{6,14},{7,15},{8,0},{9,1},... | collective-permute-start | bytes 196616 | tf_op jit(solution)/shard_map/ppermute | solution.py:179
  55.1 1.1 %all-to-all-done.1 = bf16[16,8,640]{2,1,0:T(8,128)(2,1)S(1)} async-done(((bf16[16,8,640]{2,1,0:T(8,128)(2,1)}), bf16[16,8,640]{2,1,0:T(8,128)(2,1)S(1)}, u32[]{:S(2)}, u32[]{:S(2)}) %all-to-all-start.1) | async-done | bytes 163872 | tf_op jit(solution)/shard_map/all_to_all | solution.py:316
  56.2 1.0 %collective-permute-done.21.refs_3_ = bf16[4,32,256]{2,1,0:T(8,128)(2,1)S(1)} collective-permute-done((bf16[4,32,256]{2,1,0:T(8,128)(2,1)S(1)}, bf16[4,32,256]{2,1,0:T(8,128)(2,1)S(1)}, u32[]{:S(2)}, u32[]{:S(2)}) %collective-permute-start.21) | collective-permute-done | bytes 65568 | tf_op jit(solution)/shard_map/ppermute | solution.py:179
  57.3 0.1 collective-permute-start.22
  57.4 0.7 %slice_bitcast_fusion.9 = bf16[16,8,512]{2,1,0:T(8,128)(2,1)} fusion(bf16[128,640]{1,0:T(8,128)(2,1)S(1)} %bitcast.53), kind=kLoop, calls=%fused_computation.15 | loop fusion | bytes 262144 | tf_op jit(solution)/shard_map/reshape | solution.py:322
  58.1 0.0 collective-permute-done.16.refs_1_
  58.1 0.5 collective-permute-done.20.refs_2_
  58.6 0.0 collective-permute-done.22
  58.6 0.7 %shard_map.71 = (f32[4,32,256]{2,1,0:T(8,128)}, f32[1,512]{1,0:T(1,128)}) custom-call(f32[4,32,256]{2,1,0:T(8,128)S(1)} %slice_bitcast_fusion.refs_0_, bf16[4,32,256]{2,1,0:T(8,128)(2,1)S(1)} %collective-permute-done.16.refs_1_, bf16[4,32,256]{2,1,0:T(8,128)(2,1)S(1)} %collective-permute-done.20.refs_2_, ...), custom_call_target="tpu_custom_call" | custom-call | tf_op jit(solution)/shard_map/pallas_call | solution.py:332
  (10 shorter events, 0.2 us)
Async XLA Ops:
  0.6 11.0 %collective-permute-start.2 = (bf16[1,4,32,256]{3,2,1,0:T(8,128)(2,1)}, bf16[1,4,32,256]{3,2,1,0:T(8,128)(2,1)S(1)}, u32[]{:S(2)}, u32[]{:S(2)}) collective-permute-start(bf16[1,4,32,256]{3,2,1,0:T(8,128)(2,1)} %bitcast.44), channel_id=1, source_target_pairs={{0,12},{1,13},{2,14},{3,15},{4,8},{5,9},{6,10},{7,11},{8,4},{9,5},... | collective-permute-start | bytes 196616 | tf_op jit(solution)/shard_map/ppermute | solution.py:179
  5.7 5.9 %collective-permute-start.1 = (bf16[1,4,32,256]{3,2,1,0:T(8,128)(2,1)}, bf16[1,4,32,256]{3,2,1,0:T(8,128)(2,1)S(1)}, u32[]{:S(2)}, u32[]{:S(2)}) collective-permute-start(bf16[1,4,32,256]{3,2,1,0:T(8,128)(2,1)} %bitcast.45), channel_id=1, source_target_pairs={{0,4},{1,5},{2,6},{3,7},{4,0},{5,1},{6,2},{7,3},{8,12},{9,13},{10,... | collective-permute-start | bytes 196616 | tf_op jit(solution)/shard_map/ppermute | solution.py:179
  5.7 5.8 %collective-permute-start = (bf16[1,4,32,256]{3,2,1,0:T(8,128)(2,1)}, bf16[1,4,32,256]{3,2,1,0:T(8,128)(2,1)S(1)}, u32[]{:S(2)}, u32[]{:S(2)}) collective-permute-start(bf16[1,4,32,256]{3,2,1,0:T(8,128)(2,1)} %bitcast.46), channel_id=1, source_target_pairs={{0,8},{1,9},{2,10},{3,11},{4,12},{5,13},{6,14},{7,15},{8,0},{9,1},... | collective-permute-start | bytes 196616 | tf_op jit(solution)/shard_map/ppermute | solution.py:179
  6.4 0.9 %copy-start = (bf16[4,256,32]{1,2,0:T(8,128)(2,1)S(1)}, bf16[4,256,32]{1,2,0:T(8,128)(2,1)}, u32[]{:S(2)}) copy-start(bf16[4,256,32]{1,2,0:T(8,128)(2,1)} %param.7) | copy-start | bytes 196612
  11.6 6.8 %collective-permute-start.4 = (bf16[4,4,32,256]{3,2,1,0:T(8,128)(2,1)S(1)}, bf16[4,4,32,256]{3,2,1,0:T(8,128)(2,1)S(1)}, u32[]{:S(2)}, u32[]{:S(2)}) collective-permute-start(bf16[4,4,32,256]{3,2,1,0:T(8,128)(2,1)S(1)} %shard_map.68.refs_0_), channel_id=1, source_target_pairs={{0,2},{1,3},{2,0},{3,1},{4,6},{5,7},{6,4},{7,5},{8,10},{9,11},{10,... | collective-permute-start | bytes 786440 | tf_op jit(solution)/shard_map/ppermute | solution.py:179
  13.2 7.3 %collective-permute-start.3 = (bf16[4,4,32,256]{3,2,1,0:T(8,128)(2,1)S(1)}, bf16[4,4,32,256]{3,2,1,0:T(8,128)(2,1)S(1)}, u32[]{:S(2)}, u32[]{:S(2)}) collective-permute-start(bf16[4,4,32,256]{3,2,1,0:T(8,128)(2,1)S(1)} %shard_map.68.refs_0_), channel_id=1, source_target_pairs={{0,1},{1,0},{2,3},{3,2},{4,5},{5,4},{6,7},{7,6},{8,9},{9,8},{10,11... | collective-permute-start | bytes 786440 | tf_op jit(solution)/shard_map/ppermute | solution.py:179
  14.7 13.0 %all-to-all-start = ((bf16[16,16,512]{2,1,0:T(8,128)(2,1)}), bf16[16,16,512]{2,1,0:T(8,128)(2,1)S(1)}, u32[]{:S(2)}, u32[]{:S(2)}) async-start(bf16[16,16,512]{2,1,0:T(8,128)(2,1)} %pad_maximum_fusion), calls=%async_computation | async-start | bytes 524288 | tf_op jit(solution)/shard_map/all_to_all | solution.py:269
  18.3 9.5 %collective-permute-start.7 = (bf16[4,4,32,256]{3,2,1,0:T(8,128)(2,1)S(1)}, bf16[4,4,32,256]{3,2,1,0:T(8,128)(2,1)S(1)}, u32[]{:S(2)}, u32[]{:S(2)}) collective-permute-start(bf16[4,4,32,256]{3,2,1,0:T(8,128)(2,1)S(1)} %shard_map.68.refs_0_), channel_id=1, source_target_pairs={{0,16},{16,0},{1,17},{17,1},{2,18},{18,2},{3,19},{19,3},{4,20},{20... | collective-permute-start | bytes 786440 | tf_op jit(solution)/shard_map/ppermute | solution.py:276
  18.4 8.1 %collective-permute-start.6 = (bf16[2,4,32,256]{3,2,1,0:T(8,128)(2,1)S(1)}, bf16[2,4,32,256]{3,2,1,0:T(8,128)(2,1)S(1)}, u32[]{:S(2)}, u32[]{:S(2)}) collective-permute-start(bf16[2,4,32,256]{3,2,1,0:T(8,128)(2,1)S(1)} %slice.78), channel_id=1, source_target_pairs={{0,1},{1,0},{2,3},{3,2},{4,5},{5,4},{6,7},{7,6},{8,9},{9,8},{10,11... | collective-permute-start | bytes 393224 | tf_op jit(solution)/shard_map/ppermute | solution.py:179
  20.3 7.4 %collective-permute-start.9 = (bf16[4,4,32,256]{3,2,1,0:T(8,128)(2,1)S(1)}, bf16[4,4,32,256]{3,2,1,0:T(8,128)(2,1)S(1)}, u32[]{:S(2)}, u32[]{:S(2)}) collective-permute-start(bf16[4,4,32,256]{3,2,1,0:T(8,128)(2,1)S(1)} %collective-permute-done.4.refs_2_), channel_id=1, source_target_pairs={{0,16},{16,0},{1,17},{17,1},{2,18},{18,2},{3,19},{19,3},{4,20},{20... | collective-permute-start | bytes 786440 | tf_op jit(solution)/shard_map/ppermute | solution.py:276
  20.5 7.2 %collective-permute-start.8 = (bf16[4,4,32,256]{3,2,1,0:T(8,128)(2,1)S(1)}, bf16[4,4,32,256]{3,2,1,0:T(8,128)(2,1)S(1)}, u32[]{:S(2)}, u32[]{:S(2)}) collective-permute-start(bf16[4,4,32,256]{3,2,1,0:T(8,128)(2,1)S(1)} %collective-permute-done.3.refs_1_), channel_id=1, source_target_pairs={{0,16},{16,0},{1,17},{17,1},{2,18},{18,2},{3,19},{19,3},{4,20},{20... | collective-permute-start | bytes 786440 | tf_op jit(solution)/shard_map/ppermute | solution.py:276
  20.9 6.8 %collective-permute-start.5 = (bf16[2,4,32,256]{3,2,1,0:T(8,128)(2,1)S(1)}, bf16[2,4,32,256]{3,2,1,0:T(8,128)(2,1)S(1)}, u32[]{:S(2)}, u32[]{:S(2)}) collective-permute-start(bf16[2,4,32,256]{3,2,1,0:T(8,128)(2,1)S(1)} %slice.77), channel_id=1, source_target_pairs={{0,2},{1,3},{2,0},{3,1},{4,6},{5,7},{6,4},{7,5},{8,10},{9,11},{10,... | collective-permute-start | bytes 393224 | tf_op jit(solution)/shard_map/ppermute | solution.py:179
  26.5 1.3 %collective-permute-start.11 = (bf16[2,4,32,256]{3,2,1,0:T(8,128)(2,1)S(1)}, bf16[2,4,32,256]{3,2,1,0:T(8,128)(2,1)S(1)}, u32[]{:S(2)}, u32[]{:S(2)}) collective-permute-start(bf16[2,4,32,256]{3,2,1,0:T(8,128)(2,1)S(1)} %collective-permute-done.6.refs_4_), channel_id=1, source_target_pairs={{0,16},{16,0},{1,17},{17,1},{2,18},{18,2},{3,19},{19,3},{4,20},{20... | collective-permute-start | bytes 393224 | tf_op jit(solution)/shard_map/ppermute | solution.py:276
  27.7 1.3 %collective-permute-start.10 = (bf16[2,4,32,256]{3,2,1,0:T(8,128)(2,1)S(1)}, bf16[2,4,32,256]{3,2,1,0:T(8,128)(2,1)S(1)}, u32[]{:S(2)}, u32[]{:S(2)}) collective-permute-start(bf16[2,4,32,256]{3,2,1,0:T(8,128)(2,1)S(1)} %collective-permute-done.5.refs_3_), channel_id=1, source_target_pairs={{0,16},{16,0},{1,17},{17,1},{2,18},{18,2},{3,19},{19,3},{4,20},{20... | collective-permute-start | bytes 393224 | tf_op jit(solution)/shard_map/ppermute | solution.py:276
  31.6 2.7 %collective-permute-start.12 = (bf16[16,4,32,256]{3,2,1,0:T(8,128)(2,1)S(1)}, bf16[16,4,32,256]{3,2,1,0:T(8,128)(2,1)S(1)}, u32[]{:S(2)}, u32[]{:S(2)}) collective-permute-start(bf16[16,4,32,256]{3,2,1,0:T(8,128)(2,1)S(1)} %get-tuple-element.37), channel_id=1, source_target_pairs={{0,16},{16,0},{1,17},{17,1},{2,18},{18,2},{3,19},{19,3},{4,20},{20... | collective-permute-start | bytes 3145736 | tf_op jit(solution)/shard_map/ppermute | solution.py:319
  34.8 6.3 %collective-permute-start.17 = (bf16[2,4,32,256]{3,2,1,0:T(8,128)(2,1)S(1)}, bf16[2,4,32,256]{3,2,1,0:T(8,128)(2,1)S(1)}, u32[]{:S(2)}, u32[]{:S(2)}) collective-permute-start(bf16[2,4,32,256]{3,2,1,0:T(8,128)(2,1)S(1)} %get-tuple-element.49), channel_id=1, source_target_pairs={{0,1},{1,0},{2,3},{3,2},{4,5},{5,4},{6,7},{7,6},{8,9},{9,8},{10,11... | collective-permute-start | bytes 393224 | tf_op jit(solution)/shard_map/ppermute | solution.py:179
  36.1 11.2 %collective-permute-start.19 = (bf16[2,4,32,256]{3,2,1,0:T(8,128)(2,1)S(1)}, bf16[2,4,32,256]{3,2,1,0:T(8,128)(2,1)S(1)}, u32[]{:S(2)}, u32[]{:S(2)}) collective-permute-start(bf16[2,4,32,256]{3,2,1,0:T(8,128)(2,1)S(1)} %get-tuple-element.50), channel_id=1, source_target_pairs={{0,2},{1,3},{2,0},{3,1},{4,6},{5,7},{6,4},{7,5},{8,10},{9,11},{10,... | collective-permute-start | bytes 393224 | tf_op jit(solution)/shard_map/ppermute | solution.py:179
  36.5 10.8 %collective-permute-start.18 = (bf16[2,4,32,256]{3,2,1,0:T(8,128)(2,1)S(1)}, bf16[2,4,32,256]{3,2,1,0:T(8,128)(2,1)S(1)}, u32[]{:S(2)}, u32[]{:S(2)}) collective-permute-start(bf16[2,4,32,256]{3,2,1,0:T(8,128)(2,1)S(1)} %get-tuple-element.51), channel_id=1, source_target_pairs={{0,3},{1,2},{2,1},{3,0},{4,7},{5,6},{6,5},{7,4},{8,11},{9,10},{10,... | collective-permute-start | bytes 393224 | tf_op jit(solution)/shard_map/ppermute | solution.py:179
  38.3 12.0 %collective-permute-start.15 = (bf16[2,4,32,256]{3,2,1,0:T(8,128)(2,1)S(1)}, bf16[2,4,32,256]{3,2,1,0:T(8,128)(2,1)S(1)}, u32[]{:S(2)}, u32[]{:S(2)}) collective-permute-start(bf16[2,4,32,256]{3,2,1,0:T(8,128)(2,1)S(1)} %get-tuple-element.52), channel_id=1, source_target_pairs={{0,2},{1,3},{2,0},{3,1},{4,6},{5,7},{6,4},{7,5},{8,10},{9,11},{10,... | collective-permute-start | bytes 393224 | tf_op jit(solution)/shard_map/ppermute | solution.py:179
  39.4 11.0 %collective-permute-start.14 = (bf16[2,4,32,256]{3,2,1,0:T(8,128)(2,1)S(1)}, bf16[2,4,32,256]{3,2,1,0:T(8,128)(2,1)S(1)}, u32[]{:S(2)}, u32[]{:S(2)}) collective-permute-start(bf16[2,4,32,256]{3,2,1,0:T(8,128)(2,1)S(1)} %get-tuple-element.53), channel_id=1, source_target_pairs={{0,1},{1,0},{2,3},{3,2},{4,5},{5,4},{6,7},{7,6},{8,9},{9,8},{10,11... | collective-permute-start | bytes 393224 | tf_op jit(solution)/shard_map/ppermute | solution.py:179
  41.0 9.3 %collective-permute-start.13 = (bf16[2,4,32,256]{3,2,1,0:T(8,128)(2,1)S(1)}, bf16[2,4,32,256]{3,2,1,0:T(8,128)(2,1)S(1)}, u32[]{:S(2)}, u32[]{:S(2)}) collective-permute-start(bf16[2,4,32,256]{3,2,1,0:T(8,128)(2,1)S(1)} %get-tuple-element.54), channel_id=1, source_target_pairs={{0,3},{1,2},{2,1},{3,0},{4,7},{5,6},{6,5},{7,4},{8,11},{9,10},{10,... | collective-permute-start | bytes 393224 | tf_op jit(solution)/shard_map/ppermute | solution.py:179
  42.0 14.2 %all-to-all-start.1 = ((bf16[16,8,640]{2,1,0:T(8,128)(2,1)}), bf16[16,8,640]{2,1,0:T(8,128)(2,1)S(1)}, u32[]{:S(2)}, u32[]{:S(2)}) async-start(bf16[16,8,640]{2,1,0:T(8,128)(2,1)} %bitcast.17), calls=%async_computation.1 | async-start | bytes 327680 | tf_op jit(solution)/shard_map/all_to_all | solution.py:316
  50.5 6.7 %collective-permute-start.21 = (bf16[4,32,256]{2,1,0:T(8,128)(2,1)S(1)}, bf16[4,32,256]{2,1,0:T(8,128)(2,1)S(1)}, u32[]{:S(2)}, u32[]{:S(2)}) collective-permute-start(bf16[4,32,256]{2,1,0:T(8,128)(2,1)S(1)} %get-tuple-element.55), channel_id=1, source_target_pairs={{0,12},{1,13},{2,14},{3,15},{4,8},{5,9},{6,10},{7,11},{8,4},{9,5},... | collective-permute-start | bytes 196616 | tf_op jit(solution)/shard_map/ppermute | solution.py:179
  52.9 5.2 %collective-permute-start.16 = (bf16[4,32,256]{2,1,0:T(8,128)(2,1)S(1)}, bf16[4,32,256]{2,1,0:T(8,128)(2,1)S(1)}, u32[]{:S(2)}, u32[]{:S(2)}) collective-permute-start(bf16[4,32,256]{2,1,0:T(8,128)(2,1)S(1)} %fusion.1), channel_id=1, source_target_pairs={{0,4},{1,5},{2,6},{3,7},{4,0},{5,1},{6,2},{7,3},{8,12},{9,13},{10,... | collective-permute-start | bytes 196616 | tf_op jit(solution)/shard_map/ppermute | solution.py:179
  53.0 5.6 %collective-permute-start.20 = (bf16[4,32,256]{2,1,0:T(8,128)(2,1)S(1)}, bf16[4,32,256]{2,1,0:T(8,128)(2,1)S(1)}, u32[]{:S(2)}, u32[]{:S(2)}) collective-permute-start(bf16[4,32,256]{2,1,0:T(8,128)(2,1)S(1)} %get-tuple-element.56), channel_id=1, source_target_pairs={{0,8},{1,9},{2,10},{3,11},{4,12},{5,13},{6,14},{7,15},{8,0},{9,1},... | collective-permute-start | bytes 196616 | tf_op jit(solution)/shard_map/ppermute | solution.py:179
  57.3 1.3 %collective-permute-start.22 = (f32[512]{0:T(512)S(1)}, f32[512]{0:T(512)S(1)}, u32[]{:S(2)}, u32[]{:S(2)}) collective-permute-start(f32[512]{0:T(512)S(1)} %reduce_sum.9), channel_id=1, source_target_pairs={{0,16},{16,0},{1,17},{17,1},{2,18},{18,2},{3,19},{19,3},{4,20},{20... | collective-permute-start | bytes 6152 | tf_op jit(solution)/shard_map/ppermute | solution.py:325
